TPU v7x, 32 devices: a whole 2x2x4 slice. The times are simulated.
32 devices in a mesh: ha: 8 (over z, x), wa: 4 (over y, core).
Axes of the slice: x: 2, y: 2, z: 4, core: 2. Of those that a mesh axis runs over, the one named last changes fastest.
Arguments:
- bottom: bfloat16 [24, 16, 32, 512], P(None, 'ha', 'wa'), may hold values from -6 to 6
- skipped: bfloat16 [24, 32, 64, 512], P(None, 'ha', 'wa'), may hold values from -6 to 6
- groups: int32 [24], replicated, may hold values from 0 to 4, never falling along the last dimension, each value on 1 to 8 neighbouring positions
- pixel_mask: int32 [24, 32, 64], P(None, 'ha', 'wa'), may hold values from 0 to 1
- labels: int32 [24, 32, 64], P(None, 'ha', 'wa'), may hold values 0 or 1
- conv1_weight: float32 [4608, 1024], P(('ha', 'wa')), may hold values from -0.09375 to 0.09375
- conv1_momentum: float32 [4608, 1024], P(('ha', 'wa')), may hold values from -0.00061035156 to 0.00061035156
- conv1_average: float32 [4608, 1024], P(('ha', 'wa')), may hold values from -0.09375 to 0.09375
- conv2_weight: float32 [9216, 1024], P(('ha', 'wa')), may hold values from -0.0625 to 0.0625
- conv2_momentum: float32 [9216, 1024], P(('ha', 'wa')), may hold values from -0.00061035156 to 0.00061035156
- conv2_average: float32 [9216, 1024], P(('ha', 'wa')), may hold values from -0.0625 to 0.0625
- up_weight: float32 [1024, 2048], P(('ha', 'wa')), may hold values from -0.1875 to 0.1875
- up_momentum: float32 [1024, 2048], P(('ha', 'wa')), may hold values from -0.00061035156 to 0.00061035156
- up_average: float32 [1024, 2048], P(('ha', 'wa')), may hold values from -0.1875 to 0.1875
- conv3_weight: float32 [9216, 512], P(('ha', 'wa')), may hold values from -0.0625 to 0.0625
- conv3_momentum: float32 [9216, 512], P(('ha', 'wa')), may hold values from -0.00061035156 to 0.00061035156
- conv3_average: float32 [9216, 512], P(('ha', 'wa')), may hold values from -0.0625 to 0.0625
- head_weight: float32 [512, 2], P(('ha', 'wa')), may hold values from -0.25 to 0.25
- head_momentum: float32 [512, 2], P(('ha', 'wa')), may hold values from -0.0234375 to 0.0234375
- head_average: float32 [512, 2], P(('ha', 'wa')), may hold values from -0.25 to 0.25
Outputs:
- loss_value: float32 [], replicated
- conv1_weight_new: float32 [4608, 1024], P(('ha', 'wa'))
- conv1_momentum_new: float32 [4608, 1024], P(('ha', 'wa'))
- conv1_average_new: float32 [4608, 1024], P(('ha', 'wa'))
- conv2_weight_new: float32 [9216, 1024], P(('ha', 'wa'))
- conv2_momentum_new: float32 [9216, 1024], P(('ha', 'wa'))
- conv2_average_new: float32 [9216, 1024], P(('ha', 'wa'))
- up_weight_new: float32 [1024, 2048], P(('ha', 'wa'))
- up_momentum_new: float32 [1024, 2048], P(('ha', 'wa'))
- up_average_new: float32 [1024, 2048], P(('ha', 'wa'))
- conv3_weight_new: float32 [9216, 512], P(('ha', 'wa'))
- conv3_momentum_new: float32 [9216, 512], P(('ha', 'wa'))
- conv3_average_new: float32 [9216, 512], P(('ha', 'wa'))
- head_weight_new: float32 [512, 2], P(('ha', 'wa'))
- head_momentum_new: float32 [512, 2], P(('ha', 'wa'))
- head_average_new: float32 [512, 2], P(('ha', 'wa'))
Inputs may be any that keep to these rules, and one draw needn't show every extreme that they name: `groups`: never falls along the slices; every group has 1 to 8 slices, and one group has exactly 8.
All inputs are finite; a program needn't handle non-finite values. No bound on the sum of `labels` on one device may be relied on, other than what follows from the above.
Results may differ from a plain program's by a relative error of at most 0.0065.
Values may be sent and summed in bfloat16 or wider, within the bound.
A program may use at most 320 MiB of HBM per device.

v0:
```python
import jax
import jax.numpy as jnp
from jax import lax
from jax.sharding import PartitionSpec as P

GROUPS = 5


MOMENTUM = 0.9
RATE_CONV = 600.0
RATE_HEAD = 25.0
AVERAGE_DECAY = 0.5
SMOOTHING = 1.0
HIGHEST = lax.Precision.HIGHEST


def with_halo(block, sides, width):
    for axis, dim in sides:
        count = lax.axis_size(axis)
        forward = [(i, i + 1) for i in range(count - 1)]
        backward = [(target, source) for source, target in forward]
        low = lax.ppermute(
            lax.slice_in_dim(block, block.shape[dim] - width, None, axis=dim), axis, forward
        )
        high = lax.ppermute(lax.slice_in_dim(block, 0, width, axis=dim), axis, backward)
        block = jnp.concatenate([low, block, high], axis=dim)
    return block


def smooth(source):
    return jax.nn.gelu(source, approximate=True)


def smooth_back(pre_value, gradient):
    _, pull_back = jax.vjp(smooth, pre_value)
    return pull_back(gradient)[0]


def widened_field(source):
    return with_halo(source, (("ha", 1), ("wa", 2)), 1)


def conv_taps(padded, weight):
    in_chan = padded.shape[3]
    row_count, col_count = (padded.shape[1] - 2, padded.shape[2] - 2)
    running = None
    for tap_index in range(9):
        row_off, col_off = (tap_index // 3, tap_index % 3)
        window = padded[:, row_off : row_off + row_count, col_off : col_off + col_count, :]
        taps = weight[tap_index * in_chan : (tap_index + 1) * in_chan]
        product = jnp.einsum("shwc,co->shwo", window, taps, preferred_element_type=jnp.float32)
        running = product if running is None else running + product
    return running


def conv_back(padded, grad_out, weight, need_input):
    in_chan = padded.shape[3]
    row_count, col_count = (grad_out.shape[1], grad_out.shape[2])
    pieces = []
    for tap_index in range(9):
        row_off, col_off = (tap_index // 3, tap_index % 3)
        window = padded[:, row_off : row_off + row_count, col_off : col_off + col_count, :]
        pieces.append(
            jnp.einsum("shwc,shwo->co", window, grad_out, preferred_element_type=jnp.float32)
        )
    weight_grad = jnp.concatenate(pieces, axis=0)
    if not need_input:
        return (weight_grad, None)
    grad_padded = with_halo(grad_out, (("ha", 1), ("wa", 2)), 1)
    running = None
    for tap_index in range(9):
        row_off, col_off = (tap_index // 3, tap_index % 3)
        window = grad_padded[
            :, 2 - row_off : 2 - row_off + row_count, 2 - col_off : 2 - col_off + col_count, :
        ]
        taps = weight[tap_index * in_chan : (tap_index + 1) * in_chan]
        product = jnp.einsum("shwo,co->shwc", window, taps, preferred_element_type=jnp.float32)
        running = product if running is None else running + product
    return (weight_grad, running)


def upsample(source, weight):
    slices, row_count, col_count, _ = source.shape
    flattened = jnp.einsum("shwc,cq->shwq", source, weight, preferred_element_type=jnp.float32)
    blocks = flattened.reshape(slices, row_count, col_count, 2, 2, -1).transpose(0, 1, 3, 2, 4, 5)
    return blocks.reshape(slices, 2 * row_count, 2 * col_count, -1)


def upsample_back(source, grad_up, weight):
    slices, row_count, col_count, _ = source.shape
    blocks = grad_up.reshape(slices, row_count, 2, col_count, 2, -1).transpose(0, 1, 3, 2, 4, 5)
    flattened = blocks.reshape(slices, row_count, col_count, -1)
    weight_grad = jnp.einsum("shwc,shwq->cq", source, flattened, preferred_element_type=jnp.float32)
    source_grad = jnp.einsum("shwq,cq->shwc", flattened, weight, preferred_element_type=jnp.float32)
    return (weight_grad, source_grad)


def forward(gathered, bottom, skipped):
    weight_one, weight_two, weight_up, weight_three, weight_head = gathered
    pad_zero = widened_field(bottom)
    pre_one = conv_taps(pad_zero, weight_one)
    hidden_one = smooth(pre_one).astype(jnp.bfloat16)
    pad_one = widened_field(hidden_one)
    pre_two = conv_taps(pad_one, weight_two)
    hidden_two = smooth(pre_two).astype(jnp.bfloat16)
    upsampled = upsample(hidden_two, weight_up).astype(jnp.bfloat16)
    joined = jnp.concatenate([upsampled, skipped], axis=3)
    pad_two = widened_field(joined)
    pre_three = conv_taps(pad_two, weight_three)
    hidden_three = smooth(pre_three).astype(jnp.bfloat16)
    logits = jnp.einsum(
        "shwc,ck->shwk", hidden_three, weight_head, preferred_element_type=jnp.float32
    )
    return (
        pad_zero,
        pre_one,
        pad_one,
        pre_two,
        hidden_two,
        pad_two,
        pre_three,
        hidden_three,
        logits,
    )


def pixel_terms(logits, pixel_mask, labels):
    probability = jax.nn.softmax(logits, axis=-1)
    classes = jnp.arange(logits.shape[-1])
    target = (labels[..., None] == classes[None, None, None, :]).astype(jnp.float32)
    weighted = pixel_mask[..., None].astype(jnp.float32)
    return (probability, target, weighted)


def dice_terms(logits, pixel_mask, labels, member):
    probability, target, weighted = pixel_terms(logits, pixel_mask, labels)
    per_slice = jnp.stack(
        [
            jnp.sum(weighted * probability * target, axis=(1, 2)),
            jnp.sum(weighted * probability, axis=(1, 2)),
            jnp.sum(weighted * target, axis=(1, 2)),
        ],
        axis=-1,
    )
    return jnp.einsum("skj,sg->gkj", per_slice, member, precision=HIGHEST)


def dice_back(logits, pixel_mask, labels, member, totals):
    probability, target, weighted = pixel_terms(logits, pixel_mask, labels)
    union_sum = totals[..., 1] + totals[..., 2] + SMOOTHING
    numerator = 2.0 * totals[..., 0] + SMOOTHING
    dice_score = numerator / union_sum
    loss_value = 1.0 - jnp.mean(dice_score)
    entry_count = float(dice_score.size)
    coef_common = -2.0 / (entry_count * union_sum)
    coef_prob = numerator / (entry_count * union_sum * union_sum)
    slice_common = jnp.einsum("sg,gk->sk", member, coef_common, precision=HIGHEST)
    slice_prob = jnp.einsum("sg,gk->sk", member, coef_prob, precision=HIGHEST)
    grad_prob = weighted * (target * slice_common[:, None, None, :] + slice_prob[:, None, None, :])
    inner = jnp.sum(probability * grad_prob, axis=-1, keepdims=True)
    grad_logits = (probability * (grad_prob - inner)).astype(jnp.bfloat16)
    return (loss_value, grad_logits)


def renew_state(weight, moment, average, gradient, rate):
    moment_new = MOMENTUM * moment + gradient
    weight_new = weight - rate * (gradient + MOMENTUM * moment_new)
    average_new = AVERAGE_DECAY * average + (1.0 - AVERAGE_DECAY) * weight_new
    return (weight_new, moment_new, average_new)


def body(
    bottom,
    skipped,
    groups,
    pixel_mask,
    labels,
    conv1_weight,
    conv1_momentum,
    conv1_average,
    conv2_weight,
    conv2_momentum,
    conv2_average,
    up_weight,
    up_momentum,
    up_average,
    conv3_weight,
    conv3_momentum,
    conv3_average,
    head_weight,
    head_momentum,
    head_average,
):
    gathered = (
        lax.all_gather(conv1_weight.astype(jnp.bfloat16), ("ha", "wa"), axis=0, tiled=True),
        lax.all_gather(conv2_weight.astype(jnp.bfloat16), ("ha", "wa"), axis=0, tiled=True),
        lax.all_gather(up_weight.astype(jnp.bfloat16), ("ha", "wa"), axis=0, tiled=True),
        lax.all_gather(conv3_weight.astype(jnp.bfloat16), ("ha", "wa"), axis=0, tiled=True),
        lax.all_gather(head_weight.astype(jnp.bfloat16), ("ha", "wa"), axis=0, tiled=True),
    )
    member = (groups[:, None] == jnp.arange(GROUPS)[None, :]).astype(jnp.float32)
    kept = forward(gathered, bottom, skipped)
    partial_sums = dice_terms(kept[8], pixel_mask, labels, member)
    totals = lax.psum(partial_sums, ("ha", "wa"))
    totals, gathered = lax.optimization_barrier((totals, gathered))
    kept = forward(gathered, bottom, skipped)
    pad_zero, pre_one, pad_one, pre_two, hidden_two, pad_two, pre_three, hidden_three, logits = kept
    weight_one, weight_two, weight_up, weight_three, weight_head = gathered
    loss_value, grad_logits = dice_back(logits, pixel_mask, labels, member, totals)
    head_grad = jnp.einsum(
        "shwc,shwk->ck", hidden_three, grad_logits, preferred_element_type=jnp.float32
    )
    grad_hidden = jnp.einsum(
        "shwk,ck->shwc", grad_logits, weight_head, preferred_element_type=jnp.float32
    )
    grad_pre_three = smooth_back(pre_three, grad_hidden).astype(jnp.bfloat16)
    conv3_grad, grad_joined = conv_back(pad_two, grad_pre_three, weight_three, True)
    up_chan = weight_up.shape[1] // 4
    grad_upsampled = grad_joined[..., :up_chan].astype(jnp.bfloat16)
    up_grad, grad_hidden_two = upsample_back(hidden_two, grad_upsampled, weight_up)
    grad_pre_two = smooth_back(pre_two, grad_hidden_two).astype(jnp.bfloat16)
    conv2_grad, grad_hidden_one = conv_back(pad_one, grad_pre_two, weight_two, True)
    grad_pre_one = smooth_back(pre_one, grad_hidden_one).astype(jnp.bfloat16)
    conv1_grad, _ = conv_back(pad_zero, grad_pre_one, weight_one, False)
    conv1_grad, conv2_grad, up_grad, conv3_grad, head_grad = (
        lax.psum_scatter(conv1_grad, ("ha", "wa"), scatter_dimension=0, tiled=True),
        lax.psum_scatter(conv2_grad, ("ha", "wa"), scatter_dimension=0, tiled=True),
        lax.psum_scatter(up_grad, ("ha", "wa"), scatter_dimension=0, tiled=True),
        lax.psum_scatter(conv3_grad, ("ha", "wa"), scatter_dimension=0, tiled=True),
        lax.psum_scatter(head_grad, ("ha", "wa"), scatter_dimension=0, tiled=True),
    )
    first = renew_state(conv1_weight, conv1_momentum, conv1_average, conv1_grad, RATE_CONV)
    second = renew_state(conv2_weight, conv2_momentum, conv2_average, conv2_grad, RATE_CONV)
    upward = renew_state(up_weight, up_momentum, up_average, up_grad, RATE_CONV)
    third = renew_state(conv3_weight, conv3_momentum, conv3_average, conv3_grad, RATE_CONV)
    header = renew_state(head_weight, head_momentum, head_average, head_grad, RATE_HEAD)
    return (
        loss_value,
        first[0],
        first[1],
        first[2],
        second[0],
        second[1],
        second[2],
        upward[0],
        upward[1],
        upward[2],
        third[0],
        third[1],
        third[2],
        header[0],
        header[1],
        header[2],
    )


def solution(mesh):
    in_specs = (
        P(None, "ha", "wa", None),
        P(None, "ha", "wa", None),
        P(),
        P(None, "ha", "wa"),
        P(None, "ha", "wa"),
        P(("ha", "wa"), None),
        P(("ha", "wa"), None),
        P(("ha", "wa"), None),
        P(("ha", "wa"), None),
        P(("ha", "wa"), None),
        P(("ha", "wa"), None),
        P(("ha", "wa"), None),
        P(("ha", "wa"), None),
        P(("ha", "wa"), None),
        P(("ha", "wa"), None),
        P(("ha", "wa"), None),
        P(("ha", "wa"), None),
        P(("ha", "wa"), None),
        P(("ha", "wa"), None),
        P(("ha", "wa"), None),
    )
    out_specs = (
        P(),
        P(("ha", "wa"), None),
        P(("ha", "wa"), None),
        P(("ha", "wa"), None),
        P(("ha", "wa"), None),
        P(("ha", "wa"), None),
        P(("ha", "wa"), None),
        P(("ha", "wa"), None),
        P(("ha", "wa"), None),
        P(("ha", "wa"), None),
        P(("ha", "wa"), None),
        P(("ha", "wa"), None),
        P(("ha", "wa"), None),
        P(("ha", "wa"), None),
        P(("ha", "wa"), None),
        P(("ha", "wa"), None),
    )
    return jax.shard_map(body, mesh=mesh, in_specs=in_specs, out_specs=out_specs, check_vma=False)
```

profile of v0, /device:TPU:14, one launch (start us, length us, event | category | flops | bytes accessed | tf_op | source)
XLA Modules:
  0.0 1767.7 jit_solution(5133293358508405372)
XLA Ops:
  19.0 5.4 collective-permute-done
  38.0 57.3 %all-gather.6.cloned.1.call-done = bf16[4608,1024]{1,0:T(8,128)(2,1)} async-done(((bf16[144,1024]{1,0:T(8,128)(2,1)}), bf16[4608,1024]{1,0:T(8,128)(2,1)}) %all-gather.6.cloned.1.call-update) | async-done | bytes 9437200 | tf_op jit(solution)/shard_map/all_gather | solution.py:195
  112.7 16.5 collective-permute-done.4
  138.3 89.4 %all-gather.8.cloned.1.call-done = bf16[9216,1024]{1,0:T(8,128)(2,1)} async-done(((bf16[288,1024]{1,0:T(8,128)(2,1)}), bf16[9216,1024]{1,0:T(8,128)(2,1)}) %all-gather.8.cloned.1.call-update) | async-done | bytes 18874384 | tf_op jit(solution)/shard_map/all_gather | solution.py:196
  252.7 39.9 %all-gather.10.cloned.1.call-done = bf16[1024,2048]{1,0:T(8,128)(2,1)} async-done(((bf16[32,2048]{1,0:T(8,128)(2,1)}), bf16[1024,2048]{1,0:T(8,128)(2,1)}) %all-gather.10.cloned.1.call-update) | async-done | bytes 4194320 | tf_op jit(solution)/shard_map/all_gather | solution.py:197
  292.6 8.7 fusion.71
  318.0 61.3 %all-gather = bf16[32,16,2]{1,2,0:T(2,128)(2,1)S(1)} all-gather(bf16[1,16,2]{1,2,0:T(2,128)(2,1)S(1)} %convert_bitcast_fusion), channel_id=1, replica_groups=mesh['ha'=8,'wa'=4] {'ha','wa'}, dimensions={0}, use_global_device_ids=true | all-gather | bytes 2112 | tf_op jit(solution)/shard_map/all_gather | solution.py:199
  380.1 16.1 all-gather.12.cloned.1.call-done
  396.2 4.9 fusion.252
  419.6 6.4 pad_maximum_fusion
  443.7 15.4 select_reduce_fusion.1
  460.2 40.0 %psum.7 = f32[5,2,3]{0,2,1:T(4,128)S(1)} all-reduce(f32[5,2,3]{0,2,1:T(4,128)S(1)} %fusion.451), channel_id=1, replica_groups=mesh['ha'=8,'wa'=4] {'ha','wa'}, use_global_device_ids=true, to_apply=%region_5.0 | all-reduce | flops 30 | bytes 240 | tf_op jit(solution)/shard_map/psum | solution.py:204
  526.8 12.5 collective-permute-done.12
  581.0 26.0 %collective-permute-done.16 = bf16[24,1,16,1024]{3,2,1,0:T(8,128)(2,1)S(1)} collective-permute-done((bf16[24,1,16,1024]{3,2,1,0:T(8,128)(2,1)S(1)}, bf16[24,1,16,1024]{3,2,1,0:T(8,128)(2,1)S(1)}, u32[]{:S(2)}, u32[]{:S(2)}) %collective-permute-start.16) | collective-permute-done | bytes 786464 | tf_op jit(solution)/shard_map/ppermute | solution.py:22
  631.5 5.5 fusion.263
  637.0 11.3 fusion.517
  648.3 4.9 fusion.306
  667.5 10.2 multiply_convert_fusion
  681.5 5.8 fusion.239
  701.7 5.1 bitcast_dynamic-update-slice_fusion.16
  706.7 6.0 fusion.298
  754.0 7.5 add_add_fusion
  761.5 6.6 fusion.40
  773.4 5.6 convolution_bitcast_fusion
  779.2 5.3 bitcast_dynamic-update-slice_fusion.15
  804.7 5.3 fusion.179
  819.4 10.2 collective-permute-done.25
  843.1 7.0 collective-permute-done.26
  921.2 24.4 %reduce-scatter.12.cloned.1.call-done = f32[32,2048]{1,0:T(8,128)} async-done(((f32[1024,2048]{1,0:T(8,128)}), f32[32,2048]{1,0:T(8,128)}) %reduce-scatter.12.cloned.1.call-update) | async-done | bytes 262160 | tf_op jit(solution)/shard_map/reduce_scatter | solution.py:228
  947.5 239.7 %reduce-scatter.14.cloned.1.call-done = f32[288,512]{1,0:T(8,128)} async-done(((f32[9216,512]{1,0:T(8,128)}), f32[288,512]{1,0:T(8,128)}) %reduce-scatter.14.cloned.1.call-update) | async-done | bytes 589840 | tf_op jit(solution)/shard_map/reduce_scatter | solution.py:229
  1190.1 210.3 %reduce-scatter.8.cloned.1.call-done = f32[144,1024]{1,0:T(8,128)} async-done(((f32[4608,1024]{1,0:T(8,128)}), f32[144,1024]{1,0:T(8,128)}) %reduce-scatter.8.cloned.1.call-update) | async-done | bytes 589840 | tf_op jit(solution)/shard_map/reduce_scatter | solution.py:226
  1403.3 352.7 %reduce-scatter.10.cloned.1.call-done = f32[288,1024]{1,0:T(8,128)} async-done(((f32[9216,1024]{1,0:T(8,128)}), f32[288,1024]{1,0:T(8,128)}) %reduce-scatter.10.cloned.1.call-update) | async-done | bytes 1179664 | tf_op jit(solution)/shard_map/reduce_scatter | solution.py:227
  (434 shorter events, 426.7 us)
Async XLA Ops:
  7.2 88.1 %all-gather.6.cloned.1.call-start = ((), (), s32[]{:S(2)}) async-start(), calls=%async_computation.5 | async-start | bytes 9732096 | tf_op jit(solution)/shard_map/all_gather | solution.py:195
  9.2 218.5 %all-gather.8.cloned.1.call-start = ((), (), s32[]{:S(2)}) async-start(), calls=%async_computation.6 | async-start | bytes 19464192 | tf_op jit(solution)/shard_map/all_gather | solution.py:196
  11.4 281.2 %all-gather.10.cloned.1.call-start = ((), (), s32[]{:S(2)}) async-start(), calls=%async_computation.7 | async-start | bytes 4325376 | tf_op jit(solution)/shard_map/all_gather | solution.py:197
  12.2 384.0 %all-gather.12.cloned.1.call-start = ((), (), s32[]{:S(2)}) async-start(), calls=%async_computation.8 | async-start | bytes 9732096 | tf_op jit(solution)/shard_map/all_gather | solution.py:198
  13.0 906.8 %reduce-scatter.16.cloned.1.call-start = ((), (), s32[]{:S(2)}) async-start(), calls=%async_computation.13 | async-start | bytes 270336
  13.1 11.3 collective-permute-start
  16.6 11.2 collective-permute-start.1
  106.9 22.4 %collective-permute-start.4 = (bf16[24,1,8,1024]{3,2,1,0:T(8,128)(2,1)S(1)}, bf16[24,1,8,1024]{3,2,1,0:T(8,128)(2,1)S(1)}, u32[]{:S(2)}, u32[]{:S(2)}) collective-permute-start(bf16[24,1,8,1024]{3,2,1,0:T(8,128)(2,1)S(1)} %get-tuple-element.100), channel_id=1, source_target_pairs={{0,4},{4,8},{8,12},{12,16},{16,20},{20,24},{24,28},{1,5},{5,9},{9,... | collective-permute-start | bytes 1179656 | tf_op jit(solution)/shard_map/ppermute | solution.py:22
  110.7 20.7 %collective-permute-start.5 = (bf16[24,1,8,1024]{3,2,1,0:T(8,128)(2,1)S(1)}, bf16[24,1,8,1024]{3,2,1,0:T(8,128)(2,1)S(1)}, u32[]{:S(2)}, u32[]{:S(2)}) collective-permute-start(bf16[24,1,8,1024]{3,2,1,0:T(8,128)(2,1)S(1)} %get-tuple-element.101), channel_id=1, source_target_pairs={{4,0},{8,4},{12,8},{16,12},{20,16},{24,20},{28,24},{5,1},{9,5},{13... | collective-permute-start | bytes 1179656 | tf_op jit(solution)/shard_map/ppermute | solution.py:25
  132.2 105.2 %collective-permute-start.6 = (bf16[24,4,1,1024]{3,2,1,0:T(2,128)(2,1)S(1)}, bf16[24,4,1,1024]{3,2,1,0:T(2,128)(2,1)S(1)}, u32[]{:S(2)}, u32[]{:S(2)}) collective-permute-start(bf16[24,4,1,1024]{3,2,1,0:T(2,128)(2,1)S(1)} %get-tuple-element.86), channel_id=1, source_target_pairs={{0,1},{1,2},{2,3},{4,5},{5,6},{6,7},{8,9},{9,10},{10,11},{12,13},{... | collective-permute-start | bytes 589832 | tf_op jit(solution)/shard_map/ppermute | solution.py:22
  134.1 109.7 %collective-permute-start.7 = (bf16[24,4,1,1024]{3,2,1,0:T(2,128)(2,1)S(1)}, bf16[24,4,1,1024]{3,2,1,0:T(2,128)(2,1)S(1)}, u32[]{:S(2)}, u32[]{:S(2)}) collective-permute-start(bf16[24,4,1,1024]{3,2,1,0:T(2,128)(2,1)S(1)} %get-tuple-element.87), channel_id=1, source_target_pairs={{1,0},{2,1},{3,2},{5,4},{6,5},{7,6},{9,8},{10,9},{11,10},{13,12},{... | collective-permute-start | bytes 589832 | tf_op jit(solution)/shard_map/ppermute | solution.py:25
  308.6 92.4 %collective-permute-start.8 = (bf16[24,1,16,1024]{3,2,1,0:T(8,128)(2,1)}, bf16[24,1,16,1024]{3,2,1,0:T(8,128)(2,1)}, u32[]{:S(2)}, u32[]{:S(2)}) collective-permute-start(bf16[24,1,16,1024]{3,2,1,0:T(8,128)(2,1)} %get-tuple-element.68), channel_id=1, source_target_pairs={{0,4},{4,8},{8,12},{12,16},{16,20},{20,24},{24,28},{1,5},{5,9},{9,... | collective-permute-start | bytes 2359304 | tf_op jit(solution)/shard_map/ppermute | solution.py:22
  312.2 88.9 %collective-permute-start.9 = (bf16[24,1,16,1024]{3,2,1,0:T(8,128)(2,1)}, bf16[24,1,16,1024]{3,2,1,0:T(8,128)(2,1)}, u32[]{:S(2)}, u32[]{:S(2)}) collective-permute-start(bf16[24,1,16,1024]{3,2,1,0:T(8,128)(2,1)} %get-tuple-element.69), channel_id=1, source_target_pairs={{4,0},{8,4},{12,8},{16,12},{20,16},{24,20},{28,24},{5,1},{9,5},{13... | collective-permute-start | bytes 2359304 | tf_op jit(solution)/shard_map/ppermute | solution.py:25
  403.8 14.9 collective-permute-start.10
  406.1 13.0 collective-permute-start.11
  519.7 19.6 %collective-permute-start.12 = (bf16[24,1,8,1024]{3,2,1,0:T(8,128)(2,1)S(1)}, bf16[24,1,8,1024]{3,2,1,0:T(8,128)(2,1)S(1)}, u32[]{:S(2)}, u32[]{:S(2)}) collective-permute-start(bf16[24,1,8,1024]{3,2,1,0:T(8,128)(2,1)S(1)} %get-tuple-element.98), channel_id=1, source_target_pairs={{0,4},{4,8},{8,12},{12,16},{16,20},{20,24},{24,28},{1,5},{5,9},{9,... | collective-permute-start | bytes 1179656 | tf_op jit(solution)/shard_map/ppermute | solution.py:22
  522.7 16.6 collective-permute-start.13
  570.9 36.1 %collective-permute-start.16 = (bf16[24,1,16,1024]{3,2,1,0:T(8,128)(2,1)S(1)}, bf16[24,1,16,1024]{3,2,1,0:T(8,128)(2,1)S(1)}, u32[]{:S(2)}, u32[]{:S(2)}) collective-permute-start(bf16[24,1,16,1024]{3,2,1,0:T(8,128)(2,1)S(1)} %get-tuple-element.66), channel_id=1, source_target_pairs={{0,4},{4,8},{8,12},{12,16},{16,20},{20,24},{24,28},{1,5},{5,9},{9,... | collective-permute-start | bytes 2359304 | tf_op jit(solution)/shard_map/ppermute | solution.py:22
  575.6 31.6 %collective-permute-start.17 = (bf16[24,1,16,1024]{3,2,1,0:T(8,128)(2,1)S(1)}, bf16[24,1,16,1024]{3,2,1,0:T(8,128)(2,1)S(1)}, u32[]{:S(2)}, u32[]{:S(2)}) collective-permute-start(bf16[24,1,16,1024]{3,2,1,0:T(8,128)(2,1)S(1)} %get-tuple-element.67), channel_id=1, source_target_pairs={{4,0},{8,4},{12,8},{16,12},{20,16},{24,20},{28,24},{5,1},{9,5},{13... | collective-permute-start | bytes 2359304 | tf_op jit(solution)/shard_map/ppermute | solution.py:25
  608.8 18.0 %collective-permute-start.18 = (bf16[24,6,1,1024]{3,0,2,1:T(8,128)(2,1)S(1)}, bf16[24,6,1,1024]{3,0,2,1:T(8,128)(2,1)S(1)}, u32[]{:S(2)}, u32[]{:S(2)}) collective-permute-start(bf16[24,6,1,1024]{3,0,2,1:T(8,128)(2,1)S(1)} %copy.193), channel_id=1, source_target_pairs={{0,1},{1,2},{2,3},{4,5},{5,6},{6,7},{8,9},{9,10},{10,11},{12,13},{... | collective-permute-start | bytes 884744 | tf_op jit(solution)/shard_map/ppermute | solution.py:22
  610.9 16.3 collective-permute-start.19
  694.8 250.7 %reduce-scatter.12.cloned.1.call-start = ((), (), s32[]{:S(2)}) async-start(), calls=%async_computation.11 | async-start | bytes 8650752 | tf_op jit(solution)/shard_map/reduce_scatter | solution.py:228
  694.9 20.4 %collective-permute-start.21 = (bf16[24,1,16,512]{3,2,1,0:T(8,128)(2,1)S(1)}, bf16[24,1,16,512]{3,2,1,0:T(8,128)(2,1)S(1)}, u32[]{:S(2)}, u32[]{:S(2)}) collective-permute-start(bf16[24,1,16,512]{3,2,1,0:T(8,128)(2,1)S(1)} %get-tuple-element.83), channel_id=1, source_target_pairs={{4,0},{8,4},{12,8},{16,12},{20,16},{24,20},{28,24},{5,1},{9,5},{13... | collective-permute-start | bytes 1179656 | tf_op jit(solution)/shard_map/ppermute | solution.py:25
  699.3 17.1 collective-permute-start.20
  716.8 12.1 collective-permute-start.22
  779.1 408.1 %reduce-scatter.14.cloned.1.call-start = ((), (), s32[]{:S(2)}) async-start(), calls=%async_computation.12 | async-start | bytes 19464192 | tf_op jit(solution)/shard_map/reduce_scatter | solution.py:229
  803.3 597.1 %reduce-scatter.8.cloned.1.call-start = ((), (), s32[]{:S(2)}) async-start(), calls=%async_computation.9 | async-start | bytes 19464192 | tf_op jit(solution)/shard_map/reduce_scatter | solution.py:226
  810.0 19.6 %collective-permute-start.25 = (bf16[24,1,8,1024]{3,2,1,0:T(8,128)(2,1)S(1)}, bf16[24,1,8,1024]{3,2,1,0:T(8,128)(2,1)S(1)}, u32[]{:S(2)}, u32[]{:S(2)}) collective-permute-start(bf16[24,1,8,1024]{3,2,1,0:T(8,128)(2,1)S(1)} %get-tuple-element.96), channel_id=1, source_target_pairs={{4,0},{8,4},{12,8},{16,12},{20,16},{24,20},{28,24},{5,1},{9,5},{13... | collective-permute-start | bytes 1179656 | tf_op jit(solution)/shard_map/ppermute | solution.py:25
  813.3 18.3 %collective-permute-start.24 = (bf16[24,1,8,1024]{3,2,1,0:T(8,128)(2,1)S(1)}, bf16[24,1,8,1024]{3,2,1,0:T(8,128)(2,1)S(1)}, u32[]{:S(2)}, u32[]{:S(2)}) collective-permute-start(bf16[24,1,8,1024]{3,2,1,0:T(8,128)(2,1)S(1)} %get-tuple-element.97), channel_id=1, source_target_pairs={{0,4},{4,8},{8,12},{12,16},{16,20},{20,24},{24,28},{1,5},{5,9},{9,... | collective-permute-start | bytes 1179656 | tf_op jit(solution)/shard_map/ppermute | solution.py:22
  832.4 17.6 collective-permute-start.26
  835.5 19.9 %collective-permute-start.27 = (bf16[24,4,1,1024]{3,2,1,0:T(2,128)(2,1)S(1)}, bf16[24,4,1,1024]{3,2,1,0:T(2,128)(2,1)S(1)}, u32[]{:S(2)}, u32[]{:S(2)}) collective-permute-start(bf16[24,4,1,1024]{3,2,1,0:T(2,128)(2,1)S(1)} %get-tuple-element.80), channel_id=1, source_target_pairs={{0,1},{1,2},{2,3},{4,5},{5,6},{6,7},{8,9},{9,10},{10,11},{12,13},{... | collective-permute-start | bytes 589832 | tf_op jit(solution)/shard_map/ppermute | solution.py:22
  886.7 869.2 %reduce-scatter.10.cloned.1.call-start = ((), (), s32[]{:S(2)}) async-start(), calls=%async_computation.10 | async-start | bytes 38928384 | tf_op jit(solution)/shard_map/reduce_scatter | solution.py:227
  (106 other events, 3720.8 us)
Sparse Core Ops, SparseCore 0:
  11.5 83.7 all-gather.5
  98.8 128.8 all-gather.7
  231.1 61.4 all-gather.9
  296.0 100.1 all-gather.11
  695.0 102.7 reduce-scatter.15
  800.1 145.4 reduce-scatter.11
  953.1 234.0 reduce-scatter.13
  1194.7 205.6 reduce-scatter.7
  1408.0 347.8 reduce-scatter.9
where the time goes:
time: 1780 us; the launch traced here: 1770 us
  waiting for transfers between devices  1120 us (63%)
  matrix products  345 us (19%)
  blocking collectives  101 us (6%)
  starting transfers between devices  82.2 us (5%)
  other arithmetic  53 us (3%)
  local copies, waits for them, and re-layouts  45 us (3%)
    reduce_scatter x1, waiting for transfers between devices, body(): lax.psum_scatter(conv2_grad, ('ha', 'wa'), scatter_dimension=0, tiled=True)  353 us
    reduce_scatter x1, waiting for transfers between devices, body(): lax.psum_scatter(conv3_grad, ('ha', 'wa'), scatter_dimension=0, tiled=True)  240 us
    reduce_scatter x1, waiting for transfers between devices, body(): lax.psum_scatter(conv1_grad, ('ha', 'wa'), scatter_dimension=0, tiled=True)  210 us
    dot_general x53, matrix products, conv_taps(): jnp.einsum('shwc,co->shwo', window, taps, preferred_element_type=jnp.floa...  141 us
    all_gather x1, waiting for transfers between devices, body(): lax.all_gather(conv2_weight.astype(jnp.bfloat16), ('ha', 'wa'), axis=0, t...  89.4 us
    dot_general x27, matrix products, conv_back(): jnp.einsum('shwc,shwo->co', window, grad_out, preferred_element_type=jnp....  81.4 us
    dot_general x18, matrix products, conv_back(): jnp.einsum('shwo,co->shwc', window, taps, preferred_element_type=jnp.floa...  68.6 us
    ppermute x14, waiting for transfers between devices, with_halo(): lax.ppermute(lax.slice_in_dim(block, block.shape[dim] - width, None, axis...  66.4 us
  transfers between devices with their start and end apart: 37, of which 23 were waited for; matrix products, arithmetic and copies ran while one was open for 16% of the time, Pallas kernels for 0%

commit v1 on v0

--- a/solution.py
+++ b/solution.py
@@ -1,6 +1,10 @@
+import functools
+
 import jax
 import jax.numpy as jnp
 from jax import lax
+from jax.experimental import pallas as pl
+from jax.experimental.pallas import tpu as pltpu
 from jax.sharding import PartitionSpec as P
 
 GROUPS = 5
@@ -41,42 +45,40 @@
 
 
 def conv_taps(padded, weight):
+    kernel = weight.reshape(3, 3, padded.shape[3], weight.shape[1])
+    return lax.conv_general_dilated(
+        padded,
+        kernel,
+        (1, 1),
+        "VALID",
+        dimension_numbers=("NHWC", "HWIO", "NHWC"),
+        preferred_element_type=jnp.float32,
+    )
+
+
+def conv_back(padded, grad_out, weight, back_chan):
     in_chan = padded.shape[3]
-    row_count, col_count = (padded.shape[1] - 2, padded.shape[2] - 2)
-    running = None
-    for tap_index in range(9):
-        row_off, col_off = (tap_index // 3, tap_index % 3)
-        window = padded[:, row_off : row_off + row_count, col_off : col_off + col_count, :]
-        taps = weight[tap_index * in_chan : (tap_index + 1) * in_chan]
-        product = jnp.einsum("shwc,co->shwo", window, taps, preferred_element_type=jnp.float32)
-        running = product if running is None else running + product
-    return running
-
-
-def conv_back(padded, grad_out, weight, need_input):
-    in_chan = padded.shape[3]
-    row_count, col_count = (grad_out.shape[1], grad_out.shape[2])
-    pieces = []
-    for tap_index in range(9):
-        row_off, col_off = (tap_index // 3, tap_index % 3)
-        window = padded[:, row_off : row_off + row_count, col_off : col_off + col_count, :]
-        pieces.append(
-            jnp.einsum("shwc,shwo->co", window, grad_out, preferred_element_type=jnp.float32)
-        )
-    weight_grad = jnp.concatenate(pieces, axis=0)
-    if not need_input:
+    weight_grad = lax.conv_general_dilated(
+        padded,
+        grad_out,
+        (1, 1),
+        "VALID",
+        dimension_numbers=("CHWN", "IHWO", "HWNC"),
+        preferred_element_type=jnp.float32,
+    ).reshape(9 * in_chan, grad_out.shape[3])
+    if not back_chan:
         return (weight_grad, None)
-    grad_padded = with_halo(grad_out, (("ha", 1), ("wa", 2)), 1)
-    running = None
-    for tap_index in range(9):
-        row_off, col_off = (tap_index // 3, tap_index % 3)
-        window = grad_padded[
-            :, 2 - row_off : 2 - row_off + row_count, 2 - col_off : 2 - col_off + col_count, :
-        ]
-        taps = weight[tap_index * in_chan : (tap_index + 1) * in_chan]
-        product = jnp.einsum("shwo,co->shwc", window, taps, preferred_element_type=jnp.float32)
-        running = product if running is None else running + product
-    return (weight_grad, running)
+    grad_padded = widened_field(grad_out)
+    kernel = weight.reshape(3, 3, in_chan, weight.shape[1])[::-1, ::-1, :back_chan]
+    source_grad = lax.conv_general_dilated(
+        grad_padded,
+        kernel,
+        (1, 1),
+        "VALID",
+        dimension_numbers=("NHWC", "HWOI", "NHWC"),
+        preferred_element_type=jnp.float32,
+    )
+    return (weight_grad, source_grad)
 
 
 def upsample(source, weight):
@@ -167,6 +169,754 @@
     weight_new = weight - rate * (gradient + MOMENTUM * moment_new)
     average_new = AVERAGE_DECAY * average + (1.0 - AVERAGE_DECAY) * weight_new
     return (weight_new, moment_new, average_new)
+
+
+def tiled_grads(
+    bottom, skipped, groups, pixel_mask, labels, conv1_weight, conv2_weight, up_weight, conv3_weight,
+    head_weight,
+):
+    gathered = (
+        lax.all_gather(conv1_weight.astype(jnp.bfloat16), ("ha", "wa"), axis=0, tiled=True),
+        lax.all_gather(conv2_weight.astype(jnp.bfloat16), ("ha", "wa"), axis=0, tiled=True),
+        lax.all_gather(up_weight.astype(jnp.bfloat16), ("ha", "wa"), axis=0, tiled=True),
+        lax.all_gather(conv3_weight.astype(jnp.bfloat16), ("ha", "wa"), axis=0, tiled=True),
+        lax.all_gather(head_weight.astype(jnp.bfloat16), ("ha", "wa"), axis=0, tiled=True),
+    )
+    member = (groups[:, None] == jnp.arange(GROUPS)[None, :]).astype(jnp.float32)
+    kept = forward(gathered, bottom, skipped)
+    partial_sums = dice_terms(kept[8], pixel_mask, labels, member)
+    totals = lax.psum(partial_sums, ("ha", "wa"))
+    pad_zero, pre_one, pad_one, pre_two, hidden_two, pad_two, pre_three, hidden_three, logits = kept
+    weight_one, weight_two, weight_up, weight_three, weight_head = gathered
+    loss_value, grad_logits = dice_back(logits, pixel_mask, labels, member, totals)
+    head_grad = jnp.einsum(
+        "shwc,shwk->ck", hidden_three, grad_logits, preferred_element_type=jnp.float32
+    )
+    grad_hidden = jnp.einsum(
+        "shwk,ck->shwc", grad_logits, weight_head, preferred_element_type=jnp.float32
+    )
+    grad_pre_three = smooth_back(pre_three, grad_hidden).astype(jnp.bfloat16)
+    conv3_grad, grad_joined = conv_back(pad_two, grad_pre_three, weight_three, weight_up.shape[1] // 4)
+    grad_upsampled = grad_joined.astype(jnp.bfloat16)
+    up_grad, grad_hidden_two = upsample_back(hidden_two, grad_upsampled, weight_up)
+    grad_pre_two = smooth_back(pre_two, grad_hidden_two).astype(jnp.bfloat16)
+    conv2_grad, grad_hidden_one = conv_back(pad_one, grad_pre_two, weight_two, pad_one.shape[3])
+    grad_pre_one = smooth_back(pre_one, grad_hidden_one).astype(jnp.bfloat16)
+    conv1_grad, _ = conv_back(pad_zero, grad_pre_one, weight_one, 0)
+    sums = (
+        lax.psum_scatter(conv1_grad.astype(jnp.bfloat16), ("ha", "wa"), scatter_dimension=0, tiled=True),
+        lax.psum_scatter(conv2_grad.astype(jnp.bfloat16), ("ha", "wa"), scatter_dimension=0, tiled=True),
+        lax.psum_scatter(up_grad.astype(jnp.bfloat16), ("ha", "wa"), scatter_dimension=0, tiled=True),
+        lax.psum_scatter(conv3_grad.astype(jnp.bfloat16), ("ha", "wa"), scatter_dimension=0, tiled=True),
+        lax.psum_scatter(head_grad.astype(jnp.bfloat16), ("ha", "wa"), scatter_dimension=0, tiled=True),
+    )
+    return (loss_value, *[s.astype(jnp.float32) for s in sums])
+
+
+MESH = pl.DeviceIdType.MESH
+FLOAT = jnp.float32
+HALF = jnp.bfloat16
+
+
+def place():
+    row, col = (lax.axis_index("ha"), lax.axis_index("wa"))
+    return (row // 2, row % 2, col // 2, col % 2)
+
+
+def spot(z, x, y, c):
+    return (2 * z + x, 2 * y + c)
+
+
+def greet_all():
+    row, col = (lax.axis_index("ha"), lax.axis_index("wa"))
+    rows, cols = (lax.axis_size("ha"), lax.axis_size("wa"))
+    barrier = pltpu.get_barrier_semaphore()
+    for step in range(1, rows * cols):
+        other = lax.rem(row * cols + col + step, rows * cols)
+        pl.semaphore_signal(
+            barrier, inc=1, device_id=(other // cols, lax.rem(other, cols)), device_id_type=MESH
+        )
+    pl.semaphore_wait(barrier, rows * cols - 1)
+
+
+def remote(source, target, send_sem, recv_sem, device):
+    return pltpu.make_async_remote_copy(
+        src_ref=source,
+        dst_ref=target,
+        send_sem=send_sem,
+        recv_sem=recv_sem,
+        device_id=device,
+        device_id_type=MESH,
+    )
+
+
+def gelu_of(value):
+    inner = 0.7978845608028654 * (value + 0.044715 * value * value * value)
+    return 0.5 * value * (1.0 + jnp.tanh(inner))
+
+
+def conv_slice(source, weight, parts, index, chan):
+    parts[...] = jnp.zeros_like(parts)
+
+    def row_tap(r, carry):
+        window = source[index, pl.ds(r, 16)].reshape(512, chan)
+        for c in range(3):
+            start = pl.multiple_of((3 * r + c) * chan, chan)
+            parts[c] += jnp.dot(
+                window, weight[pl.ds(start, chan), :], preferred_element_type=FLOAT
+            )
+        return carry
+
+    lax.fori_loop(0, 3, row_tap, 0)
+    shape = (16, 32, 256)
+    column = lax.broadcasted_iota(jnp.int32, shape, 1)
+    low = jnp.where(column > 0, pltpu.roll(parts[0].reshape(shape), 1, 1), 0.0)
+    high = jnp.where(column < 31, pltpu.roll(parts[2].reshape(shape), 31, 1), 0.0)
+    return parts[1].reshape(shape) + low + high
+
+
+def front_kernel(
+    compute,
+    bot, skip, w1, w2, wu, w3, wh,
+    x0_out, h1_out, h2_out, sk_out, w2_out, wu_out, w3_out, wh_out, pre1_out, pre2_out,
+    xr, x0, w1q, w2q, h1s, h1, parts, h2s,
+    send, here, r_bot, r_grp, r_w1, r_w1x, r_w2, r_w2x, r_h1, r_h2, r_skip, r_wh, r_w3, r_wu,
+):
+    z, x, y, c = place()
+    ha, wa = (2 * z + x, 2 * y + c)
+    x_peer, y_peer, c_peer = (spot(z, 1 - x, y, c), spot(z, x, 1 - y, c), spot(z, x, y, 1 - c))
+    mine = ha * 4 + wa
+    greet_all()
+    sends = []
+    stays = []
+
+    def go(source, target, recv_sem, device):
+        copy = remote(source, target, send.at[len(sends)], recv_sem, device)
+        copy.start()
+        sends.append(copy)
+        return copy
+
+    def stay(source, target):
+        copy = pltpu.make_async_copy(source, target, here.at[len(stays)])
+        copy.start()
+        stays.append([copy, False])
+        return stays[-1]
+
+    def settle(entry):
+        entry[0].wait()
+        entry[1] = True
+
+    own_bot = stay(bot.at[ha], xr.at[ha, wa])
+    bots = [
+        go(bot.at[lax.rem(ha + d, 8)], xr.at[ha, wa], r_bot.at[d - 1], (lax.rem(ha + d, 8), wa))
+        for d in range(1, 8)
+    ]
+
+    def spread(shard, whole, rows, recv):
+        place_rows = whole.at[pl.ds(pl.multiple_of(mine * rows, rows), rows)]
+        own = stay(shard.at[:, pl.ds(pl.multiple_of(wa * 256, 256), 256)], place_rows)
+        copies = [[], [], [], []]
+        for dz in range(4):
+            for dw in range(4):
+                if dz == 0 and dw == 0:
+                    continue
+                to = lax.rem(wa + dw, 4)
+                copies[dz].append(
+                    go(
+                        shard.at[:, pl.ds(pl.multiple_of(to * 256, 256), 256)],
+                        place_rows,
+                        recv.at[dz, dw],
+                        (lax.rem(z + dz, 4) * 2 + x, to),
+                    )
+                )
+        return (own, copies)
+
+    def pass_x(whole, rows, got, recv):
+        own, copies = got
+        settle(own)
+        passed = []
+        for dz in range(4):
+            for copy in copies[dz]:
+                copy.wait_recv()
+            origin = lax.rem(z + 4 - dz, 4)
+            block = whole.at[pl.ds(pl.multiple_of((origin * 2 + x) * 4 * rows, 4 * rows), 4 * rows)]
+            passed.append(go(block, block, recv.at[dz], x_peer))
+        return passed
+
+    got_w1 = spread(w1, w1q, 144, r_w1)
+    got_w2 = spread(w2, w2q, 288, r_w2)
+
+    settle(own_bot)
+    for copy in bots:
+        copy.wait_recv()
+    to_c = go(xr.at[:, wa], xr.at[:, wa], r_grp.at[0], c_peer)
+    to_y = go(xr.at[:, wa], xr.at[:, wa], r_grp.at[1], y_peer)
+
+    def spread_z(shard, whole, recv):
+        own = stay(shard, whole.at[z, x, y, c])
+        copies = [
+            go(shard, whole.at[z, x, y, c], recv.at[d - 1], spot(lax.rem(z + d, 4), x, y, c))
+            for d in range(1, 4)
+        ]
+        return (own, copies)
+
+    def spread_two(whole, got, recv, half):
+        own, copies = got
+        settle(own)
+        for copy in copies:
+            copy.wait_recv()
+        low, high = (pl.ds(0, half), pl.ds(half, half))
+        part = whole.at[:, x, y, c]
+        core = go(part, part, recv.at[3], c_peer)
+        part = whole.at[:, x, y, c, :, low]
+        first = go(part, part, recv.at[4], x_peer)
+        part = whole.at[:, x, y, c, :, high]
+        second = go(part, part, recv.at[5], y_peer)
+        return (core, first, second)
+
+    def spread_three(whole, got, recv, half):
+        core, first, second = got
+        low, high = (pl.ds(0, half), pl.ds(half, half))
+        first.wait_recv()
+        part = whole.at[:, :, y, c, :, low]
+        third = go(part, part, recv.at[6], y_peer)
+        part = whole.at[:, 1 - x, y, c, :, low]
+        core_first = go(part, part, recv.at[8], c_peer)
+        second.wait_recv()
+        part = whole.at[:, x, :, c, :, high]
+        fourth = go(part, part, recv.at[7], x_peer)
+        part = whole.at[:, x, 1 - y, c, :, high]
+        core_second = go(part, part, recv.at[9], c_peer)
+        return (core, core_first, core_second, third, fourth)
+
+    def spread_four(whole, got, recv, half):
+        core, core_first, core_second, third, fourth = got
+        low, high = (pl.ds(0, half), pl.ds(half, half))
+        third.wait_recv()
+        part = whole.at[:, :, 1 - y, c, :, low]
+        core_third = go(part, part, recv.at[10], c_peer)
+        fourth.wait_recv()
+        part = whole.at[:, 1 - x, :, c, :, high]
+        core_fourth = go(part, part, recv.at[11], c_peer)
+        return (core, core_first, core_second, core_third, core_fourth)
+
+    own_head = stay(wh, wh_out.at[mine])
+    heads = []
+    for step in range(1, 32):
+        other = lax.rem(mine + step, 32)
+        heads.append(go(wh, wh_out.at[mine], r_wh.at[step - 1], (other // 4, lax.rem(other, 4))))
+
+    passed_w1 = pass_x(w1q, 144, got_w1, r_w1x)
+    got_w3 = spread_z(w3, w3_out, r_w3)
+
+    to_y.wait_recv()
+    part = xr.at[:, 2 * (1 - y) + c]
+    on_c = go(part, part, r_grp.at[2], c_peer)
+    to_c.wait_recv()
+    on_c.wait_recv()
+
+    if compute:
+        x0[:, 0] = jnp.zeros((3, 32, 512), HALF)
+        x0[:, 17] = jnp.zeros((3, 32, 512), HALF)
+        h1[:, 0] = jnp.zeros((3, 32, 1024), HALF)
+        h1[:, 17] = jnp.zeros((3, 32, 1024), HALF)
+
+        def reorder(h, carry):
+            block = xr[h].astype(FLOAT).reshape(4, 3, 2, 8, 512)
+            for s in range(3):
+                for r in range(2):
+                    row = jnp.concatenate([block[w, s, r] for w in range(4)], axis=0)
+                    x0[s, 2 * h + 1 + r] = row.astype(HALF)
+            return carry
+
+        lax.fori_loop(0, 8, reorder, 0)
+    stay(x0.at[:, pl.ds(1, 16)], x0_out)
+
+    for copy in passed_w1:
+        copy.wait_recv()
+    if compute:
+
+        def one(s, carry):
+            value = conv_slice(x0, w1q, parts, s, 512)
+            pre1_out[s] = value
+            h1s[s] = gelu_of(value).astype(HALF)
+            return carry
+
+        lax.fori_loop(0, 3, one, 0)
+
+    def lanes(col):
+        return h1.at[:, pl.ds(1, 16), :, pl.ds(pl.multiple_of(col * 256, 256), 256)]
+
+    own_h1 = stay(h1s, lanes(wa))
+    h1_c = go(h1s, lanes(wa), r_h1.at[0], c_peer)
+    h1_y = go(h1s, lanes(wa), r_h1.at[1], y_peer)
+
+    passed_w2 = pass_x(w2q, 288, got_w2, r_w2x)
+    got_wu = spread_z(wu, wu_out, r_wu)
+    own_skip = stay(skip.at[ha], sk_out.at[ha])
+    skips = [
+        go(skip.at[lax.rem(ha + d, 8)], sk_out.at[ha], r_skip.at[d - 1], (lax.rem(ha + d, 8), wa))
+        for d in range(1, 8)
+    ]
+    got_w3 = spread_two(w3_out, got_w3, r_w3, 256)
+
+    h1_y.wait_recv()
+    h1_on = go(lanes(2 * (1 - y) + c), lanes(2 * (1 - y) + c), r_h1.at[2], c_peer)
+    settle(own_h1)
+    h1_c.wait_recv()
+    h1_on.wait_recv()
+    stay(h1.at[:, pl.ds(1, 16)], h1_out)
+
+    for copy in passed_w2:
+        copy.wait_recv()
+    stay(w2q, w2_out)
+    if compute:
+
+        def two(s, carry):
+            value = conv_slice(h1, w2q, parts, s, 1024)
+            pre2_out[s] = value
+            hidden = gelu_of(value)
+            for w in range(4):
+                tile = hidden[:, 8 * w : 8 * w + 8].reshape(128, 256)
+                h2s[w, pl.ds(pl.multiple_of(s * 128, 128), 128)] = tile.astype(HALF)
+                left = hidden[:, 8 * w - 1] if w > 0 else jnp.zeros((16, 256), FLOAT)
+                h2s[w, pl.ds(pl.multiple_of(384 + s * 16, 16), 16)] = left.astype(HALF)
+                right = hidden[:, 8 * w + 8] if w < 3 else jnp.zeros((16, 256), FLOAT)
+                h2s[w, pl.ds(pl.multiple_of(432 + s * 16, 16), 16)] = right.astype(HALF)
+            return carry
+
+        lax.fori_loop(0, 3, two, 0)
+    h2_lanes = h2_out.at[:, pl.ds(pl.multiple_of(wa * 256, 256), 256)]
+    stay(h2s.at[wa], h2_lanes)
+    h2_got = [
+        go(h2s.at[lax.rem(wa + d, 4)], h2_lanes, r_h2.at[d - 1], (ha, lax.rem(wa + d, 4)))
+        for d in range(1, 4)
+    ]
+
+    got_wu = spread_two(wu_out, got_wu, r_wu, 1024)
+    got_w3 = spread_three(w3_out, got_w3, r_w3, 256)
+    got_wu = spread_three(wu_out, got_wu, r_wu, 1024)
+    got_w3 = spread_four(w3_out, got_w3, r_w3, 256)
+    got_wu = spread_four(wu_out, got_wu, r_wu, 1024)
+    for copy in list(got_w3) + list(got_wu) + h2_got + skips + heads:
+        copy.wait_recv()
+    for entry in stays:
+        if not entry[1]:
+            settle(entry)
+    for copy in sends:
+        copy.wait_send()
+
+
+def front(bot, skip, w1, w2, wu, w3, wh, compute=True):
+    anywhere = pl.BlockSpec(memory_space=pl.ANY)
+    inside = pl.BlockSpec(memory_space=pltpu.VMEM)
+    shape = jax.ShapeDtypeStruct
+    dma = pltpu.SemaphoreType.DMA
+    return pl.pallas_call(
+        functools.partial(front_kernel, compute),
+        name="front",
+        out_shape=(
+            shape((3, 16, 32, 512), HALF),
+            shape((3, 16, 32, 1024), HALF),
+            shape((480, 1024), HALF),
+            shape((8, 192, 512), HALF),
+            shape((9216, 256), HALF),
+            shape((4, 2, 2, 2, 32, 2048), HALF),
+            shape((4, 2, 2, 2, 288, 512), HALF),
+            shape((32, 16, 128), HALF),
+            shape((3, 16, 32, 256), FLOAT),
+            shape((3, 16, 32, 256), FLOAT),
+        ),
+        in_specs=[anywhere] * 7,
+        out_specs=[anywhere] * 8 + [inside] * 2,
+        scratch_shapes=[
+            pltpu.VMEM((8, 4, 48, 512), HALF),
+            pltpu.VMEM((3, 18, 32, 512), HALF),
+            pltpu.VMEM((4608, 256), HALF),
+            pltpu.VMEM((9216, 256), HALF),
+            pltpu.VMEM((3, 16, 32, 256), HALF),
+            pltpu.VMEM((3, 18, 32, 1024), HALF),
+            pltpu.VMEM((3, 512, 256), FLOAT),
+            pltpu.VMEM((4, 480, 256), HALF),
+            dma((136,)),
+            dma((16,)),
+            dma((7,)),
+            dma((3,)),
+            dma((4, 4)),
+            dma((4,)),
+            dma((4, 4)),
+            dma((4,)),
+            dma((3,)),
+            dma((3,)),
+            dma((7,)),
+            dma((31,)),
+            dma((12,)),
+            dma((12,)),
+        ],
+        compiler_params=pltpu.CompilerParams(
+            collective_id=0, has_side_effects=True, vmem_limit_bytes=60 * 1024 * 1024
+        ),
+    )(bot, skip, w1, w2, wu, w3, wh)
+
+
+def sum_kernel(part, out, got, send, recv):
+    row, col = (lax.axis_index("ha"), lax.axis_index("wa"))
+    mine = row * 4 + col
+    greet_all()
+    copies = []
+    for step in range(1, 32):
+        other = lax.rem(mine + step, 32)
+        copy = remote(
+            part,
+            got.at[step],
+            send.at[step - 1],
+            recv.at[step - 1],
+            (other // 4, lax.rem(other, 4)),
+        )
+        copy.start()
+        copies.append(copy)
+    total = part[...]
+    for step in range(1, 32):
+        copies[step - 1].wait_recv()
+        total = total + got[step]
+    out[...] = total
+    for copy in copies:
+        copy.wait_send()
+
+
+def sum_all(part):
+    inside = pl.BlockSpec(memory_space=pltpu.VMEM)
+    return pl.pallas_call(
+        sum_kernel,
+        name="sum_all",
+        out_shape=jax.ShapeDtypeStruct((8, 128), FLOAT),
+        in_specs=[inside],
+        out_specs=inside,
+        scratch_shapes=[
+            pltpu.VMEM((32, 8, 128), FLOAT),
+            pltpu.SemaphoreType.DMA((31,)),
+            pltpu.SemaphoreType.DMA((31,)),
+        ],
+        compiler_params=pltpu.CompilerParams(collective_id=1, has_side_effects=True),
+    )(part)
+
+
+def add_into(total, term, count, pick):
+    def step(i, carry):
+        at_total, at_term = pick(i)
+        value = total[at_total].astype(FLOAT) + term[at_term].astype(FLOAT)
+        total[at_total] = value.astype(HALF)
+        return carry
+
+    lax.fori_loop(0, count, step, 0)
+
+
+def back_kernel(
+    d3, du, d2, d1, dh,
+    g3, gu, g2, g1, gh,
+    l3, c3, y3, x3, z3, lu, cu, yu, xu, zu, m2, a2, b2, t2, m1, a1, b1, t1, hh,
+    send, here, r_3, r_u, r_2, r_1, r_h,
+):
+    z, x, y, c = place()
+    ha, wa = (2 * z + x, 2 * y + c)
+    x_peer, y_peer, c_peer = (spot(z, 1 - x, y, c), spot(z, x, 1 - y, c), spot(z, x, y, 1 - c))
+    mine = ha * 4 + wa
+    greet_all()
+    sends = []
+    stays = []
+
+    def go(source, target, recv_sem, device):
+        copy = remote(source, target, send.at[len(sends)], recv_sem, device)
+        copy.start()
+        sends.append(copy)
+        return copy
+
+    def stay(source, target):
+        copy = pltpu.make_async_copy(source, target, here.at[len(stays)])
+        copy.start()
+        stays.append([copy, False])
+        return stays[-1]
+
+    def settle(entry):
+        entry[0].wait()
+        entry[1] = True
+
+    def all_core(grad, own, core, recv):
+        return (stay(grad.at[:, :, :, c], own), go(grad.at[:, :, :, 1 - c], core, recv.at[0], c_peer))
+
+    def all_y(own, core, along_y, recv, got):
+        settle(got[0])
+        got[1].wait_recv()
+        add_into(own, core, 8, lambda i: ((i // 2, i % 2, 1 - y),) * 2)
+        copy = go(own.at[:, :, 1 - y], along_y, recv.at[1], y_peer)
+        add_into(own, core, 8, lambda i: ((i // 2, i % 2, y),) * 2)
+        return copy
+
+    def all_x(own, along_y, along_x, recv, got):
+        got.wait_recv()
+        add_into(own, along_y, 4, lambda i: ((i, 1 - x, y), (i, 1 - x)))
+        copy = go(own.at[:, 1 - x, y], along_x, recv.at[2], x_peer)
+        add_into(own, along_y, 4, lambda i: ((i, x, y), (i, x)))
+        return copy
+
+    def all_z(own, along_x, along_z, recv, got):
+        got.wait_recv()
+        add_into(own, along_x, 4, lambda i: ((i, x, y), (i,)))
+        return [
+            go(
+                own.at[lax.rem(z + d, 4), x, y],
+                along_z.at[d - 1],
+                recv.at[2 + d],
+                spot(lax.rem(z + d, 4), x, y, c),
+            )
+            for d in range(1, 4)
+        ]
+
+    def all_end(own, along_z, out, got):
+        total = own[z, x, y].astype(FLOAT)
+        for d in range(3):
+            got[d].wait_recv()
+            total = total + along_z[d].astype(FLOAT)
+        out[...] = total
+
+    def quarter_x(grad, own, along_x, recv):
+        return (stay(grad.at[:, x], own), go(grad.at[:, 1 - x], along_x, recv.at[0], x_peer))
+
+    def quarter_z(own, along_x, along_z, recv, got):
+        settle(got[0])
+        got[1].wait_recv()
+        add_into(own, along_x, 16, lambda i: ((i // 4, i % 4),) * 2)
+        return [
+            go(
+                own.at[lax.rem(z + d, 4)],
+                along_z.at[d - 1],
+                recv.at[d],
+                spot(lax.rem(z + d, 4), x, y, c),
+            )
+            for d in range(1, 4)
+        ]
+
+    def quarter_w(own, along_z, total, out, recv, got):
+        for copy in got:
+            copy.wait_recv()
+
+        def step(w, carry):
+            value = own[z, w].astype(FLOAT)
+            for d in range(3):
+                value = value + along_z[d, w].astype(FLOAT)
+            total[w] = value.astype(HALF)
+            return carry
+
+        lax.fori_loop(0, 4, step, 0)
+        target = out.at[:, pl.ds(pl.multiple_of(wa * 256, 256), 256)]
+        stay(total.at[wa], target)
+        return [
+            go(total.at[lax.rem(wa + d, 4)], target, recv.at[3 + d], (ha, lax.rem(wa + d, 4)))
+            for d in range(1, 4)
+        ]
+
+    s3 = all_core(d3, l3, c3, r_3)
+    su = all_core(du, lu, cu, r_u)
+    s2 = quarter_x(d2, m2, a2, r_2)
+    s1 = quarter_x(d1, m1, a1, r_1)
+    own_head = stay(dh.at[mine], hh.at[0])
+    heads = []
+    for step in range(1, 32):
+        other = lax.rem(mine + step, 32)
+        heads.append(
+            go(dh.at[other], hh.at[step], r_h.at[step - 1], (other // 4, lax.rem(other, 4)))
+        )
+    s3 = all_y(l3, c3, y3, r_3, s3)
+    su = all_y(lu, cu, yu, r_u, su)
+    s2 = quarter_z(m2, a2, b2, r_2, s2)
+    s3 = all_x(l3, y3, x3, r_3, s3)
+    su = all_x(lu, yu, xu, r_u, su)
+    s1 = quarter_z(m1, a1, b1, r_1, s1)
+    s3 = all_z(l3, x3, z3, r_3, s3)
+    su = all_z(lu, xu, zu, r_u, su)
+    s2 = quarter_w(m2, b2, t2, g2, r_2, s2)
+    s1 = quarter_w(m1, b1, t1, g1, r_1, s1)
+    settle(own_head)
+    total = hh[0]
+    for step in range(1, 32):
+        heads[step - 1].wait_recv()
+        total = total + hh[step]
+    gh[...] = total
+    all_end(l3, z3, g3, s3)
+    all_end(lu, zu, gu, su)
+    for copy in s2 + s1:
+        copy.wait_recv()
+    for entry in stays:
+        if not entry[1]:
+            settle(entry)
+    for copy in sends:
+        copy.wait_send()
+
+
+def back(d3, du, d2, d1, dh):
+    anywhere = pl.BlockSpec(memory_space=pl.ANY)
+    inside = pl.BlockSpec(memory_space=pltpu.VMEM)
+    shape = jax.ShapeDtypeStruct
+    dma = pltpu.SemaphoreType.DMA
+
+    def whole(rows, cols):
+        return [
+            pltpu.VMEM((4, 2, 2, rows, cols), HALF),
+            pltpu.VMEM((4, 2, 2, rows, cols), HALF),
+            pltpu.VMEM((4, 2, rows, cols), HALF),
+            pltpu.VMEM((4, rows, cols), HALF),
+            pltpu.VMEM((3, rows, cols), HALF),
+        ]
+
+    def quarter(rows):
+        return [
+            pltpu.VMEM((4, 4, rows, 256), HALF),
+            pltpu.VMEM((4, 4, rows, 256), HALF),
+            pltpu.VMEM((3, 4, rows, 256), HALF),
+            pltpu.VMEM((4, rows, 256), HALF),
+        ]
+
+    return pl.pallas_call(
+        back_kernel,
+        name="back",
+        out_shape=(
+            shape((288, 512), FLOAT),
+            shape((32, 2048), FLOAT),
+            shape((288, 1024), HALF),
+            shape((144, 1024), HALF),
+            shape((16, 128), FLOAT),
+        ),
+        in_specs=[anywhere] * 5,
+        out_specs=[inside] * 5,
+        scratch_shapes=whole(288, 512)
+        + whole(32, 2048)
+        + quarter(288)
+        + quarter(144)
+        + [
+            pltpu.VMEM((32, 16, 128), FLOAT),
+            dma((64,)),
+            dma((8,)),
+            dma((6,)),
+            dma((6,)),
+            dma((7,)),
+            dma((7,)),
+            dma((31,)),
+        ],
+        compiler_params=pltpu.CompilerParams(
+            collective_id=2, has_side_effects=True, vmem_limit_bytes=60 * 1024 * 1024
+        ),
+    )(d3, du, d2, d1, dh)
+
+
+def conv_with(source, weight, col_rim):
+    chan = source.shape[3]
+    return lax.conv_general_dilated(
+        source,
+        weight.reshape(3, 3, chan, weight.shape[1]),
+        (1, 1),
+        ((1, 1), (col_rim, col_rim)),
+        dimension_numbers=("NHWC", "HWIO", "NHWC"),
+        preferred_element_type=FLOAT,
+    )
+
+
+def conv_weight_grad(source, grad, col_rim):
+    return lax.conv_general_dilated(
+        source,
+        grad,
+        (1, 1),
+        ((1, 1), (col_rim, col_rim)),
+        dimension_numbers=("CHWN", "IHWO", "HWNC"),
+        preferred_element_type=FLOAT,
+    ).reshape(9 * source.shape[3], grad.shape[3])
+
+
+def conv_source_grad(grad, weight, chan, col_rim):
+    kernel = weight.reshape(3, 3, -1, weight.shape[1])[::-1, ::-1, :chan]
+    return lax.conv_general_dilated(
+        grad,
+        kernel,
+        (1, 1),
+        ((1, 1), (col_rim, col_rim)),
+        dimension_numbers=("NHWC", "HWOI", "NHWC"),
+        preferred_element_type=FLOAT,
+    )
+
+
+def with_cols(block):
+    return with_halo(block, (("wa", 2),), 1)
+
+
+def sliced_grads(
+    bottom, skipped, groups, pixel_mask, labels, weight_one, weight_two, weight_up, weight_three,
+    weight_head,
+):
+    ha = lax.axis_index("ha")
+    code = lax.all_to_all(pixel_mask + 2 * labels, "ha", 0, 1, tiled=True)
+    mask, label = (code % 2, code // 2)
+    head_rows = jnp.pad(weight_head.astype(HALF), ((0, 0), (0, 126)))
+    x0, h1, h2, skip, w2, wu, w3, wh, pre_one, pre_two = front(
+        bottom.reshape(8, 48, 512),
+        skipped.reshape(8, 192, 512),
+        weight_one.astype(HALF),
+        weight_two.astype(HALF),
+        weight_up.astype(HALF),
+        weight_three.astype(HALF),
+        head_rows,
+    )
+    wu = wu.reshape(1024, 2048)
+    w3 = w3.reshape(9216, 512)
+    wh = wh.reshape(512, 128)[:, :2]
+    skip = skip.reshape(8, 3, 4, 16, 512).transpose(1, 0, 2, 3, 4).reshape(3, 32, 16, 512)
+    skip = with_cols(skip)
+    hidden_two = h2[:384].reshape(3, 16, 8, 1024)
+    ups = upsample(hidden_two, wu).astype(HALF)
+    taps = wu.reshape(1024, 2, 2, 512)
+    rims = [
+        jnp.einsum(
+            "pc,caq->paq",
+            h2[384 + 48 * side : 432 + 48 * side],
+            taps[:, :, 1 - side],
+            preferred_element_type=FLOAT,
+        )
+        .astype(HALF)
+        .reshape(3, 32, 1, 512)
+        for side in range(2)
+    ]
+    joined = jnp.concatenate(
+        [jnp.concatenate([rims[0], ups, rims[1]], axis=2), skip], axis=3
+    )
+    pre_three = conv_with(joined, w3, 0)
+    hidden_three = smooth(pre_three).astype(HALF)
+    logits = jnp.einsum("shwc,ck->shwk", hidden_three, wh, preferred_element_type=FLOAT)
+    member = (groups[:, None] == jnp.arange(GROUPS)[None, :]).astype(FLOAT)
+    member = lax.dynamic_slice_in_dim(member, 3 * ha, 3, axis=0)
+    sums = dice_terms(logits, mask, label, member).reshape(1, 30)
+    sums = sum_all(jnp.pad(sums, ((0, 7), (0, 98))))
+    totals = sums[0, :30].reshape(GROUPS, 2, 3)
+    loss_value, grad_logits = dice_back(logits, mask, label, member, totals)
+    head_grad = jnp.einsum("shwc,shwk->ck", hidden_three, grad_logits, preferred_element_type=FLOAT)
+    grad_hidden = jnp.einsum("shwk,ck->shwc", grad_logits, wh, preferred_element_type=FLOAT)
+    grad_three = smooth_back(pre_three, grad_hidden).astype(HALF)
+    grad_wide = with_cols(grad_three)
+    d3 = conv_weight_grad(joined, grad_three, 0).astype(HALF)
+    grad_ups = conv_source_grad(grad_wide, w3, 512, 0).astype(HALF)
+    du, grad_hidden_two = upsample_back(hidden_two, grad_ups, wu)
+    grad_hidden_two = lax.all_to_all(grad_hidden_two.astype(HALF), "wa", 3, 2, tiled=True)
+    grad_two = smooth_back(pre_two, grad_hidden_two.astype(FLOAT)).astype(HALF)
+    d2 = conv_weight_grad(h1, grad_two, 1).astype(HALF)
+    grad_hidden_one = conv_source_grad(grad_two, w2, 1024, 1).astype(HALF)
+    grad_hidden_one = lax.psum_scatter(grad_hidden_one, "wa", scatter_dimension=3, tiled=True)
+    grad_one = smooth_back(pre_one, grad_hidden_one.astype(FLOAT)).astype(HALF)
+    d1 = conv_weight_grad(x0, grad_one, 1).astype(HALF)
+    g3, gu, g2, g1, gh = back(
+        d3.reshape(4, 2, 2, 2, 288, 512),
+        du.astype(HALF).reshape(4, 2, 2, 2, 32, 2048),
+        d2.reshape(4, 2, 4, 288, 256),
+        d1.reshape(4, 2, 4, 144, 256),
+        jnp.pad(head_grad, ((0, 0), (0, 126))).reshape(32, 16, 128),
+    )
+    return (loss_value, g1.astype(FLOAT), g2.astype(FLOAT), gu, g3, gh[:, :2])
 
 
 def body(
@@ -191,43 +941,20 @@
     head_momentum,
     head_average,
 ):
-    gathered = (
-        lax.all_gather(conv1_weight.astype(jnp.bfloat16), ("ha", "wa"), axis=0, tiled=True),
-        lax.all_gather(conv2_weight.astype(jnp.bfloat16), ("ha", "wa"), axis=0, tiled=True),
-        lax.all_gather(up_weight.astype(jnp.bfloat16), ("ha", "wa"), axis=0, tiled=True),
-        lax.all_gather(conv3_weight.astype(jnp.bfloat16), ("ha", "wa"), axis=0, tiled=True),
-        lax.all_gather(head_weight.astype(jnp.bfloat16), ("ha", "wa"), axis=0, tiled=True),
-    )
-    member = (groups[:, None] == jnp.arange(GROUPS)[None, :]).astype(jnp.float32)
-    kept = forward(gathered, bottom, skipped)
-    partial_sums = dice_terms(kept[8], pixel_mask, labels, member)
-    totals = lax.psum(partial_sums, ("ha", "wa"))
-    totals, gathered = lax.optimization_barrier((totals, gathered))
-    kept = forward(gathered, bottom, skipped)
-    pad_zero, pre_one, pad_one, pre_two, hidden_two, pad_two, pre_three, hidden_three, logits = kept
-    weight_one, weight_two, weight_up, weight_three, weight_head = gathered
-    loss_value, grad_logits = dice_back(logits, pixel_mask, labels, member, totals)
-    head_grad = jnp.einsum(
-        "shwc,shwk->ck", hidden_three, grad_logits, preferred_element_type=jnp.float32
-    )
-    grad_hidden = jnp.einsum(
-        "shwk,ck->shwc", grad_logits, weight_head, preferred_element_type=jnp.float32
-    )
-    grad_pre_three = smooth_back(pre_three, grad_hidden).astype(jnp.bfloat16)
-    conv3_grad, grad_joined = conv_back(pad_two, grad_pre_three, weight_three, True)
-    up_chan = weight_up.shape[1] // 4
-    grad_upsampled = grad_joined[..., :up_chan].astype(jnp.bfloat16)
-    up_grad, grad_hidden_two = upsample_back(hidden_two, grad_upsampled, weight_up)
-    grad_pre_two = smooth_back(pre_two, grad_hidden_two).astype(jnp.bfloat16)
-    conv2_grad, grad_hidden_one = conv_back(pad_one, grad_pre_two, weight_two, True)
-    grad_pre_one = smooth_back(pre_one, grad_hidden_one).astype(jnp.bfloat16)
-    conv1_grad, _ = conv_back(pad_zero, grad_pre_one, weight_one, False)
-    conv1_grad, conv2_grad, up_grad, conv3_grad, head_grad = (
-        lax.psum_scatter(conv1_grad, ("ha", "wa"), scatter_dimension=0, tiled=True),
-        lax.psum_scatter(conv2_grad, ("ha", "wa"), scatter_dimension=0, tiled=True),
-        lax.psum_scatter(up_grad, ("ha", "wa"), scatter_dimension=0, tiled=True),
-        lax.psum_scatter(conv3_grad, ("ha", "wa"), scatter_dimension=0, tiled=True),
-        lax.psum_scatter(head_grad, ("ha", "wa"), scatter_dimension=0, tiled=True),
+    split = bottom.shape[0] == 24 and bottom.shape[1:3] == (2, 8) and bottom.shape[3] == 512
+    split = split and (lax.axis_size("ha"), lax.axis_size("wa")) == (8, 4)
+    grads = sliced_grads if split else tiled_grads
+    loss_value, conv1_grad, conv2_grad, up_grad, conv3_grad, head_grad = grads(
+        bottom,
+        skipped,
+        groups,
+        pixel_mask,
+        labels,
+        conv1_weight,
+        conv2_weight,
+        up_weight,
+        conv3_weight,
+        head_weight,
     )
     first = renew_state(conv1_weight, conv1_momentum, conv1_average, conv1_grad, RATE_CONV)
     second = renew_state(conv2_weight, conv2_momentum, conv2_average, conv2_grad, RATE_CONV)

time: 1780 us -> 778 us (0.44)
  waiting for transfers between devices: 1120 us -> 21.3 us
  Pallas kernels: 0 us -> 402 us
  matrix products: 345 us -> 198 us
  blocking collectives: 101 us -> 0 us
  starting transfers between devices: 82.2 us -> 20.6 us
  local copies, waits for them, and re-layouts: 45 us -> 76.7 us
  other arithmetic: 53 us -> 29.1 us
    reduce_scatter x4 -> x1, waiting for transfers between devices: 827 us -> 14.4 us  [sliced_grads(): lax.psum_scatter(grad_hidden_one, 'wa', scatter_dimension=3, tiled=True)]
    pallas_call x0 -> x3, Pallas kernels: none -> 402 us  [the longest x1 216 us: front(): pl.pallas_call(functools.partial(front_kernel, compute), name='front', ou...]
    dot_general x100 -> x4, matrix products: 302 us -> 11.7 us  [the longest x2 4.37 us: sliced_grads(): jnp.einsum('pc,caq->paq', h2[384 + 48 * side:432 + 48 * side], taps[:, :,...]
    all_gather x4 -> x0, waiting for transfers between devices: 203 us -> none  [the longest x1 89.4 us: body(): lax.all_gather(conv2_weight.astype(jnp.bfloat16), ('ha', 'wa'), axis=0, t...]
    conv_general_dilated x0 -> x6, matrix products: none -> 173 us  [the longest x3 77 us: conv_weight_grad(): lax.conv_general_dilated(source, grad, (1, 1), ((1, 1), (col_rim, col_rim...]
    ppermute x14 -> x2, waiting for transfers between devices: 66.4 us -> 0.11 us  [with_halo(): lax.ppermute(lax.slice_in_dim(block, block.shape[dim] - width, None, axis...]
    all_gather x1 -> x0, blocking collectives: 61.3 us -> none  [body(): lax.all_gather(head_weight.astype(jnp.bfloat16), ('ha', 'wa'), axis=0, ti...]
    psum x1 -> x0, blocking collectives: 40 us -> none  [body(): totals = lax.psum(partial_sums, ('ha', 'wa'))]
  transfers between devices with their start and end apart: 37 -> 7, of which waited for: 23 -> 4; matrix products, arithmetic and copies ran while one was open for 16% -> 9% of each run, Pallas kernels for 0% -> 0%
where the time goes in v1:
time: 778 us; the launch traced here: 765 us
  Pallas kernels  402 us (52%)
  matrix products  198 us (25%)
  local copies, waits for them, and re-layouts  76.7 us (10%)
  other arithmetic  29.1 us (4%)
  waiting for transfers between devices  21.3 us (3%)
  starting transfers between devices  20.6 us (3%)
  between operations  16.7 us (2%)
    pallas_call x1, Pallas kernels, front(): pl.pallas_call(functools.partial(front_kernel, compute), name='front', ou...  216 us
    pallas_call x1, Pallas kernels, back(): pl.pallas_call(back_kernel, name='back', out_shape=(shape((288, 512), FLO...  176 us
    conv_general_dilated x3, matrix products, conv_weight_grad(): lax.conv_general_dilated(source, grad, (1, 1), ((1, 1), (col_rim, col_rim...  77 us
    conv_general_dilated x2, matrix products, conv_source_grad(): lax.conv_general_dilated(grad, kernel, (1, 1), ((1, 1), (col_rim, col_rim...  51.9 us
    conv_general_dilated x1, matrix products, conv_with(): lax.conv_general_dilated(source, weight.reshape(3, 3, chan, weight.shape[...  43.9 us
    unnamed x112, local copies, waits for them, and re-layouts  21.9 us
  transfers between devices with their start and end apart: 7, of which 4 were waited for; matrix products, arithmetic and copies ran while one was open for 9% of the time, Pallas kernels for 0%

profile of v1, /device:TPU:14, one launch (start us, length us, event | category | flops | bytes accessed | tf_op | source)
XLA Modules:
  0.0 764.7 jit_solution(15128637373776929115)
XLA Ops:
  13.4 215.6 %front.1 = (bf16[3,16,32,512]{3,2,1,0:T(8,128)(2,1)}, bf16[3,16,32,1024]{3,2,1,0:T(8,128)(2,1)}, bf16[480,1024]{1,0:T(8,128)(2,1)}, bf16[8,192,512]{2,1,0:T(8,12...) custom-call(bf16[8,48,512]{2,1,0:T(8,128)(2,1)} %bitcast.156, ...), custom_call_target="tpu_custom_call" | custom-call | tf_op jit(solution)/shard_map/front/pallas_call | solution.py:515
  229.0 2.9 copy.272
  234.3 3.3 collective-permute-start.1
  238.4 5.9 all-to-all-start
  244.3 7.8 %reshape_reshape.7 = bf16[1024,2,2,512]{3,2,1,0:T(2,128)(2,1)} reshape(bf16[4,2,2,2,32,2048]{5,4,3,2,1,0:T(8,128)(2,1)} %get-tuple-element.32) | data formatting | bytes 8388608 | tf_op jit(solution)/shard_map/reshape;reshape | solution.py:874
  252.2 9.5 %fusion.110 = (bf16[1024,2,1,512]{3,2,1,0:T(2,128)(2,1)S(1)}, bf16[1024,2,1,512]{3,2,1,0:T(2,128)(2,1)}) fusion(bf16[1024,2,2,512]{3,2,1,0:T(2,128)(2,1)} %reshape_reshape.7), kind=kLoop, calls=%fused_computation.155 | loop fusion | bytes 8388608 | tf_op jit(solution)/shard_map/slice | solution.py:879
  263.2 6.4 copy.323
  269.5 3.0 fusion.60
  272.6 5.2 fusion.52
  279.6 4.3 copy.324
  287.0 6.8 maximum_maximum_fusion
  293.8 43.9 %fusion.115 = f32[3,32,16,512]{3,0,2,1:T(4,128)S(1)} fusion(bf16[3,32,18,1024]{3,0,2,1:T(4,128)(2,1)S(1)} %maximum_maximum_fusion, bf16[3,3,1024,512]{3,2,1,0:T(8,128)(2,1)} %bitcast.162), kind=kOutput, calls=%fused_computation.160 | convolution fusion | flops 14193524736 | bytes 16121856 | tf_op jit(solution)/shard_map/conv_general_dilated | solution.py:813
  343.3 10.4 %sum_all.1 = f32[8,128]{1,0:T(8,128)} custom-call(f32[8,128]{1,0:T(8,128)} %pad.13.part), custom_call_target="tpu_custom_call" | custom-call | tf_op jit(solution)/shard_map/sum_all/pallas_call | solution.py:589
  355.7 4.2 fusion.55
  359.9 3.1 fusion.11
  364.1 41.0 %convolution_convert_fusion = bf16[3,3,1024,512]{3,2,1,0:T(8,128)(2,1)} fusion(bf16[3,32,18,1024]{3,0,2,1:T(4,128)(2,1)S(1)} %bitcast.144, bf16[3,32,16,512]{3,2,1,0:T(8,128)(2,1)S(1)} %fusion.11), kind=kOutput, calls=%fused_computation.2 | convolution fusion | flops 14198243328 | bytes 14548992 | tf_op jit(solution)/shard_map/conv_general_dilated | solution.py:824
  407.9 3.5 collective-permute-start.3
  416.2 25.3 %fusion.24 = bf16[3,32,16,512]{3,0,2,1:T(4,128)(2,1)S(1)} fusion(bf16[3,3,1024,512]{3,2,1,0:T(8,128)(2,1)} %bitcast.163, bf16[3,32,18,512]{3,2,1,0:T(8,128)(2,1)S(1)} %pad_maximum_fusion), kind=kOutput, calls=%fused_computation.36 | convolution fusion | flops 7097548800 | bytes 8060928 | tf_op jit(solution)/shard_map/conv_general_dilated | solution.py:836
  444.1 6.1 copy.297
  450.2 8.6 %reshape.196 = bf16[4,2,49152]{2,1,0:T(2,128)(2,1)} reshape(bf16[1024,3,8,16]{3,2,1,0:T(8,128)(2,1)} %bitcast.134) | data formatting | bytes 1572864
  458.8 3.6 all-to-all-start.1
  462.4 4.3 bitcast_convert_fusion
  466.7 5.0 all-to-all-done.1
  471.7 5.8 reshape.197
  477.5 6.9 copy.298
  485.5 26.5 %fusion.63 = bf16[3,16,32,1024]{3,0,2,1:T(4,128)(2,1)S(1)} fusion(bf16[3,3,1024,256]{3,2,1,0:T(8,128)(2,1)} %bitcast.164, bf16[3,16,32,256]{3,2,1,0:T(8,128)(2,1)S(1)} %fusion.40), kind=kOutput, calls=%fused_computation.76 | convolution fusion | flops 6801063936 | bytes 8650752 | tf_op jit(solution)/shard_map/conv_general_dilated | solution.py:836
  512.1 2.9 copy.380
  516.1 23.6 %fusion.12 = bf16[3,3,1024,256]{3,2,1,0:T(8,128)(2,1)} fusion(bf16[3,16,32,1024]{3,2,1,0:T(8,128)(2,1)} %get-tuple-element.36, bf16[3,16,32,256]{3,2,1,0:T(8,128)(2,1)S(1)} %copy-done.17), kind=kOutput, calls=%fused_computation.19 | convolution fusion | flops 6803423232 | bytes 8650752 | tf_op jit(solution)/shard_map/conv_general_dilated | solution.py:824
  539.7 14.4 %reduce-scatter.2.cloned.1.call-done = bf16[3,16,32,256]{3,2,1,0:T(8,128)(2,1)} async-done(((bf16[3,16,32,1024]{3,2,1,0:T(8,128)(2,1)}), bf16[3,16,32,256]{3,2,1,0:T(8,128)(2,1)}) %reduce-scatter.2.cloned.1.call-update) | async-done | bytes 786448 | tf_op jit(solution)/shard_map/reduce_scatter | solution.py:909
  556.4 12.4 %fusion.21 = bf16[3,3,512,256]{3,2,1,0:T(8,128)(2,1)} fusion(bf16[3,16,32,512]{3,2,1,0:T(8,128)(2,1)S(1)} %copy-done.45, bf16[3,16,32,256]{3,2,1,0:T(8,128)(2,1)S(1)} %fusion.31), kind=kOutput, calls=%fused_computation.33 | convolution fusion | flops 3401711616 | bytes 4718592 | tf_op jit(solution)/shard_map/conv_general_dilated | solution.py:824
  568.8 175.8 %back.1 = (f32[288,512]{1,0:T(8,128)}, f32[32,2048]{1,0:T(8,128)}, bf16[288,1024]{1,0:T(8,128)(2,1)}, bf16[144,1024]{1,0:T(8,128)(2,1)}, f32[16,128]{1,0:T(8,128)}) custom-call(bf16[4,2,2,2,288,512]{5,4,3,2,1,0:T(8,128)(2,1)} %bitcast.140, bf16[4,2,2,2,32,2048]{5,4,3,2,1,0:T(8,128)(2,1)} %bitcast.145, bf16[4,2,4,288,256]{4,3,2,1,0:T(8,128)(2,1)} %bitcast.142, ...), custom_call_target="tpu_custom_call" | custom-call | tf_op jit(solution)/shard_map/back/pallas_call | solution.py:779
  748.7 3.4 add_multiply_fusion
  (173 shorter events, 46.4 us)
Async XLA Ops:
  229.0 8.6 %copy-start.31 = (s32[24,4,16]{0,2,1:T(8,128)S(1)}, s32[24,4,16]{0,2,1:T(8,128)}, u32[]{:S(2)}) copy-start(s32[24,4,16]{0,2,1:T(8,128)} %param.23) | copy-start | bytes 18436
  229.0 8.6 %copy-start.32 = (s32[24,4,16]{0,2,1:T(8,128)S(1)}, s32[24,4,16]{0,2,1:T(8,128)}, u32[]{:S(2)}) copy-start(s32[24,4,16]{0,2,1:T(8,128)} %param.24) | copy-start | bytes 18436
  232.0 54.9 %collective-permute-start = (bf16[3,32,1,512]{3,0,2,1:T(4,128)(2,1)S(1)}, bf16[3,32,1,512]{3,0,2,1:T(4,128)(2,1)S(1)}, u32[]{:S(2)}, u32[]{:S(2)}) collective-permute-start(bf16[3,32,1,512]{3,0,2,1:T(4,128)(2,1)S(1)} %get-tuple-element.163), channel_id=1, source_target_pairs={{0,1},{1,2},{2,3},{4,5},{5,6},{6,7},{8,9},{9,10},{10,11},{12,13},{... | collective-permute-start | bytes 294920 | tf_op jit(solution)/shard_map/ppermute | solution.py:26
  234.3 52.6 %collective-permute-start.1 = (bf16[3,32,1,512]{3,0,2,1:T(4,128)(2,1)S(1)}, bf16[3,32,1,512]{3,0,2,1:T(4,128)(2,1)S(1)}, u32[]{:S(2)}, u32[]{:S(2)}) collective-permute-start(bf16[3,32,1,512]{3,0,2,1:T(4,128)(2,1)S(1)} %get-tuple-element.164), channel_id=1, source_target_pairs={{1,0},{2,1},{3,2},{5,4},{6,5},{7,6},{9,8},{10,9},{11,10},{13,12},{... | collective-permute-start | bytes 294920 | tf_op jit(solution)/shard_map/ppermute | solution.py:29
  238.4 47.2 %all-to-all-start = ((s32[8,1,192]{2,1,0:T(1,128)}), s32[8,1,192]{2,1,0:T(1,128)S(1)}, u32[]{:S(2)}, u32[]{:S(2)}) async-start(s32[8,1,192]{2,1,0:T(1,128)} %reshape.194), calls=%async_computation | async-start | bytes 16384 | tf_op jit(solution)/shard_map/all_to_all | solution.py:855
  252.2 9.5 %copy-start.18 = (bf16[480,1024]{1,0:T(8,128)(2,1)S(1)}, bf16[480,1024]{1,0:T(8,128)(2,1)}, u32[]{:S(2)}) copy-start(bf16[480,1024]{1,0:T(8,128)(2,1)} %get-tuple-element.31) | copy-start | bytes 2949124
  261.8 10.8 %copy-start.14 = (bf16[384,1024]{1,0:T(8,128)(2,1)}, bf16[384,1024]{1,0:T(8,128)(2,1)S(1)}, u32[]{:S(2)}) copy-start(bf16[384,1024]{1,0:T(8,128)(2,1)S(1)} %slice.50) | copy-start | bytes 2359300
  279.4 6.1 copy-start.47
  293.8 43.9 %copy-start.1 = (bf16[3,32,18,1024]{3,0,2,1:T(4,128)(2,1)}, bf16[3,32,18,1024]{3,0,2,1:T(4,128)(2,1)S(1)}, u32[]{:S(2)}) copy-start(bf16[3,32,18,1024]{3,0,2,1:T(4,128)(2,1)S(1)} %maximum_maximum_fusion) | copy-start | bytes 10616836
  355.6 8.4 %slice-start = ((s8[4718592]{0:T(1024)(128)(4,1)}), s8[4194304]{0:T(1024)(128)(4,1)S(1)}, s32[]{:S(2)}) async-start(s8[4718592]{0:T(1024)(128)(4,1)} %bitcast.143), calls=%async_computation.4 | async-start | bytes 8388608
  364.1 41.1 %copy-start.28 = (f32[512,2]{1,0:T(8,128)S(1)}, f32[512,2]{1,0:T(8,128)}, u32[]{:S(2)}) copy-start(f32[512,2]{1,0:T(8,128)} %fusion.55) | copy-start | bytes 12292
  364.1 41.8 %copy-start.30 = (bf16[3,32,1,512]{3,2,1,0:T(2,128)(2,1)S(1)}, bf16[3,32,1,512]{3,2,1,0:T(2,128)(2,1)}, u32[]{:S(2)}) copy-start(bf16[3,32,1,512]{3,2,1,0:T(2,128)(2,1)} %get-tuple-element.165) | copy-start | bytes 294916
  364.1 43.8 %copy-start.29 = (bf16[3,32,1,512]{3,2,1,0:T(2,128)(2,1)S(1)}, bf16[3,32,1,512]{3,2,1,0:T(2,128)(2,1)}, u32[]{:S(2)}) copy-start(bf16[3,32,1,512]{3,2,1,0:T(2,128)(2,1)} %get-tuple-element.166) | copy-start | bytes 294916
  364.1 47.4 %copy-start.37 = (f32[5,2,1]{0,1,2:T(2,128)S(1)}, f32[5,2,1]{0,1,2:T(2,128)}, u32[]{:S(2)}) copy-start(f32[5,2,1]{0,1,2:T(2,128)} %copy-done.36) | copy-start | bytes 124
  364.1 47.4 %copy-start.39 = (f32[5,2,1]{0,1,2:T(2,128)S(1)}, f32[5,2,1]{0,1,2:T(2,128)}, u32[]{:S(2)}) copy-start(f32[5,2,1]{0,1,2:T(2,128)} %copy-done.38) | copy-start | bytes 124
  364.1 47.4 %copy-start.41 = (f32[5,2,1]{0,1,2:T(2,128)S(1)}, f32[5,2,1]{0,1,2:T(2,128)}, u32[]{:S(2)}) copy-start(f32[5,2,1]{0,1,2:T(2,128)} %copy-done.40) | copy-start | bytes 124
  405.9 7.0 collective-permute-start.2
  407.9 6.7 collective-permute-start.3
  416.2 26.0 %copy-start = (bf16[4,2,2,2,32,2048]{5,4,3,2,1,0:T(8,128)(2,1)S(1)}, bf16[4,2,2,2,32,2048]{5,4,3,2,1,0:T(8,128)(2,1)}, u32[]{:S(2)}) copy-start(bf16[4,2,2,2,32,2048]{5,4,3,2,1,0:T(8,128)(2,1)} %get-tuple-element.32) | copy-start | bytes 12582916
  450.2 12.1 %copy-start.15 = (bf16[384,1024]{1,0:T(8,128)(2,1)S(1)}, bf16[384,1024]{1,0:T(8,128)(2,1)}, u32[]{:S(2)}) copy-start(bf16[384,1024]{1,0:T(8,128)(2,1)} %copy-done.14) | copy-start | bytes 2359300
  458.8 12.9 %all-to-all-start.1 = ((bf16[4,2,49152]{2,1,0:T(2,128)(2,1)}), bf16[4,2,49152]{2,1,0:T(2,128)(2,1)S(1)}, u32[]{:S(2)}, u32[]{:S(2)}) async-start(bf16[4,2,49152]{2,1,0:T(2,128)(2,1)} %reshape.196), calls=%async_computation.1 | async-start | bytes 1572864 | tf_op jit(solution)/shard_map/all_to_all | solution.py:905
  462.4 91.8 %reduce-scatter.2.cloned.1.call-start = ((), (), s32[]{:S(2)}) async-start(), calls=%async_computation.3 | async-start | bytes 3932160 | tf_op jit(solution)/shard_map/reduce_scatter | solution.py:909
  477.5 7.0 copy-start.9
  485.5 26.6 %copy-start.16 = (bf16[3,16,32,256]{3,2,1,0:T(8,128)(2,1)}, bf16[3,16,32,256]{3,2,1,0:T(8,128)(2,1)S(1)}, u32[]{:S(2)}) copy-start(bf16[3,16,32,256]{3,2,1,0:T(8,128)(2,1)S(1)} %fusion.40) | copy-start | bytes 2359300
  516.1 38.0 %copy-start.8 = (f32[3,16,32,256]{3,2,1,0:T(8,128)S(1)}, f32[3,16,32,256]{3,2,1,0:T(8,128)}, u32[]{:S(2)}) copy-start(f32[3,16,32,256]{3,2,1,0:T(8,128)} %get-tuple-element.40) | copy-start | bytes 4718596
  539.7 16.7 %copy-start.45 = (bf16[3,16,32,512]{3,2,1,0:T(8,128)(2,1)S(1)}, bf16[3,16,32,512]{3,2,1,0:T(8,128)(2,1)}, u32[]{:S(2)}) copy-start(bf16[3,16,32,512]{3,2,1,0:T(8,128)(2,1)} %get-tuple-element.38) | copy-start | bytes 4718596
  568.8 175.9 %copy-start.33 = (f32[16,2]{1,0:T(8,128)S(1)}, f32[16,2]{1,0:T(8,128)}, u32[]{:S(2)}) copy-start(f32[16,2]{1,0:T(8,128)} %copy.310) | copy-start | bytes 388
  568.8 175.9 %copy-start.34 = (f32[16,2]{1,0:T(8,128)S(1)}, f32[16,2]{1,0:T(8,128)}, u32[]{:S(2)}) copy-start(f32[16,2]{1,0:T(8,128)} %copy.308) | copy-start | bytes 388
  568.8 175.9 %copy-start.35 = (f32[16,2]{1,0:T(8,128)S(1)}, f32[16,2]{1,0:T(8,128)}, u32[]{:S(2)}) copy-start(f32[16,2]{1,0:T(8,128)} %copy.311) | copy-start | bytes 388
  568.8 179.8 %copy-start.2 = (f32[288,1024]{1,0:T(8,128)S(1)}, f32[288,1024]{1,0:T(8,128)}, u32[]{:S(2)}) copy-start(f32[288,1024]{1,0:T(8,128)} %param.28) | copy-start | bytes 3538948
  568.8 179.8 %copy-start.10 = (f32[288,1024]{1,0:T(8,128)S(1)}, f32[288,1024]{1,0:T(8,128)}, u32[]{:S(2)}) copy-start(f32[288,1024]{1,0:T(8,128)} %param.30) | copy-start | bytes 3538948
  568.8 179.8 %copy-start.11 = (f32[288,1024]{1,0:T(8,128)S(1)}, f32[288,1024]{1,0:T(8,128)}, u32[]{:S(2)}) copy-start(f32[288,1024]{1,0:T(8,128)} %param.29) | copy-start | bytes 3538948
  (25 other events, 69.3 us)
Sparse Core Ops, SparseCore 0:
  515.1 38.9 reduce-scatter.1

commit v2 on v1

--- a/solution.py
+++ b/solution.py
@@ -601,27 +601,37 @@
     )(part)
 
 
-def add_into(total, term, count, pick):
-    def step(i, carry):
-        at_total, at_term = pick(i)
-        value = total[at_total].astype(FLOAT) + term[at_term].astype(FLOAT)
-        total[at_total] = value.astype(HALF)
-        return carry
-
-    lax.fori_loop(0, count, step, 0)
+def gelu_slope(value):
+    square = value * value
+    bend = jnp.tanh(0.7978845608028654 * value * (1.0 + 0.044715 * square))
+    rise = 0.7978845608028654 * (1.0 + 3.0 * 0.044715 * square)
+    return 0.5 * (1.0 + bend) + 0.5 * value * (1.0 - bend * bend) * rise
+
+
+def across(source, window):
+    return lax.dot_general(source, window, (((0,), (0,)), ((), ())), preferred_element_type=FLOAT)
+
+
+def against(window, weight):
+    return lax.dot_general(window, weight, (((1,), (1,)), ((), ())), preferred_element_type=FLOAT)
+
+
+def add_rows(total, start, term, rows):
+    where = pl.ds(pl.multiple_of(start, 16), rows)
+    total[where] = (total[where].astype(FLOAT) + term.astype(FLOAT)).astype(HALF)
 
 
 def back_kernel(
-    d3, du, d2, d1, dh,
+    gs_in, w3_in, wu_in, w2_in, joined_in, h2_in, h1_in, x0_in, pre1_in, pre2_in, dh,
     g3, gu, g2, g1, gh,
-    l3, c3, y3, x3, z3, lu, cu, yu, xu, zu, m2, a2, b2, t2, m1, a1, b1, t1, hh,
-    send, here, r_3, r_u, r_2, r_1, r_h,
+    gs3, joined, slot, acc, flat, wu, h2, gh2, from_wa, pre, gs2, d_core, d_y,
+    du_c, du_y, du_x, du_z, d3, d3_c, d3_y, d3_x, d3_z, d2, d2_x, d2_z, d1_x, d1_z, hh,
+    send, here, r_wa, r_d, r_u, r_3, r_2, r_1, r_h, free,
 ):
     z, x, y, c = place()
     ha, wa = (2 * z + x, 2 * y + c)
     x_peer, y_peer, c_peer = (spot(z, 1 - x, y, c), spot(z, x, 1 - y, c), spot(z, x, y, 1 - c))
     mine = ha * 4 + wa
-    greet_all()
     sends = []
     stays = []
 
@@ -637,88 +647,24 @@
         stays.append([copy, False])
         return stays[-1]
 
-    def settle(entry):
-        entry[0].wait()
-        entry[1] = True
-
-    def all_core(grad, own, core, recv):
-        return (stay(grad.at[:, :, :, c], own), go(grad.at[:, :, :, 1 - c], core, recv.at[0], c_peer))
-
-    def all_y(own, core, along_y, recv, got):
-        settle(got[0])
-        got[1].wait_recv()
-        add_into(own, core, 8, lambda i: ((i // 2, i % 2, 1 - y),) * 2)
-        copy = go(own.at[:, :, 1 - y], along_y, recv.at[1], y_peer)
-        add_into(own, core, 8, lambda i: ((i // 2, i % 2, y),) * 2)
-        return copy
-
-    def all_x(own, along_y, along_x, recv, got):
-        got.wait_recv()
-        add_into(own, along_y, 4, lambda i: ((i, 1 - x, y), (i, 1 - x)))
-        copy = go(own.at[:, 1 - x, y], along_x, recv.at[2], x_peer)
-        add_into(own, along_y, 4, lambda i: ((i, x, y), (i, x)))
-        return copy
-
-    def all_z(own, along_x, along_z, recv, got):
-        got.wait_recv()
-        add_into(own, along_x, 4, lambda i: ((i, x, y), (i,)))
-        return [
-            go(
-                own.at[lax.rem(z + d, 4), x, y],
-                along_z.at[d - 1],
-                recv.at[2 + d],
-                spot(lax.rem(z + d, 4), x, y, c),
-            )
-            for d in range(1, 4)
-        ]
-
-    def all_end(own, along_z, out, got):
-        total = own[z, x, y].astype(FLOAT)
-        for d in range(3):
-            got[d].wait_recv()
-            total = total + along_z[d].astype(FLOAT)
-        out[...] = total
-
-    def quarter_x(grad, own, along_x, recv):
-        return (stay(grad.at[:, x], own), go(grad.at[:, 1 - x], along_x, recv.at[0], x_peer))
-
-    def quarter_z(own, along_x, along_z, recv, got):
-        settle(got[0])
-        got[1].wait_recv()
-        add_into(own, along_x, 16, lambda i: ((i // 4, i % 4),) * 2)
-        return [
-            go(
-                own.at[lax.rem(z + d, 4)],
-                along_z.at[d - 1],
-                recv.at[d],
-                spot(lax.rem(z + d, 4), x, y, c),
-            )
-            for d in range(1, 4)
-        ]
-
-    def quarter_w(own, along_z, total, out, recv, got):
-        for copy in got:
-            copy.wait_recv()
-
-        def step(w, carry):
-            value = own[z, w].astype(FLOAT)
-            for d in range(3):
-                value = value + along_z[d, w].astype(FLOAT)
-            total[w] = value.astype(HALF)
-            return carry
-
-        lax.fori_loop(0, 4, step, 0)
-        target = out.at[:, pl.ds(pl.multiple_of(wa * 256, 256), 256)]
-        stay(total.at[wa], target)
-        return [
-            go(total.at[lax.rem(wa + d, 4)], target, recv.at[3 + d], (ha, lax.rem(wa + d, 4)))
-            for d in range(1, 4)
-        ]
-
-    s3 = all_core(d3, l3, c3, r_3)
-    su = all_core(du, lu, cu, r_u)
-    s2 = quarter_x(d2, m2, a2, r_2)
-    s1 = quarter_x(d1, m1, a1, r_1)
+    def settle(*entries):
+        for entry in entries:
+            entry[0].wait()
+            entry[1] = True
+
+    got_gs = stay(gs_in, gs3)
+    got_w3 = [
+        stay(
+            w3_in.at[pl.ds(1024 * t, 512), pl.ds(256 * half, 256)],
+            slot.at[pl.ds(4608 * half + 512 * t, 512)],
+        )
+        for half in range(2)
+        for t in range(9)
+    ]
+    got_wu = stay(wu_in, wu)
+    got_h2 = stay(h2_in.at[pl.ds(0, 384)], h2)
+    got_joined = stay(joined_in, joined)
+    greet_all()
     own_head = stay(dh.at[mine], hh.at[0])
     heads = []
     for step in range(1, 32):
@@ -726,24 +672,324 @@
         heads.append(
             go(dh.at[other], hh.at[step], r_h.at[step - 1], (other // 4, lax.rem(other, 4)))
         )
-    s3 = all_y(l3, c3, y3, r_3, s3)
-    su = all_y(lu, cu, yu, r_u, su)
-    s2 = quarter_z(m2, a2, b2, r_2, s2)
-    s3 = all_x(l3, y3, x3, r_3, s3)
-    su = all_x(lu, yu, xu, r_u, su)
-    s1 = quarter_z(m1, a1, b1, r_1, s1)
-    s3 = all_z(l3, x3, z3, r_3, s3)
-    su = all_z(lu, xu, zu, r_u, su)
-    s2 = quarter_w(m2, b2, t2, g2, r_2, s2)
-    s1 = quarter_w(m1, b1, t1, g1, r_1, s1)
+
+    order = lax.broadcasted_iota(jnp.int32, (256, 256), 0)
+    inner = order % 128
+    pick = (inner // 8) * 16 + (inner % 8) * 2 + order // 128
+    apart = jnp.where(lax.broadcasted_iota(jnp.int32, (256, 256), 1) == pick, 1.0, 0.0).astype(HALF)
+    settle(got_gs, *got_w3)
+
+    def three_source(s, carry):
+        acc[...] = jnp.zeros_like(acc)
+
+        def tap(t, inner_carry):
+            window = gs3[2 - t % 3, s, pl.ds(2 - t // 3, 32)].reshape(512, 512)
+            for half in range(2):
+                rows = pl.ds(pl.multiple_of(4608 * half + 512 * t, 512), 512)
+                acc[...] += against(window[:, 256 * half : 256 * half + 256], slot[rows])
+            return inner_carry
+
+        lax.fori_loop(0, 9, tap, 0)
+        fine = acc[...].astype(HALF).reshape(16, 2, 16, 512)
+        for a in range(2):
+            parted = jnp.dot(
+                apart, fine[:, a].reshape(256, 512), preferred_element_type=FLOAT
+            ).astype(HALF)
+            for b in range(2):
+                rows = pl.ds(pl.multiple_of(128 * s, 128), 128)
+                flat[rows, pl.ds(512 * (2 * a + b), 512)] = parted[128 * b : 128 * b + 128]
+        return carry
+
+    lax.fori_loop(0, 3, three_source, 0)
+    got_w2 = stay(w2_in, slot)
+    settle(got_wu, got_h2)
+    for part in range(4):
+        lanes = slice(256 * part, 256 * part + 256)
+        gh2[:, lanes] = against(flat[...], wu[lanes, :]).astype(HALF)
+
+    def wa_lanes(col):
+        return gh2.at[:, pl.ds(pl.multiple_of(col * 256, 256), 256)]
+
+    own_wa = stay(wa_lanes(wa), from_wa.at[wa])
+    got_wa = [
+        go(
+            wa_lanes(lax.rem(wa + d, 4)),
+            from_wa.at[wa],
+            r_wa.at[d - 1],
+            (ha, lax.rem(wa + d, 4)),
+        )
+        for d in range(1, 4)
+    ]
+    for part in range(4):
+        lanes = slice(512 * part, 512 * part + 512)
+        wu[:, lanes] = across(h2[...], flat[:, lanes]).astype(HALF)
+
+    def block(grad, rows, bz, bx, by, bc):
+        number = ((bz * 2 + bx) * 2 + by) * 2 + bc
+        return grad.at[pl.ds(pl.multiple_of(number * rows, 16), rows)]
+
+    def all_core(grad, rows, core, recv, some):
+        return [
+            go(
+                block(grad, rows, bz, bx, by, 1 - c),
+                core.at[((bz - some[0]) * 2 + bx) * 2 + by],
+                recv.at[((bz - some[0]) * 2 + bx) * 2 + by],
+                c_peer,
+            )
+            for bz in some
+            for bx in range(2)
+            for by in range(2)
+        ]
+
+    def all_y(grad, rows, core, along_y, recv, some, got):
+        for copy in got:
+            copy.wait_recv()
+
+        def step(by):
+            def add(i, carry):
+                number = (((some[0] * 2 + i) * 2) + by) * 2 + c
+                add_rows(grad, number * rows, core[i * 2 + by], rows)
+                return carry
+
+            lax.fori_loop(0, 2 * len(some), add, 0)
+
+        step(1 - y)
+        copies = [
+            go(
+                block(grad, rows, bz, bx, 1 - y, c),
+                along_y.at[bz * 2 + bx],
+                recv.at[16 + bz * 2 + bx],
+                y_peer,
+            )
+            for bz in some
+            for bx in range(2)
+        ]
+        step(y)
+        return copies
+
+    def all_x(grad, rows, along_y, along_x, recv, got):
+        for copy in got:
+            copy.wait_recv()
+
+        def step(bx):
+            def add(bz, carry):
+                number = ((bz * 2 + bx) * 2 + y) * 2 + c
+                add_rows(grad, number * rows, along_y[bz * 2 + bx], rows)
+                return carry
+
+            lax.fori_loop(0, 4, add, 0)
+
+        step(1 - x)
+        copies = [
+            go(block(grad, rows, bz, 1 - x, y, c), along_x.at[bz], recv.at[24 + bz], x_peer)
+            for bz in range(4)
+        ]
+        step(x)
+        return copies
+
+    def all_z(grad, rows, along_x, along_z, recv, got):
+        for copy in got:
+            copy.wait_recv()
+
+        def add(bz, carry):
+            number = ((bz * 2 + x) * 2 + y) * 2 + c
+            add_rows(grad, number * rows, along_x[bz], rows)
+            return carry
+
+        lax.fori_loop(0, 4, add, 0)
+        return [
+            go(
+                block(grad, rows, lax.rem(z + d, 4), x, y, c),
+                along_z.at[d - 1],
+                recv.at[27 + d],
+                spot(lax.rem(z + d, 4), x, y, c),
+            )
+            for d in range(1, 4)
+        ]
+
+    def all_end(grad, rows, along_z, out, got):
+        total = grad[pl.ds(pl.multiple_of(mine * rows, 16), rows)].astype(FLOAT)
+        for d in range(3):
+            got[d].wait_recv()
+            total = total + along_z[d].astype(FLOAT)
+        out[...] = total
+
+    def quarter_x(grad, rows, along_x, recv, bz):
+        source = grad.at[pl.ds(pl.multiple_of((bz * 2 + 1 - x) * 4 * rows, 16), 4 * rows)]
+        return go(source, along_x.at[bz], recv.at[bz], x_peer)
+
+    def quarter_z(grad, rows, along_x, along_z, recv, got):
+        for copy in got:
+            copy.wait_recv()
+
+        def add(d, carry):
+            bz = lax.rem(z + d, 4)
+            add_rows(grad, (bz * 2 + x) * 4 * rows, along_x[bz], 4 * rows)
+            return carry
+
+        lax.fori_loop(0, 4, add, 0)
+        return [
+            go(
+                grad.at[
+                    pl.ds(pl.multiple_of((lax.rem(z + d, 4) * 2 + x) * 4 * rows, 16), 4 * rows)
+                ],
+                along_z.at[d - 1],
+                recv.at[3 + d],
+                spot(lax.rem(z + d, 4), x, y, c),
+            )
+            for d in range(1, 4)
+        ]
+
+    def quarter_w(grad, rows, along_z, out, recv, got):
+        for copy in got:
+            copy.wait_recv()
+
+        own = pl.ds(pl.multiple_of(ha * 4 * rows, 16), 4 * rows)
+        value = grad[own].astype(FLOAT)
+        for d in range(3):
+            value = value + along_z[d].astype(FLOAT)
+        grad[own] = value.astype(HALF)
+        target = out.at[:, pl.ds(pl.multiple_of(wa * 256, 256), 256)]
+
+        def piece(col):
+            return grad.at[pl.ds(pl.multiple_of((ha * 4 + col) * rows, 16), rows)]
+
+        stay(piece(wa), target)
+        return [
+            go(
+                piece(lax.rem(wa + d, 4)),
+                target,
+                recv.at[6 + d],
+                (ha, lax.rem(wa + d, 4)),
+            )
+            for d in range(1, 4)
+        ]
+
+    su = all_core(wu, 32, du_c, r_u, (0, 1, 2, 3))
+    settle(got_joined)
+
+    def three_weight(t, carry):
+        window = gs3[2 - t % 3, :, pl.ds(2 - t // 3, 32)].reshape(1536, 512)
+        rows = pl.ds(pl.multiple_of(1024 * t, 1024), 1024)
+        d3[rows] = across(joined[...], window).astype(HALF)
+        return carry
+
+    lax.fori_loop(0, 5, three_weight, 0)
+    s3 = all_core(d3, 288, d3_c, r_3, (0, 1))
+    su = all_y(wu, 32, du_c, du_y, r_u, (0, 1, 2, 3), su)
+    s3_low = all_y(d3, 288, d3_c, d3_y, r_3, (0, 1), s3)
+    pl.semaphore_signal(free, inc=1, device_id=c_peer, device_id_type=MESH)
+    lax.fori_loop(5, 9, three_weight, 0)
+    pl.semaphore_wait(free, 1)
+    s3 = all_core(d3, 288, d3_c, r_3, (2, 3))
+    got_h1 = stay(h1_in, joined)
+
+    settle(own_wa)
+    for copy in got_wa:
+        copy.wait_recv()
+
+    def put_columns(target, s, value):
+        column = lax.broadcasted_iota(jnp.int32, (16, 32, 256), 1)
+        target[0, s, pl.ds(1, 16)] = jnp.where(column > 0, pltpu.roll(value, 1, 1), 0.0).astype(HALF)
+        target[1, s, pl.ds(1, 16)] = value.astype(HALF)
+        target[2, s, pl.ds(1, 16)] = jnp.where(column < 31, pltpu.roll(value, 31, 1), 0.0).astype(
+            HALF
+        )
+
+    for e in range(3):
+        gs2[e, :, 0] = jnp.zeros((3, 32, 256), HALF)
+        gs2[e, :, 17] = jnp.zeros((3, 32, 256), HALF)
+    settle(stay(pre2_in, pre))
+
+    def two_grad(s, carry):
+        rows = pl.ds(pl.multiple_of(128 * s, 128), 128)
+        parts = [from_wa[w, rows].astype(FLOAT).reshape(16, 8, 256) for w in range(4)]
+        put_columns(gs2, s, jnp.concatenate(parts, axis=1) * gelu_slope(pre[s]))
+        return carry
+
+    lax.fori_loop(0, 3, two_grad, 0)
+    got_pre1 = stay(pre1_in, pre)
+    settle(got_h1)
+
+    def two_weight(t, carry):
+        window = gs2[2 - t % 3, :, pl.ds(2 - t // 3, 16)].reshape(1536, 256)
+        rows = pl.ds(pl.multiple_of(1024 * t, 1024), 1024)
+        d2[rows] = across(joined[...], window).astype(HALF)
+        return carry
+
+    s2 = []
+    for bz, (first, last) in enumerate(((0, 3), (3, 5), (5, 7), (7, 9))):
+        lax.fori_loop(first, last, two_weight, 0)
+        s2.append(quarter_x(d2, 288, d2_x, r_2, bz))
+
+    s3_high = all_y(d3, 288, d3_c, d3_y, r_3, (2, 3), s3)
+    got_x0 = stay(x0_in, joined.at[:, pl.ds(0, 512)])
+    settle(got_w2)
+
+    def source_two(s):
+        for half in range(2):
+            acc[...] = jnp.zeros_like(acc)
+
+            def tap(t, inner_carry):
+                window = gs2[2 - t % 3, s, pl.ds(2 - t // 3, 16)].reshape(512, 256)
+                rows = pl.ds(pl.multiple_of(1024 * t + 512 * half, 512), 512)
+                acc[...] += against(window, slot[rows])
+                return inner_carry
+
+            lax.fori_loop(0, 9, tap, 0)
+            gs3[half, s, pl.ds(0, 32)] = acc[...].astype(HALF).reshape(32, 16, 512)
+
+    def d_lanes(halves, s, core):
+        return gs3.at[halves, s, pl.ds(0, 32), :, pl.ds(pl.multiple_of(256 * core, 256), 256)]
+
+    sd = []
+    for s in range(3):
+        source_two(s)
+        sd.append(go(d_lanes(pl.ds(0, 2), s, 1 - c), d_core.at[s], r_d.at[s], c_peer))
+        if s == 0:
+            su = all_x(wu, 32, du_y, du_x, r_u, su)
+    sy = []
+    own_lanes = pl.ds(pl.multiple_of(256 * c, 256), 256)
+    for s in range(3):
+        sd[s].wait_recv()
+        for half in range(2):
+            value = gs3[half, s, pl.ds(0, 32), :, own_lanes].astype(FLOAT)
+            value = value + d_core[s, half].astype(FLOAT)
+            gs3[half, s, pl.ds(0, 32), :, own_lanes] = value.astype(HALF)
+        sy.append(go(d_lanes(1 - y, s, c), d_y.at[s], r_d.at[3 + s], y_peer))
+    s2 = quarter_z(d2, 288, d2_x, d2_z, r_2, s2)
+    settle(got_pre1)
+    for s in range(3):
+        sy[s].wait_recv()
+        value = gs3[y, s, pl.ds(0, 32), :, own_lanes].astype(FLOAT) + d_y[s].astype(FLOAT)
+        put_columns(gs2, s, value.reshape(16, 32, 256) * gelu_slope(pre[s]))
+    settle(got_x0)
+
+    def one_weight(t, carry):
+        window = gs2[2 - t % 3, :, pl.ds(2 - t // 3, 16)].reshape(1536, 256)
+        rows = pl.ds(pl.multiple_of(512 * t, 512), 512)
+        slot[rows] = across(joined[:, 0:512], window).astype(HALF)
+        return carry
+
+    s1 = []
+    for bz, (first, last) in enumerate(((0, 3), (3, 5), (5, 7), (7, 9))):
+        lax.fori_loop(first, last, one_weight, 0)
+        s1.append(quarter_x(slot, 144, d1_x, r_1, bz))
+
+    s3 = all_x(d3, 288, d3_y, d3_x, r_3, s3_low + s3_high)
+    su = all_z(wu, 32, du_x, du_z, r_u, su)
+    s2 = quarter_w(d2, 288, d2_z, g2, r_2, s2)
+    s1 = quarter_z(slot, 144, d1_x, d1_z, r_1, s1)
+    s3 = all_z(d3, 288, d3_x, d3_z, r_3, s3)
     settle(own_head)
     total = hh[0]
     for step in range(1, 32):
         heads[step - 1].wait_recv()
         total = total + hh[step]
     gh[...] = total
-    all_end(l3, z3, g3, s3)
-    all_end(lu, zu, gu, su)
+    all_end(wu, 32, du_z, gu, su)
+    s1 = quarter_w(slot, 144, d1_z, g1, r_1, s1)
+    all_end(d3, 288, d3_z, g3, s3)
     for copy in s2 + s1:
         copy.wait_recv()
     for entry in stays:
@@ -753,28 +999,14 @@
         copy.wait_send()
 
 
-def back(d3, du, d2, d1, dh):
+def back(gs, w3, wu, w2, joined, h2, h1, x0, pre1, pre2, dh):
     anywhere = pl.BlockSpec(memory_space=pl.ANY)
     inside = pl.BlockSpec(memory_space=pltpu.VMEM)
     shape = jax.ShapeDtypeStruct
     dma = pltpu.SemaphoreType.DMA
 
-    def whole(rows, cols):
-        return [
-            pltpu.VMEM((4, 2, 2, rows, cols), HALF),
-            pltpu.VMEM((4, 2, 2, rows, cols), HALF),
-            pltpu.VMEM((4, 2, rows, cols), HALF),
-            pltpu.VMEM((4, rows, cols), HALF),
-            pltpu.VMEM((3, rows, cols), HALF),
-        ]
-
-    def quarter(rows):
-        return [
-            pltpu.VMEM((4, 4, rows, 256), HALF),
-            pltpu.VMEM((4, 4, rows, 256), HALF),
-            pltpu.VMEM((3, 4, rows, 256), HALF),
-            pltpu.VMEM((4, rows, 256), HALF),
-        ]
+    def room(*dims):
+        return pltpu.VMEM(dims, HALF)
 
     return pl.pallas_call(
         back_kernel,
@@ -786,26 +1018,52 @@
             shape((144, 1024), HALF),
             shape((16, 128), FLOAT),
         ),
-        in_specs=[anywhere] * 5,
-        out_specs=[inside] * 5,
-        scratch_shapes=whole(288, 512)
-        + whole(32, 2048)
-        + quarter(288)
-        + quarter(144)
-        + [
+        in_specs=[anywhere] * 11,
+        out_specs=[inside, inside, anywhere, anywhere, inside],
+        scratch_shapes=[
+            room(3, 3, 34, 16, 512),
+            room(1536, 1024),
+            room(9216, 256),
+            pltpu.VMEM((512, 512), FLOAT),
+            room(384, 2048),
+            room(1024, 2048),
+            room(384, 1024),
+            room(384, 1024),
+            room(4, 384, 256),
+            pltpu.VMEM((3, 16, 32, 256), FLOAT),
+            room(3, 3, 18, 32, 256),
+            room(3, 2, 32, 16, 256),
+            room(3, 32, 16, 256),
+            room(16, 32, 2048),
+            room(8, 32, 2048),
+            room(4, 32, 2048),
+            room(3, 32, 2048),
+            room(9216, 512),
+            room(8, 288, 512),
+            room(8, 288, 512),
+            room(4, 288, 512),
+            room(3, 288, 512),
+            room(9216, 256),
+            room(4, 1152, 256),
+            room(3, 1152, 256),
+            room(4, 576, 256),
+            room(3, 576, 256),
             pltpu.VMEM((32, 16, 128), FLOAT),
-            dma((64,)),
-            dma((8,)),
+            dma((144,)),
+            dma((40,)),
+            dma((3,)),
             dma((6,)),
-            dma((6,)),
-            dma((7,)),
-            dma((7,)),
             dma((31,)),
+            dma((31,)),
+            dma((10,)),
+            dma((10,)),
+            dma((31,)),
+            pltpu.SemaphoreType.REGULAR,
         ],
         compiler_params=pltpu.CompilerParams(
-            collective_id=2, has_side_effects=True, vmem_limit_bytes=60 * 1024 * 1024
+            collective_id=2, has_side_effects=True, vmem_limit_bytes=64 * 1024 * 1024
         ),
-    )(d3, du, d2, d1, dh)
+    )(gs, w3, wu, w2, joined, h2, h1, x0, pre1, pre2, dh)
 
 
 def conv_with(source, weight, col_rim):
@@ -816,29 +1074,6 @@
         (1, 1),
         ((1, 1), (col_rim, col_rim)),
         dimension_numbers=("NHWC", "HWIO", "NHWC"),
-        preferred_element_type=FLOAT,
-    )
-
-
-def conv_weight_grad(source, grad, col_rim):
-    return lax.conv_general_dilated(
-        source,
-        grad,
-        (1, 1),
-        ((1, 1), (col_rim, col_rim)),
-        dimension_numbers=("CHWN", "IHWO", "HWNC"),
-        preferred_element_type=FLOAT,
-    ).reshape(9 * source.shape[3], grad.shape[3])
-
-
-def conv_source_grad(grad, weight, chan, col_rim):
-    kernel = weight.reshape(3, 3, -1, weight.shape[1])[::-1, ::-1, :chan]
-    return lax.conv_general_dilated(
-        grad,
-        kernel,
-        (1, 1),
-        ((1, 1), (col_rim, col_rim)),
-        dimension_numbers=("NHWC", "HWOI", "NHWC"),
         preferred_element_type=FLOAT,
     )
 
@@ -899,21 +1134,19 @@
     grad_hidden = jnp.einsum("shwk,ck->shwc", grad_logits, wh, preferred_element_type=FLOAT)
     grad_three = smooth_back(pre_three, grad_hidden).astype(HALF)
     grad_wide = with_cols(grad_three)
-    d3 = conv_weight_grad(joined, grad_three, 0).astype(HALF)
-    grad_ups = conv_source_grad(grad_wide, w3, 512, 0).astype(HALF)
-    du, grad_hidden_two = upsample_back(hidden_two, grad_ups, wu)
-    grad_hidden_two = lax.all_to_all(grad_hidden_two.astype(HALF), "wa", 3, 2, tiled=True)
-    grad_two = smooth_back(pre_two, grad_hidden_two.astype(FLOAT)).astype(HALF)
-    d2 = conv_weight_grad(h1, grad_two, 1).astype(HALF)
-    grad_hidden_one = conv_source_grad(grad_two, w2, 1024, 1).astype(HALF)
-    grad_hidden_one = lax.psum_scatter(grad_hidden_one, "wa", scatter_dimension=3, tiled=True)
-    grad_one = smooth_back(pre_one, grad_hidden_one.astype(FLOAT)).astype(HALF)
-    d1 = conv_weight_grad(x0, grad_one, 1).astype(HALF)
+    grad_rows = jnp.pad(grad_wide, ((0, 0), (1, 1), (0, 0), (0, 0)))
+    shifts = jnp.stack([grad_rows[:, :, e : e + 16] for e in range(3)])
     g3, gu, g2, g1, gh = back(
-        d3.reshape(4, 2, 2, 2, 288, 512),
-        du.astype(HALF).reshape(4, 2, 2, 2, 32, 2048),
-        d2.reshape(4, 2, 4, 288, 256),
-        d1.reshape(4, 2, 4, 144, 256),
+        shifts,
+        w3,
+        wu,
+        w2,
+        joined[:, :, 1:17].reshape(1536, 1024),
+        h2,
+        h1.reshape(1536, 1024),
+        x0.reshape(1536, 512),
+        pre_one,
+        pre_two,
         jnp.pad(head_grad, ((0, 0), (0, 126))).reshape(32, 16, 128),
     )
     return (loss_value, g1.astype(FLOAT), g2.astype(FLOAT), gu, g3, gh[:, :2])

time: 778 us -> 617 us (0.79)
  matrix products: 198 us -> 64.4 us
  Pallas kernels: 402 us -> 447 us
  local copies, waits for them, and re-layouts: 76.7 us -> 48.7 us
  waiting for transfers between devices: 21.3 us -> 0.01 us
  between operations: 16.7 us -> 3.39 us
    conv_general_dilated x5 -> x0, matrix products: 129 us -> none  [the longest x3 77 us: conv_weight_grad(): lax.conv_general_dilated(source, grad, (1, 1), ((1, 1), (col_rim, col_rim...]
    pallas_call x1, Pallas kernels: 176 us -> 221 us  [back(): pl.pallas_call(back_kernel, name='back', out_shape=(shape((288, 512), FLO...]
    unnamed x112 -> x68, local copies, waits for them, and re-layouts: 21.9 us -> 7.03 us
    reduce_scatter x1 -> x0, waiting for transfers between devices: 14.4 us -> none  [sliced_grads(): lax.psum_scatter(grad_hidden_one, 'wa', scatter_dimension=3, tiled=True)]
    convert_element_type x2 -> x0, local copies, waits for them, and re-layouts: 13 us -> none  [the longest x1 6.94 us: sliced_grads(): grad_two = smooth_back(pre_two, grad_hidden_two.astype(FLOAT)).astype(HALF)]
  transfers between devices with their start and end apart: 7 -> 5, of which waited for: 4 -> 0; matrix products, arithmetic and copies ran while one was open for 9% -> 8% of each run, Pallas kernels for 0% -> 0%
where the time goes in v2:
time: 617 us; the launch traced here: 608 us
  Pallas kernels  447 us (72%)
  matrix products  64.4 us (10%)
  local copies, waits for them, and re-layouts  48.7 us (8%)
  other arithmetic  27.5 us (4%)
  starting transfers between devices  16.8 us (3%)
    pallas_call x1, Pallas kernels, back(): pl.pallas_call(back_kernel, name='back', out_shape=(shape((288, 512), FLO...  221 us
    pallas_call x1, Pallas kernels, front(): pl.pallas_call(functools.partial(front_kernel, compute), name='front', ou...  216 us
    conv_general_dilated x1, matrix products, conv_with(): lax.conv_general_dilated(source, weight.reshape(3, 3, chan, weight.shape[...  44.7 us
  transfers between devices with their start and end apart: 5, of which 0 were waited for; matrix products, arithmetic and copies ran while one was open for 8% of the time, Pallas kernels for 0%

profile of v2, /device:TPU:14, one launch (start us, length us, event | category | flops | bytes accessed | tf_op | source)
XLA Modules:
  0.0 608.2 jit_solution(13967617090356617600)
XLA Ops:
  0.7 2.2 convert_element_type.67.w2
  2.9 1.8 convert_element_type.66.w1
  4.7 1.8 convert_element_type.69.w3
  7.9 215.7 %front.1 = (bf16[3,16,32,512]{3,2,1,0:T(8,128)(2,1)}, bf16[3,16,32,1024]{3,2,1,0:T(8,128)(2,1)}, bf16[480,1024]{1,0:T(8,128)(2,1)}, bf16[8,192,512]{2,1,0:T(8,12...) custom-call(bf16[8,48,512]{2,1,0:T(8,128)(2,1)} %bitcast.120, ...), custom_call_target="tpu_custom_call" | custom-call | tf_op jit(solution)/shard_map/front/pallas_call | solution.py:515
  223.6 2.9 copy.200
  226.6 2.3 collective-permute-start
  228.9 3.3 collective-permute-start.1
  233.0 5.7 all-to-all-start
  238.7 7.8 %reshape_reshape.6 = bf16[1024,2,2,512]{3,2,1,0:T(2,128)(2,1)} reshape(bf16[4,2,2,2,32,2048]{5,4,3,2,1,0:T(8,128)(2,1)} %get-tuple-element.32) | data formatting | bytes 8388608 | tf_op jit(solution)/shard_map/reshape;reshape | solution.py:1109
  246.5 8.8 %fusion.84 = (bf16[1024,2,1,512]{3,2,1,0:T(2,128)(2,1)S(1)}, bf16[1024,2,1,512]{3,2,1,0:T(2,128)(2,1)S(1)}) fusion(bf16[1024,2,2,512]{3,2,1,0:T(2,128)(2,1)} %reshape_reshape.6), kind=kLoop, calls=%fused_computation.130 | loop fusion | bytes 8388608 | tf_op jit(solution)/shard_map/slice | solution.py:1114
  255.4 1.4 fusion.37
  257.5 6.6 %copy.237 = bf16[2048,1024]{1,0:T(8,128)(2,1)} copy(bf16[2048,1024]{0,1:T(8,128)(2,1)} %bitcast.103) | data formatting | bytes 8388608 | tf_op jit(solution)/shard_map/shwc,cq->shwq/dot_general | solution.py:86
  264.1 5.2 fusion.30
  271.4 4.2 copy.238
  279.6 44.7 %fusion.2 = f32[3,32,16,512]{3,0,2,1:T(4,128)S(1)} fusion(bf16[3,3,1024,512]{3,2,1,0:T(8,128)(2,1)} %bitcast.109, bf16[3,32,1,512]{3,0,2,1:T(4,128)(2,1)S(1)} %collective-permute-done.1, bf16[3,32,16,512]{3,0,2,1:T(4,128)(2,1)S(1)} %bitcast.107, bf16[3,32,1,512]{3,0,2,1:T(4,128)(2,1)S(1)} %collective-permute-done, bf16[3,32,1,512]{3,0,2,1:T(4,128)(2,1)S(1)} %copy.199, ...), kind=kOutput, calls=%fused_computation.5 | convolution fusion | flops 14214758400 | bytes 16121856 | tf_op jit(solution)/shard_map/conv_general_dilated | solution.py:1071
  324.3 2.0 copy-done.1
  326.3 2.8 multiply_convert_fusion
  329.1 3.4 fusion.88
  334.1 10.4 %sum_all.1 = f32[8,128]{1,0:T(8,128)} custom-call(f32[8,128]{1,0:T(8,128)} %pad.17.part), custom_call_target="tpu_custom_call" | custom-call | tf_op jit(solution)/shard_map/sum_all/pallas_call | solution.py:589
  346.3 5.2 fusion.33
  351.6 3.2 fusion.20
  355.9 2.0 collective-permute-start.2
  357.9 3.5 collective-permute-start.3
  361.5 2.0 maximum_maximum_fusion
  363.5 3.0 copy.220
  367.8 1.7 fusion.25
  369.5 1.2 slice_bitcast_fusion.2
  370.8 2.7 pad_maximum_fusion.gs_in
  373.5 221.3 %back.1 = (f32[288,512]{1,0:T(8,128)}, f32[32,2048]{1,0:T(8,128)}, bf16[288,1024]{1,0:T(8,128)(2,1)}, bf16[144,1024]{1,0:T(8,128)(2,1)}, f32[16,128]{1,0:T(8,128)}) custom-call(bf16[3,3,34,16,512]{4,3,2,1,0:T(8,128)(2,1)} %pad_maximum_fusion.gs_in, bf16[9216,512]{1,0:T(8,128)(2,1)} %bitcast.110, bf16[1024,2048]{1,0:T(8,128)(2,1)} %bitcast.104, ...), custom_call_target="tpu_custom_call" | custom-call | tf_op jit(solution)/shard_map/back/pallas_call | solution.py:1011
  597.5 4.7 add_multiply_fusion
  602.2 1.4 add_multiply_fusion.1
  604.3 1.4 add_multiply_fusion.2
  (113 shorter events, 18.4 us)
Async XLA Ops:
  0.6 5.9 copy-start.8
  0.7 6.5 %copy-start.23 = (f32[16,2]{0,1:T(2,128)S(1)}, f32[16,2]{0,1:T(2,128)}, u32[]{:S(2)}) copy-start(f32[16,2]{0,1:T(2,128)} %param.37) | copy-start | bytes 388
  7.9 224.3 %copy-start.21 = (s32[24,4,16]{0,2,1:T(8,128)S(1)}, s32[24,4,16]{0,2,1:T(8,128)}, u32[]{:S(2)}) copy-start(s32[24,4,16]{0,2,1:T(8,128)} %param.23) | copy-start | bytes 18436
  7.9 224.3 %copy-start.22 = (s32[24,4,16]{0,2,1:T(8,128)S(1)}, s32[24,4,16]{0,2,1:T(8,128)}, u32[]{:S(2)}) copy-start(s32[24,4,16]{0,2,1:T(8,128)} %param.24) | copy-start | bytes 18436
  226.6 53.0 %collective-permute-start = (bf16[3,32,1,512]{3,0,2,1:T(4,128)(2,1)S(1)}, bf16[3,32,1,512]{3,0,2,1:T(4,128)(2,1)S(1)}, u32[]{:S(2)}, u32[]{:S(2)}) collective-permute-start(bf16[3,32,1,512]{3,0,2,1:T(4,128)(2,1)S(1)} %get-tuple-element.150), channel_id=1, source_target_pairs={{0,1},{1,2},{2,3},{4,5},{5,6},{6,7},{8,9},{9,10},{10,11},{12,13},{... | collective-permute-start | bytes 294920 | tf_op jit(solution)/shard_map/ppermute | solution.py:26
  228.9 50.7 %collective-permute-start.1 = (bf16[3,32,1,512]{3,0,2,1:T(4,128)(2,1)S(1)}, bf16[3,32,1,512]{3,0,2,1:T(4,128)(2,1)S(1)}, u32[]{:S(2)}, u32[]{:S(2)}) collective-permute-start(bf16[3,32,1,512]{3,0,2,1:T(4,128)(2,1)S(1)} %get-tuple-element.151), channel_id=1, source_target_pairs={{1,0},{2,1},{3,2},{5,4},{6,5},{7,6},{9,8},{10,9},{11,10},{13,12},{... | collective-permute-start | bytes 294920 | tf_op jit(solution)/shard_map/ppermute | solution.py:29
  233.0 44.6 %all-to-all-start = ((s32[8,1,192]{2,1,0:T(1,128)}), s32[8,1,192]{2,1,0:T(1,128)S(1)}, u32[]{:S(2)}, u32[]{:S(2)}) async-start(s32[8,1,192]{2,1,0:T(1,128)} %reshape.174), calls=%async_computation | async-start | bytes 16384 | tf_op jit(solution)/shard_map/all_to_all | solution.py:1090
  246.5 8.8 %copy-start.3 = (bf16[480,1024]{1,0:T(8,128)(2,1)S(1)}, bf16[480,1024]{1,0:T(8,128)(2,1)}, u32[]{:S(2)}) copy-start(bf16[480,1024]{1,0:T(8,128)(2,1)} %get-tuple-element.31.h2_in) | copy-start | bytes 2949124
  264.1 5.2 copy-start.25
  269.3 7.0 %copy-start.24 = (f32[16,2]{0,1:T(2,128)S(1)}, f32[16,2]{0,1:T(2,128)}, u32[]{:S(2)}) copy-start(f32[16,2]{0,1:T(2,128)} %param.39) | copy-start | bytes 388
  269.3 7.7 %copy-start.27 = (s32[24]{0:T(128)S(1)}, s32[24]{0:T(128)}, u32[]{:S(2)}) copy-start(s32[24]{0:T(128)} %param.22) | copy-start | bytes 292
  324.3 2.0 copy-start.1
  326.3 2.8 copy-start.26
  326.3 6.2 %copy-start.15 = (s32[3,32,16]{2,1,0:T(8,128)S(1)}, s32[3,32,16]{2,1,0:T(8,128)}, u32[]{:S(2)}) copy-start(s32[3,32,16]{2,1,0:T(8,128)} %get-tuple-element.154) | copy-start | bytes 18436
  326.3 6.3 %copy-start.16 = (f32[3,32,16]{2,1,0:T(8,128)S(1)}, f32[3,32,16]{2,1,0:T(8,128)}, u32[]{:S(2)}) copy-start(f32[3,32,16]{2,1,0:T(8,128)} %get-tuple-element.155) | copy-start | bytes 18436
  326.3 6.8 %copy-start.28 = (s32[3]{0:T(128)S(1)}, s32[3]{0:T(128)}, u32[]{:S(2)}) copy-start(s32[3]{0:T(128)} %dynamic-slice) | copy-start | bytes 40
  346.3 5.3 copy-start.2
  351.6 9.9 %copy-start = (bf16[3,16,2,8,2,512]{5,0,4,3,2,1:T(4,128)(2,1)S(1)}, bf16[3,16,2,8,2,512]{5,0,4,3,2,1:T(4,128)(2,1)}, u32[]{:S(2)}) copy-start(bf16[3,16,2,8,2,512]{5,0,4,3,2,1:T(4,128)(2,1)} %copy.238) | copy-start | bytes 4718596
  354.8 3.1 copy-start.4
  355.9 11.9 %collective-permute-start.2 = (bf16[3,32,1,512]{3,2,1,0:T(2,128)(2,1)S(1)}, bf16[3,32,1,512]{3,2,1,0:T(2,128)(2,1)S(1)}, u32[]{:S(2)}, u32[]{:S(2)}) collective-permute-start(bf16[3,32,1,512]{3,2,1,0:T(2,128)(2,1)S(1)} %get-tuple-element.152), channel_id=1, source_target_pairs={{0,1},{1,2},{2,3},{4,5},{5,6},{6,7},{8,9},{9,10},{10,11},{12,13},{... | collective-permute-start | bytes 294920 | tf_op jit(solution)/shard_map/ppermute | solution.py:26
  357.9 9.9 %collective-permute-start.3 = (bf16[3,32,1,512]{3,2,1,0:T(2,128)(2,1)S(1)}, bf16[3,32,1,512]{3,2,1,0:T(2,128)(2,1)S(1)}, u32[]{:S(2)}, u32[]{:S(2)}) collective-permute-start(bf16[3,32,1,512]{3,2,1,0:T(2,128)(2,1)S(1)} %get-tuple-element.153), channel_id=1, source_target_pairs={{1,0},{2,1},{3,2},{5,4},{6,5},{7,6},{9,8},{10,9},{11,10},{13,12},{... | collective-permute-start | bytes 294920 | tf_op jit(solution)/shard_map/ppermute | solution.py:29
  363.5 4.3 copy-start.5
  597.5 4.7 copy-start.6
  597.5 4.7 copy-start.10
  597.5 4.7 copy-start.11
  597.5 4.7 copy-start.12
  602.1 1.9 copy-start.14
  602.1 2.1 copy-start.17
  602.2 3.5 copy-start.9
  602.2 3.4 copy-start.18
  602.2 3.4 copy-start.19
  602.2 3.4 copy-start.20
  (2 other events, 3.1 us)

commit v3 on v2

--- a/solution.py
+++ b/solution.py
@@ -275,12 +275,25 @@
     return parts[1].reshape(shape) + low + high
 
 
+def put_shifts(target, lanes, s, value, left, right):
+    column = lax.broadcasted_iota(jnp.int32, value.shape, 1)
+    last = value.shape[1] - 1
+    rows = pl.ds(1, value.shape[0])
+    low = jnp.where(column > 0, pltpu.roll(value, 1, 1), left)
+    target[0, s, rows, :, lanes] = low.astype(HALF)
+    target[1, s, rows, :, lanes] = value.astype(HALF)
+    high = jnp.where(column < last, pltpu.roll(value, last, 1), right)
+    target[2, s, rows, :, lanes] = high.astype(HALF)
+
+
 def front_kernel(
     compute,
-    bot, skip, w1, w2, wu, w3, wh,
-    x0_out, h1_out, h2_out, sk_out, w2_out, wu_out, w3_out, wh_out, pre1_out, pre2_out,
-    xr, x0, w1q, w2q, h1s, h1, parts, h2s,
+    bot, skip, code, w1, w2, wu, w3, wh,
+    x0_out, h1_out, h2_out, joined_out, w2_out, wu_out, w3_out, pre1_out, pre2_out, pre3_out,
+    hidden_out, logit_out, code_out, sums_out, head_out,
+    xr, x0, w1q, w2q, h1s, h1, parts, h2s, h2v, wuv, w3v, skv, rims, rims_got, tiles, whv,
     send, here, r_bot, r_grp, r_w1, r_w1x, r_w2, r_w2x, r_h1, r_h2, r_skip, r_wh, r_w3, r_wu,
+    r_code, r_rim, r_sum,
 ):
     z, x, y, c = place()
     ha, wa = (2 * z + x, 2 * y + c)
@@ -302,55 +315,48 @@
         stays.append([copy, False])
         return stays[-1]
 
-    def settle(entry):
-        entry[0].wait()
-        entry[1] = True
-
-    own_bot = stay(bot.at[ha], xr.at[ha, wa])
-    bots = [
-        go(bot.at[lax.rem(ha + d, 8)], xr.at[ha, wa], r_bot.at[d - 1], (lax.rem(ha + d, 8), wa))
-        for d in range(1, 8)
-    ]
-
-    def spread(shard, whole, rows, recv):
-        place_rows = whole.at[pl.ds(pl.multiple_of(mine * rows, rows), rows)]
-        own = stay(shard.at[:, pl.ds(pl.multiple_of(wa * 256, 256), 256)], place_rows)
-        copies = [[], [], [], []]
-        for dz in range(4):
-            for dw in range(4):
-                if dz == 0 and dw == 0:
-                    continue
-                to = lax.rem(wa + dw, 4)
-                copies[dz].append(
-                    go(
-                        shard.at[:, pl.ds(pl.multiple_of(to * 256, 256), 256)],
-                        place_rows,
-                        recv.at[dz, dw],
-                        (lax.rem(z + dz, 4) * 2 + x, to),
-                    )
-                )
+    def settle(*entries):
+        for entry in entries:
+            entry[0].wait()
+            entry[1] = True
+
+    def arrive(*copies):
+        for copy in copies:
+            copy.wait_recv()
+
+    def spread(shard, whole, rows, first, count, recv):
+        start = pl.multiple_of(mine * rows + first, 16)
+        place_rows = whole.at[pl.ds(start, count)]
+        source_rows = pl.ds(first, count)
+        lanes = [pl.ds(pl.multiple_of(lax.rem(wa + dw, 4) * 256, 256), 256) for dw in range(4)]
+        own = stay(shard.at[source_rows, lanes[0]], place_rows)
+        copies = [
+            go(
+                shard.at[source_rows, lanes[dw]],
+                place_rows,
+                recv.at[dz, dw],
+                (lax.rem(z + dz, 4) * 2 + x, lax.rem(wa + dw, 4)),
+            )
+            for dz in (1, 2, 3, 0)
+            for dw in range(4)
+            if dz + dw > 0
+        ]
         return (own, copies)
 
-    def pass_x(whole, rows, got, recv):
+    def pass_x(whole, rows, first, count, got, recv):
         own, copies = got
         settle(own)
+        arrive(*copies)
+        if count == rows:
+            spans = [(dz, 0, 4 * rows) for dz in range(4)]
+        else:
+            spans = [(dz, w * rows + first, count) for dz in range(4) for w in range(4)]
         passed = []
-        for dz in range(4):
-            for copy in copies[dz]:
-                copy.wait_recv()
-            origin = lax.rem(z + 4 - dz, 4)
-            block = whole.at[pl.ds(pl.multiple_of((origin * 2 + x) * 4 * rows, 4 * rows), 4 * rows)]
-            passed.append(go(block, block, recv.at[dz], x_peer))
+        for number, (dz, offset, length) in enumerate(spans):
+            start = (lax.rem(z + 4 - dz, 4) * 2 + x) * 4 * rows + offset
+            block = whole.at[pl.ds(pl.multiple_of(start, 16), length)]
+            passed.append(go(block, block, recv.at[number], x_peer))
         return passed
-
-    got_w1 = spread(w1, w1q, 144, r_w1)
-    got_w2 = spread(w2, w2q, 288, r_w2)
-
-    settle(own_bot)
-    for copy in bots:
-        copy.wait_recv()
-    to_c = go(xr.at[:, wa], xr.at[:, wa], r_grp.at[0], c_peer)
-    to_y = go(xr.at[:, wa], xr.at[:, wa], r_grp.at[1], y_peer)
 
     def spread_z(shard, whole, recv):
         own = stay(shard, whole.at[z, x, y, c])
@@ -360,66 +366,80 @@
         ]
         return (own, copies)
 
-    def spread_two(whole, got, recv, half):
-        own, copies = got
-        settle(own)
-        for copy in copies:
-            copy.wait_recv()
-        low, high = (pl.ds(0, half), pl.ds(half, half))
-        part = whole.at[:, x, y, c]
-        core = go(part, part, recv.at[3], c_peer)
+    def spread_two(whole, got, recv, half, width):
+        settle(got[0])
+        arrive(*got[1])
+        low, high = (pl.ds(0, half), pl.ds(half, width - half))
         part = whole.at[:, x, y, c, :, low]
         first = go(part, part, recv.at[4], x_peer)
         part = whole.at[:, x, y, c, :, high]
         second = go(part, part, recv.at[5], y_peer)
+        part = whole.at[:, x, y, c]
+        core = go(part, part, recv.at[3], c_peer)
         return (core, first, second)
 
-    def spread_three(whole, got, recv, half):
+    def spread_three(whole, got, recv, half, width):
         core, first, second = got
-        low, high = (pl.ds(0, half), pl.ds(half, half))
-        first.wait_recv()
+        low, high = (pl.ds(0, half), pl.ds(half, width - half))
+        arrive(first)
         part = whole.at[:, :, y, c, :, low]
         third = go(part, part, recv.at[6], y_peer)
         part = whole.at[:, 1 - x, y, c, :, low]
         core_first = go(part, part, recv.at[8], c_peer)
-        second.wait_recv()
+        arrive(second)
         part = whole.at[:, x, :, c, :, high]
         fourth = go(part, part, recv.at[7], x_peer)
         part = whole.at[:, x, 1 - y, c, :, high]
         core_second = go(part, part, recv.at[9], c_peer)
         return (core, core_first, core_second, third, fourth)
 
-    def spread_four(whole, got, recv, half):
+    def spread_four(whole, got, recv, half, width):
         core, core_first, core_second, third, fourth = got
-        low, high = (pl.ds(0, half), pl.ds(half, half))
-        third.wait_recv()
+        low, high = (pl.ds(0, half), pl.ds(half, width - half))
+        arrive(third)
         part = whole.at[:, :, 1 - y, c, :, low]
         core_third = go(part, part, recv.at[10], c_peer)
-        fourth.wait_recv()
+        arrive(fourth)
         part = whole.at[:, 1 - x, :, c, :, high]
         core_fourth = go(part, part, recv.at[11], c_peer)
-        return (core, core_first, core_second, core_third, core_fourth)
-
-    own_head = stay(wh, wh_out.at[mine])
+        arrive(core, core_first, core_second, core_third, core_fourth)
+
+    own_bot = stay(bot.at[ha], xr.at[ha, wa])
+    bots = [
+        go(bot.at[lax.rem(ha + d, 8)], xr.at[ha, wa], r_bot.at[d - 1], (lax.rem(ha + d, 8), wa))
+        for d in range(1, 8)
+    ]
+    got_w1 = spread(w1, w1q, 144, 0, 144, r_w1)
+    own_code = stay(code.at[ha], code_out.at[ha])
+    codes = [
+        go(code.at[lax.rem(ha + d, 8)], code_out.at[ha], r_code.at[d - 1], (lax.rem(ha + d, 8), wa))
+        for d in range(1, 8)
+    ]
+    own_head = stay(wh, whv.at[mine])
     heads = []
     for step in range(1, 32):
         other = lax.rem(mine + step, 32)
-        heads.append(go(wh, wh_out.at[mine], r_wh.at[step - 1], (other // 4, lax.rem(other, 4))))
-
-    passed_w1 = pass_x(w1q, 144, got_w1, r_w1x)
-    got_w3 = spread_z(w3, w3_out, r_w3)
-
-    to_y.wait_recv()
-    part = xr.at[:, 2 * (1 - y) + c]
-    on_c = go(part, part, r_grp.at[2], c_peer)
-    to_c.wait_recv()
-    on_c.wait_recv()
-
+        heads.append(go(wh, whv.at[mine], r_wh.at[step - 1], (other // 4, lax.rem(other, 4))))
+    settle(own_bot)
+    arrive(*bots)
+    to_c = go(xr.at[:, wa], xr.at[:, wa], r_grp.at[0], c_peer)
+    to_y = go(xr.at[:, wa], xr.at[:, wa], r_grp.at[1], y_peer)
     if compute:
         x0[:, 0] = jnp.zeros((3, 32, 512), HALF)
         x0[:, 17] = jnp.zeros((3, 32, 512), HALF)
         h1[:, 0] = jnp.zeros((3, 32, 1024), HALF)
         h1[:, 17] = jnp.zeros((3, 32, 1024), HALF)
+        for shift in range(3):
+            tiles[shift, :, 0] = jnp.zeros((3, 16, 1024), HALF)
+            tiles[shift, :, 33] = jnp.zeros((3, 16, 1024), HALF)
+    passed_w1 = pass_x(w1q, 144, 0, 144, got_w1, r_w1x)
+    got_w2a = spread(w2, w2q, 288, 0, 144, r_w2.at[0])
+    arrive(to_y)
+    part = xr.at[:, 2 * (1 - y) + c]
+    on_c = go(part, part, r_grp.at[2], c_peer)
+    arrive(to_c, on_c)
+
+    if compute:
 
         def reorder(h, carry):
             block = xr[h].astype(FLOAT).reshape(4, 3, 2, 8, 512)
@@ -431,9 +451,9 @@
 
         lax.fori_loop(0, 8, reorder, 0)
     stay(x0.at[:, pl.ds(1, 16)], x0_out)
-
-    for copy in passed_w1:
-        copy.wait_recv()
+    passed_w2a = pass_x(w2q, 288, 0, 144, got_w2a, r_w2x.at[0])
+    got_w2b = spread(w2, w2q, 288, 144, 144, r_w2.at[1])
+    arrive(*passed_w1)
     if compute:
 
         def one(s, carry):
@@ -451,24 +471,21 @@
     h1_c = go(h1s, lanes(wa), r_h1.at[0], c_peer)
     h1_y = go(h1s, lanes(wa), r_h1.at[1], y_peer)
 
-    passed_w2 = pass_x(w2q, 288, got_w2, r_w2x)
-    got_wu = spread_z(wu, wu_out, r_wu)
-    own_skip = stay(skip.at[ha], sk_out.at[ha])
+    passed_w2b = pass_x(w2q, 288, 144, 144, got_w2b, r_w2x.at[1])
+    got_wu = spread_z(wu, wuv, r_wu)
+    got_w3 = spread_z(w3, w3v, r_w3)
+    own_skip = stay(skip.at[ha], skv.at[ha])
     skips = [
-        go(skip.at[lax.rem(ha + d, 8)], sk_out.at[ha], r_skip.at[d - 1], (lax.rem(ha + d, 8), wa))
+        go(skip.at[lax.rem(ha + d, 8)], skv.at[ha], r_skip.at[d - 1], (lax.rem(ha + d, 8), wa))
         for d in range(1, 8)
     ]
-    got_w3 = spread_two(w3_out, got_w3, r_w3, 256)
-
-    h1_y.wait_recv()
+    arrive(h1_y)
     h1_on = go(lanes(2 * (1 - y) + c), lanes(2 * (1 - y) + c), r_h1.at[2], c_peer)
     settle(own_h1)
-    h1_c.wait_recv()
-    h1_on.wait_recv()
+    arrive(h1_c, h1_on)
     stay(h1.at[:, pl.ds(1, 16)], h1_out)
-
-    for copy in passed_w2:
-        copy.wait_recv()
+    got_wu = spread_two(wuv, got_wu, r_wu, 1536, 2048)
+    arrive(*passed_w2a, *passed_w2b)
     stay(w2q, w2_out)
     if compute:
 
@@ -486,20 +503,134 @@
             return carry
 
         lax.fori_loop(0, 3, two, 0)
-    h2_lanes = h2_out.at[:, pl.ds(pl.multiple_of(wa * 256, 256), 256)]
-    stay(h2s.at[wa], h2_lanes)
+    h2_lanes = h2v.at[:, pl.ds(pl.multiple_of(wa * 256, 256), 256)]
+    own_h2 = stay(h2s.at[wa], h2_lanes)
     h2_got = [
         go(h2s.at[lax.rem(wa + d, 4)], h2_lanes, r_h2.at[d - 1], (ha, lax.rem(wa + d, 4)))
         for d in range(1, 4)
     ]
-
-    got_wu = spread_two(wu_out, got_wu, r_wu, 1024)
-    got_w3 = spread_three(w3_out, got_w3, r_w3, 256)
-    got_wu = spread_three(wu_out, got_wu, r_wu, 1024)
-    got_w3 = spread_four(w3_out, got_w3, r_w3, 256)
-    got_wu = spread_four(wu_out, got_wu, r_wu, 1024)
-    for copy in list(got_w3) + list(got_wu) + h2_got + skips + heads:
-        copy.wait_recv()
+    got_w3 = spread_two(w3v, got_w3, r_w3, 384, 512)
+    got_wu = spread_three(wuv, got_wu, r_wu, 1536, 2048)
+
+    settle(own_skip)
+    arrive(*skips)
+
+    def skip_slice(s):
+        return skv[:, 64 * s : 64 * s + 64].astype(FLOAT).reshape(32, 16, 512)
+
+    if compute:
+        for s in range(3):
+            value = skip_slice(s)
+            rims[0, s] = value[:, 0].astype(HALF)
+            rims[1, s] = value[:, 15].astype(HALF)
+    before = (ha, lax.rem(wa + 3, 4))
+    after = (ha, lax.rem(wa + 1, 4))
+    rim_right = go(rims.at[0], rims_got.at[1], r_rim.at[1], before)
+    rim_left = go(rims.at[1], rims_got.at[0], r_rim.at[0], after)
+    got_w3 = spread_three(w3v, got_w3, r_w3, 384, 512)
+    arrive(rim_right, rim_left)
+    if compute:
+        for s in range(3):
+            left = jnp.where(wa > 0, rims_got[0, s].astype(FLOAT), 0.0)
+            right = jnp.where(wa < 3, rims_got[1, s].astype(FLOAT), 0.0)
+            put_shifts(
+                tiles, pl.ds(512, 512), s, skip_slice(s), left[:, None, :], right[:, None, :]
+            )
+    spread_four(wuv, got_wu, r_wu, 1536, 2048)
+    stay(wuv, wu_out)
+    settle(own_h2)
+    arrive(*h2_got)
+    stay(h2v, h2_out)
+    if compute:
+        order = lax.broadcasted_iota(jnp.int32, (256, 256), 1)
+        inner = order % 128
+        pick = (inner // 8) * 16 + (inner % 8) * 2 + order // 128
+        woven = jnp.where(lax.broadcasted_iota(jnp.int32, (256, 256), 0) == pick, 1.0, 0.0)
+        woven = woven.astype(HALF)
+        wide = wuv.reshape(1024, 2048)
+        for s in range(3):
+            fine, sides = ([], ([], []))
+            for a in range(2):
+                weight = wide[:, 1024 * a : 1024 * a + 1024]
+                flat = jnp.dot(
+                    h2v[128 * s : 128 * s + 128], weight, preferred_element_type=FLOAT
+                ).astype(HALF)
+                flat = jnp.concatenate([flat[:, :512], flat[:, 512:]], axis=0)
+                flat = jnp.dot(woven, flat, preferred_element_type=FLOAT)
+                fine.append(flat.reshape(16, 16, 512))
+                for side in range(2):
+                    start = 384 + 48 * side + 16 * s
+                    rim = jnp.dot(
+                        h2v[start : start + 16],
+                        weight[:, 512 * (1 - side) : 512 * (1 - side) + 512],
+                        preferred_element_type=FLOAT,
+                    )
+                    sides[side].append(rim.astype(HALF).astype(FLOAT)[:, None, :])
+            value = jnp.stack(fine, axis=1).reshape(32, 16, 512)
+            left, right = [jnp.stack(side, axis=1).reshape(32, 1, 512) for side in sides]
+            put_shifts(tiles, pl.ds(0, 512), s, value, left, right)
+    stay(tiles.at[1, :, pl.ds(1, 32)], joined_out)
+    settle(own_head)
+    arrive(*heads)
+    settle(own_code)
+    arrive(*codes)
+    spread_four(w3v, got_w3, r_w3, 384, 512)
+    stay(w3v, w3_out)
+    if compute:
+        head = whv.reshape(512, 128)[...].astype(FLOAT).T[:16].astype(HALF)
+        head_out[...] = head
+        rows = w3v.reshape(9216, 512)
+        row = lax.broadcasted_iota(jnp.int32, (8, 128), 0)
+        lane = lax.broadcasted_iota(jnp.int32, (8, 128), 1)
+        sums_out[0] = jnp.zeros((8, 128), FLOAT)
+
+        def three(s, carry):
+            pre3_out[s] = jnp.zeros((512, 512), FLOAT)
+
+            def tap(t, inner_carry):
+                window = tiles[t % 3, s, pl.ds(t // 3, 32)].reshape(512, 1024)
+                start = pl.multiple_of(1024 * t, 1024)
+                pre3_out[s] += jnp.dot(
+                    window, rows[pl.ds(start, 1024), :], preferred_element_type=FLOAT
+                )
+                return inner_carry
+
+            lax.fori_loop(0, 9, tap, 0)
+            hidden = gelu_of(pre3_out[s]).astype(HALF)
+            hidden_out[s] = hidden
+            logits = lax.dot_general(
+                head, hidden, (((1,), (1,)), ((), ())), preferred_element_type=FLOAT
+            )
+            logit_out[s] = logits
+            return carry
+
+        lax.fori_loop(0, 3, three, 0)
+        total = jnp.zeros((8, 128), FLOAT)
+        for s in range(3):
+            probability, target, weighted = class_terms(logit_out, code_out, s)
+            for k in range(2):
+                terms = (
+                    weighted * probability[k] * target[k],
+                    weighted * probability[k],
+                    weighted * target[k],
+                )
+                for j, term in enumerate(terms):
+                    value = jnp.sum(term, axis=1, keepdims=True)
+                    here_is = jnp.logical_and(row == s, lane == 3 * k + j)
+                    total = total + jnp.where(here_is, value, 0.0)
+        sums_out[0] = total
+    sums = []
+    for step in range(1, 32):
+        other = lax.rem(mine + step, 32)
+        sums.append(
+            go(
+                sums_out.at[0],
+                sums_out.at[step],
+                r_sum.at[step - 1],
+                (other // 4, lax.rem(other, 4)),
+            )
+        )
+    arrive(*sums)
     for entry in stays:
         if not entry[1]:
             settle(entry)
@@ -507,11 +638,27 @@
         copy.wait_send()
 
 
-def front(bot, skip, w1, w2, wu, w3, wh, compute=True):
+def class_terms(logits, codes, s):
+    pieces = [codes[2 * q, s : s + 1] + codes[2 * q + 1, s : s + 1] for q in range(4)]
+    both = jnp.concatenate(pieces, axis=1)
+    label = jnp.where(both >= 2.0, 1.0, 0.0)
+    weighted = both - 2.0 * label
+    first, second = (logits[s, 0:1], logits[s, 1:2])
+    top = jnp.maximum(first, second)
+    first, second = (jnp.exp(first - top), jnp.exp(second - top))
+    scale = 1.0 / (first + second)
+    return ((first * scale, second * scale), (1.0 - label, label), weighted)
+
+
+def front(bot, skip, code, w1, w2, wu, w3, wh, compute=True):
     anywhere = pl.BlockSpec(memory_space=pl.ANY)
     inside = pl.BlockSpec(memory_space=pltpu.VMEM)
     shape = jax.ShapeDtypeStruct
     dma = pltpu.SemaphoreType.DMA
+
+    def room(*dims):
+        return pltpu.VMEM(dims, HALF)
+
     return pl.pallas_call(
         functools.partial(front_kernel, compute),
         name="front",
@@ -519,86 +666,60 @@
             shape((3, 16, 32, 512), HALF),
             shape((3, 16, 32, 1024), HALF),
             shape((480, 1024), HALF),
-            shape((8, 192, 512), HALF),
+            shape((3, 32, 16, 1024), HALF),
             shape((9216, 256), HALF),
             shape((4, 2, 2, 2, 32, 2048), HALF),
             shape((4, 2, 2, 2, 288, 512), HALF),
-            shape((32, 16, 128), HALF),
             shape((3, 16, 32, 256), FLOAT),
             shape((3, 16, 32, 256), FLOAT),
+            shape((3, 512, 512), FLOAT),
+            shape((3, 512, 512), HALF),
+            shape((3, 16, 512), FLOAT),
+            shape((8, 8, 128), FLOAT),
+            shape((32, 8, 128), FLOAT),
+            shape((16, 512), HALF),
         ),
-        in_specs=[anywhere] * 7,
-        out_specs=[anywhere] * 8 + [inside] * 2,
+        in_specs=[anywhere] * 8,
+        out_specs=[anywhere] * 7 + [inside] * 8,
         scratch_shapes=[
-            pltpu.VMEM((8, 4, 48, 512), HALF),
-            pltpu.VMEM((3, 18, 32, 512), HALF),
-            pltpu.VMEM((4608, 256), HALF),
-            pltpu.VMEM((9216, 256), HALF),
-            pltpu.VMEM((3, 16, 32, 256), HALF),
-            pltpu.VMEM((3, 18, 32, 1024), HALF),
+            room(8, 4, 48, 512),
+            room(3, 18, 32, 512),
+            room(4608, 256),
+            room(9216, 256),
+            room(3, 16, 32, 256),
+            room(3, 18, 32, 1024),
             pltpu.VMEM((3, 512, 256), FLOAT),
-            pltpu.VMEM((4, 480, 256), HALF),
-            dma((136,)),
-            dma((16,)),
+            room(4, 480, 256),
+            room(480, 1024),
+            room(4, 2, 2, 2, 32, 2048),
+            room(4, 2, 2, 2, 288, 512),
+            room(8, 192, 512),
+            room(2, 3, 32, 512),
+            room(2, 3, 32, 512),
+            room(3, 3, 34, 16, 1024),
+            room(32, 16, 128),
+            dma((220,)),
+            dma((24,)),
             dma((7,)),
             dma((3,)),
             dma((4, 4)),
             dma((4,)),
-            dma((4, 4)),
-            dma((4,)),
+            dma((2, 4, 4)),
+            dma((2, 16)),
             dma((3,)),
             dma((3,)),
             dma((7,)),
             dma((31,)),
             dma((12,)),
             dma((12,)),
+            dma((7,)),
+            dma((2,)),
+            dma((31,)),
         ],
         compiler_params=pltpu.CompilerParams(
-            collective_id=0, has_side_effects=True, vmem_limit_bytes=60 * 1024 * 1024
+            collective_id=0, has_side_effects=True, vmem_limit_bytes=64 * 1024 * 1024
         ),
-    )(bot, skip, w1, w2, wu, w3, wh)
-
-
-def sum_kernel(part, out, got, send, recv):
-    row, col = (lax.axis_index("ha"), lax.axis_index("wa"))
-    mine = row * 4 + col
-    greet_all()
-    copies = []
-    for step in range(1, 32):
-        other = lax.rem(mine + step, 32)
-        copy = remote(
-            part,
-            got.at[step],
-            send.at[step - 1],
-            recv.at[step - 1],
-            (other // 4, lax.rem(other, 4)),
-        )
-        copy.start()
-        copies.append(copy)
-    total = part[...]
-    for step in range(1, 32):
-        copies[step - 1].wait_recv()
-        total = total + got[step]
-    out[...] = total
-    for copy in copies:
-        copy.wait_send()
-
-
-def sum_all(part):
-    inside = pl.BlockSpec(memory_space=pltpu.VMEM)
-    return pl.pallas_call(
-        sum_kernel,
-        name="sum_all",
-        out_shape=jax.ShapeDtypeStruct((8, 128), FLOAT),
-        in_specs=[inside],
-        out_specs=inside,
-        scratch_shapes=[
-            pltpu.VMEM((32, 8, 128), FLOAT),
-            pltpu.SemaphoreType.DMA((31,)),
-            pltpu.SemaphoreType.DMA((31,)),
-        ],
-        compiler_params=pltpu.CompilerParams(collective_id=1, has_side_effects=True),
-    )(part)
+    )(bot, skip, code, w1, w2, wu, w3, wh)
 
 
 def gelu_slope(value):
@@ -622,11 +743,12 @@
 
 
 def back_kernel(
-    gs_in, w3_in, wu_in, w2_in, joined_in, h2_in, h1_in, x0_in, pre1_in, pre2_in, dh,
+    w3_in, wu_in, w2_in, joined_in, h2_in, h1_in, x0_in, pre1_in, pre2_in, pre3_in, hidden_in,
+    logits, codes, slopes, head,
     g3, gu, g2, g1, gh,
-    gs3, joined, slot, acc, flat, wu, h2, gh2, from_wa, pre, gs2, d_core, d_y,
+    gs3, rims, rims_got, dh, joined, slot, acc, flat, wu, h2, gh2, from_wa, pre, gs2, d_core, d_y,
     du_c, du_y, du_x, du_z, d3, d3_c, d3_y, d3_x, d3_z, d2, d2_x, d2_z, d1_x, d1_z, hh,
-    send, here, r_wa, r_d, r_u, r_3, r_2, r_1, r_h, free,
+    send, here, r_rim, r_wa, r_d, r_u, r_3, r_2, r_1, r_h, free,
 ):
     z, x, y, c = place()
     ha, wa = (2 * z + x, 2 * y + c)
@@ -652,7 +774,8 @@
             entry[0].wait()
             entry[1] = True
 
-    got_gs = stay(gs_in, gs3)
+    got_hidden = stay(hidden_in, d3.at[pl.ds(0, 1536)])
+    got_pre3 = stay(pre3_in.at[0], acc)
     got_w3 = [
         stay(
             w3_in.at[pl.ds(1024 * t, 512), pl.ds(256 * half, 256)],
@@ -665,6 +788,39 @@
     got_h2 = stay(h2_in.at[pl.ds(0, 384)], h2)
     got_joined = stay(joined_in, joined)
     greet_all()
+
+    settle(got_hidden)
+    head_sum = jnp.zeros((16, 512), FLOAT)
+    class_row = lax.broadcasted_iota(jnp.int32, (16, 512), 0)
+    for e in range(3):
+        gs3[e, :, 0] = jnp.zeros((3, 16, 512), HALF)
+        gs3[e, :, 33] = jnp.zeros((3, 16, 512), HALF)
+    for s in range(3):
+        probability, target, weighted = class_terms(logits, codes, s)
+        grads = [
+            weighted * (target[k] * slopes[s : s + 1, k : k + 1] + slopes[s : s + 1, 2 + k : 3 + k])
+            for k in range(2)
+        ]
+        inner = probability[0] * grads[0] + probability[1] * grads[1]
+        grads = [probability[k] * (grads[k] - inner) for k in range(2)]
+        grads = jnp.where(class_row == 0, grads[0], jnp.where(class_row == 1, grads[1], 0.0))
+        grads = grads.astype(HALF)
+        hidden = d3[512 * s : 512 * s + 512]
+        head_sum = head_sum + jnp.dot(grads, hidden, preferred_element_type=FLOAT)
+        settle(got_pre3)
+        value = (across(grads, head[...]) * gelu_slope(acc[...])).astype(HALF)
+        if s < 2:
+            got_pre3 = stay(pre3_in.at[s + 1], acc)
+        gs3[1, s, 1:33] = value.reshape(32, 16, 512)
+        value = value.astype(FLOAT).reshape(32, 16, 512)
+        rims[0, s] = value[:, 0].astype(HALF)
+        rims[1, s] = value[:, 15].astype(HALF)
+    before = (ha, lax.rem(wa + 3, 4))
+    after = (ha, lax.rem(wa + 1, 4))
+    rim_right = go(rims.at[0], rims_got.at[1], r_rim.at[1], before)
+    rim_left = go(rims.at[1], rims_got.at[0], r_rim.at[0], after)
+    rows = jnp.concatenate([head_sum, jnp.zeros((112, 512), FLOAT)], axis=0)
+    dh[...] = rows.T.reshape(32, 16, 128)
     own_head = stay(dh.at[mine], hh.at[0])
     heads = []
     for step in range(1, 32):
@@ -672,12 +828,19 @@
         heads.append(
             go(dh.at[other], hh.at[step], r_h.at[step - 1], (other // 4, lax.rem(other, 4)))
         )
+    rim_right.wait_recv()
+    rim_left.wait_recv()
+    for s in range(3):
+        left = jnp.where(wa > 0, rims_got[0, s].astype(FLOAT), 0.0)
+        right = jnp.where(wa < 3, rims_got[1, s].astype(FLOAT), 0.0)
+        value = gs3[1, s, 1:33].astype(FLOAT)
+        put_shifts(gs3, pl.ds(0, 512), s, value, left[:, None, :], right[:, None, :])
 
     order = lax.broadcasted_iota(jnp.int32, (256, 256), 0)
     inner = order % 128
     pick = (inner // 8) * 16 + (inner % 8) * 2 + order // 128
     apart = jnp.where(lax.broadcasted_iota(jnp.int32, (256, 256), 1) == pick, 1.0, 0.0).astype(HALF)
-    settle(got_gs, *got_w3)
+    settle(*got_w3)
 
     def three_source(s, carry):
         acc[...] = jnp.zeros_like(acc)
@@ -999,7 +1162,7 @@
         copy.wait_send()
 
 
-def back(gs, w3, wu, w2, joined, h2, h1, x0, pre1, pre2, dh):
+def back(*args):
     anywhere = pl.BlockSpec(memory_space=pl.ANY)
     inside = pl.BlockSpec(memory_space=pltpu.VMEM)
     shape = jax.ShapeDtypeStruct
@@ -1018,10 +1181,13 @@
             shape((144, 1024), HALF),
             shape((16, 128), FLOAT),
         ),
-        in_specs=[anywhere] * 11,
+        in_specs=[anywhere] * 11 + [inside] * 4,
         out_specs=[inside, inside, anywhere, anywhere, inside],
         scratch_shapes=[
             room(3, 3, 34, 16, 512),
+            room(2, 3, 32, 512),
+            room(2, 3, 32, 512),
+            pltpu.VMEM((32, 16, 128), FLOAT),
             room(1536, 1024),
             room(9216, 256),
             pltpu.VMEM((512, 512), FLOAT),
@@ -1051,6 +1217,7 @@
             pltpu.VMEM((32, 16, 128), FLOAT),
             dma((144,)),
             dma((40,)),
+            dma((2,)),
             dma((3,)),
             dma((6,)),
             dma((31,)),
@@ -1063,23 +1230,17 @@
         compiler_params=pltpu.CompilerParams(
             collective_id=2, has_side_effects=True, vmem_limit_bytes=64 * 1024 * 1024
         ),
-    )(gs, w3, wu, w2, joined, h2, h1, x0, pre1, pre2, dh)
-
-
-def conv_with(source, weight, col_rim):
-    chan = source.shape[3]
-    return lax.conv_general_dilated(
-        source,
-        weight.reshape(3, 3, chan, weight.shape[1]),
-        (1, 1),
-        ((1, 1), (col_rim, col_rim)),
-        dimension_numbers=("NHWC", "HWIO", "NHWC"),
-        preferred_element_type=FLOAT,
-    )
-
-
-def with_cols(block):
-    return with_halo(block, (("wa", 2),), 1)
+    )(*args)
+
+
+def dice_slopes(totals):
+    union_sum = totals[..., 1] + totals[..., 2] + SMOOTHING
+    numerator = 2.0 * totals[..., 0] + SMOOTHING
+    dice_score = numerator / union_sum
+    loss_value = 1.0 - jnp.mean(dice_score)
+    entry_count = float(dice_score.size)
+    common = -2.0 / (entry_count * union_sum)
+    return (loss_value, jnp.concatenate([common, numerator / (entry_count * union_sum**2)], axis=1))
 
 
 def sliced_grads(
@@ -1087,12 +1248,14 @@
     weight_head,
 ):
     ha = lax.axis_index("ha")
-    code = lax.all_to_all(pixel_mask + 2 * labels, "ha", 0, 1, tiled=True)
-    mask, label = (code % 2, code // 2)
+    code = (pixel_mask + 2 * labels).astype(FLOAT).reshape(8, 3, 64)
+    pads = [jnp.pad(code, ((0, 0), (0, 5), (64 * odd, 64 - 64 * odd))) for odd in range(2)]
+    code = jnp.where(ha % 2 == 0, *pads)
     head_rows = jnp.pad(weight_head.astype(HALF), ((0, 0), (0, 126)))
-    x0, h1, h2, skip, w2, wu, w3, wh, pre_one, pre_two = front(
+    x0, h1, h2, joined, w2, wu, w3, pre_one, pre_two, pre_three, hidden_three, logits, code, sums, head = front(
         bottom.reshape(8, 48, 512),
         skipped.reshape(8, 192, 512),
+        code,
         weight_one.astype(HALF),
         weight_two.astype(HALF),
         weight_up.astype(HALF),
@@ -1101,53 +1264,36 @@
     )
     wu = wu.reshape(1024, 2048)
     w3 = w3.reshape(9216, 512)
-    wh = wh.reshape(512, 128)[:, :2]
-    skip = skip.reshape(8, 3, 4, 16, 512).transpose(1, 0, 2, 3, 4).reshape(3, 32, 16, 512)
-    skip = with_cols(skip)
-    hidden_two = h2[:384].reshape(3, 16, 8, 1024)
-    ups = upsample(hidden_two, wu).astype(HALF)
-    taps = wu.reshape(1024, 2, 2, 512)
-    rims = [
-        jnp.einsum(
-            "pc,caq->paq",
-            h2[384 + 48 * side : 432 + 48 * side],
-            taps[:, :, 1 - side],
-            preferred_element_type=FLOAT,
-        )
-        .astype(HALF)
-        .reshape(3, 32, 1, 512)
-        for side in range(2)
-    ]
-    joined = jnp.concatenate(
-        [jnp.concatenate([rims[0], ups, rims[1]], axis=2), skip], axis=3
-    )
-    pre_three = conv_with(joined, w3, 0)
-    hidden_three = smooth(pre_three).astype(HALF)
-    logits = jnp.einsum("shwc,ck->shwk", hidden_three, wh, preferred_element_type=FLOAT)
     member = (groups[:, None] == jnp.arange(GROUPS)[None, :]).astype(FLOAT)
+    step = lax.axis_index("ha") * 4 + lax.axis_index("wa")
+    origin = (step - jnp.arange(32)) % 32
+    at_group = jnp.einsum(
+        "dh,hsg->dsg",
+        (origin[:, None] // 4 == jnp.arange(8)[None, :]).astype(FLOAT),
+        member.reshape(8, 3, GROUPS),
+        precision=HIGHEST,
+    )
+    totals = jnp.einsum("dsg,dsq->gq", at_group, sums[:, :3, :6], precision=HIGHEST)
+    totals = totals.reshape(GROUPS, 2, 3)
+    loss_value, slopes = dice_slopes(totals)
     member = lax.dynamic_slice_in_dim(member, 3 * ha, 3, axis=0)
-    sums = dice_terms(logits, mask, label, member).reshape(1, 30)
-    sums = sum_all(jnp.pad(sums, ((0, 7), (0, 98))))
-    totals = sums[0, :30].reshape(GROUPS, 2, 3)
-    loss_value, grad_logits = dice_back(logits, mask, label, member, totals)
-    head_grad = jnp.einsum("shwc,shwk->ck", hidden_three, grad_logits, preferred_element_type=FLOAT)
-    grad_hidden = jnp.einsum("shwk,ck->shwc", grad_logits, wh, preferred_element_type=FLOAT)
-    grad_three = smooth_back(pre_three, grad_hidden).astype(HALF)
-    grad_wide = with_cols(grad_three)
-    grad_rows = jnp.pad(grad_wide, ((0, 0), (1, 1), (0, 0), (0, 0)))
-    shifts = jnp.stack([grad_rows[:, :, e : e + 16] for e in range(3)])
+    slopes = jnp.einsum("sg,gq->sq", member, slopes, precision=HIGHEST)
     g3, gu, g2, g1, gh = back(
-        shifts,
         w3,
         wu,
         w2,
-        joined[:, :, 1:17].reshape(1536, 1024),
+        joined.reshape(1536, 1024),
         h2,
         h1.reshape(1536, 1024),
         x0.reshape(1536, 512),
         pre_one,
         pre_two,
-        jnp.pad(head_grad, ((0, 0), (0, 126))).reshape(32, 16, 128),
+        pre_three,
+        hidden_three.reshape(1536, 512),
+        logits,
+        code,
+        jnp.pad(slopes, ((0, 5), (0, 124))),
+        head,
     )
     return (loss_value, g1.astype(FLOAT), g2.astype(FLOAT), gu, g3, gh[:, :2])
 

time: 617 us -> 525 us (0.85)
  matrix products: 64.4 us -> 1.85 us
  local copies, waits for them, and re-layouts: 48.7 us -> 7.02 us
  Pallas kernels: 447 us -> 488 us
  starting transfers between devices: 16.8 us -> 0 us
  other arithmetic: 27.5 us -> 15.1 us
    conv_general_dilated x1 -> x0, matrix products: 44.7 us -> none  [conv_with(): lax.conv_general_dilated(source, weight.reshape(3, 3, chan, weight.shape[...]
    pallas_call x1, Pallas kernels: 216 us -> 256 us  [front(): pl.pallas_call(functools.partial(front_kernel, compute), name='front', ou...]
    dot_general x8 -> x3, matrix products: 16.3 us -> 1.85 us  [the longest x1 0.94 us: sliced_grads(): jnp.einsum('dsg,dsq->gq', at_group, sums[:, :3, :6], precision=HIGHEST)]
    slice x7 -> x1, local copies, waits for them, and re-layouts: 13.1 us -> 0.91 us  [sliced_grads(): sums[:, :3, :6]]
    ppermute x4 -> x0, starting transfers between devices: 11.1 us -> none  [the longest x2 6.8 us: with_halo(): lax.ppermute(lax.slice_in_dim(block, 0, width, axis=dim), axis, backward)]
    pallas_call x1, Pallas kernels: 221 us -> 232 us  [back(): pl.pallas_call(back_kernel, name='back', out_shape=(shape((288, 512), FLO...]
    pallas_call x1 -> x0, Pallas kernels: 10.4 us -> none  [sum_all(): pl.pallas_call(sum_kernel, name='sum_all', out_shape=jax.ShapeDtypeStruct...]
    another operation x6 -> x0, local copies, waits for them, and re-layouts: 9.38 us -> none  [the longest x1 7.8 us: sliced_grads(): taps = wu.reshape(1024, 2, 2, 512)]
  transfers between devices with their start and end apart: 5 -> 0, of which waited for: 0 -> 0; matrix products, arithmetic and copies ran while one was open for 8% -> 0% of each run, Pallas kernels for 0% -> 0%
where the time goes in v3:
time: 525 us; the launch traced here: 515 us
  Pallas kernels  488 us (93%)
  other arithmetic  15.1 us (3%)
  local copies, waits for them, and re-layouts  7.02 us (1%)
    pallas_call x1, Pallas kernels, front(): pl.pallas_call(functools.partial(front_kernel, compute), name='front', ou...  256 us
    pallas_call x1, Pallas kernels, back(): pl.pallas_call(back_kernel, name='back', out_shape=(shape((288, 512), FLO...  232 us

profile of v3, /device:TPU:14, one launch (start us, length us, event | category | flops | bytes accessed | tf_op | source)
XLA Modules:
  0.0 514.8 jit_solution(12529051938479481449)
XLA Ops:
  0.7 0.8 eq.45
  1.5 0.1 copy.58
  1.6 0.7 fusion.5
  2.3 0.8 add_convert_fusion
  3.1 0.1 copy.59
  3.2 0.1 reshape.129
  3.3 0.7 pad_select_fusion.code
  4.0 1.9 convert_element_type.35.w1
  5.9 0.9 convert_element_type.36.w2
  6.8 0.7 convert_element_type.37.wu
  7.4 0.8 convert_element_type.38.w3
  8.2 0.1 copy.60
  8.3 0.6 pad.18.wh
  8.9 256.2 %front.1 = (bf16[3,16,32,512]{3,2,1,0:T(8,128)(2,1)}, bf16[3,16,32,1024]{3,2,1,0:T(8,128)(2,1)}, bf16[480,1024]{1,0:T(8,128)(2,1)}, bf16[3,32,16,1024]{3,2,1,0:T...) custom-call(bf16[8,48,512]{2,1,0:T(8,128)(2,1)} %bitcast.25, ...), custom_call_target="tpu_custom_call" | custom-call | tf_op jit(solution)/shard_map/front/pallas_call | solution.py:662
  265.1 0.9 slice.15
  266.0 0.9 convolution_bitcast_fusion
  267.0 0.6 multiply_divide_fusion
  268.3 0.7 dynamic-slice
  269.0 0.2 fusion.9
  269.2 0.6 pad.19.slopes
  269.8 231.8 %back.1 = (f32[288,512]{1,0:T(8,128)}, f32[32,2048]{1,0:T(8,128)}, bf16[288,1024]{1,0:T(8,128)(2,1)}, bf16[144,1024]{1,0:T(8,128)(2,1)}, f32[16,128]{1,0:T(8,128)}) custom-call(bf16[9216,512]{1,0:T(8,128)(2,1)} %bitcast.18, bf16[1024,2048]{1,0:T(8,128)(2,1)} %bitcast.19, bf16[9216,256]{1,0:T(8,128)(2,1)} %get-tuple-element.39.w2_in, ...), custom_call_target="tpu_custom_call" | custom-call | tf_op jit(solution)/shard_map/back/pallas_call | solution.py:1174
  501.6 3.1 add_multiply_fusion.2
  504.8 3.4 add_multiply_fusion
  508.2 0.9 add_multiply_fusion.3
  509.1 0.2 copy-done.3
  509.3 0.3 copy-done.8
  509.6 0.2 copy-done.9
  509.8 1.4 add_multiply_fusion.1
  511.4 0.1 copy.63
  511.5 0.6 copy.67
  512.2 0.6 copy.68
  512.8 0.6 copy.69
  (43 shorter events, 0.3 us)
Async XLA Ops:
  0.6 5.2 %copy-start = (f32[288,1024]{1,0:T(8,128)S(1)}, f32[288,1024]{1,0:T(8,128)}, u32[]{:S(2)}) copy-start(f32[288,1024]{1,0:T(8,128)} %param.28) | copy-start | bytes 3538948
  4.0 2.8 copy-start.6
  5.9 1.6 copy-start.2
  5.9 2.3 copy-start.16
  501.6 3.1 copy-start.1
  501.6 3.1 copy-start.4
  501.6 3.1 copy-start.5
  504.7 3.4 copy-start.7
  504.7 3.4 copy-start.11
  504.7 3.4 copy-start.12
  504.7 3.4 copy-start.13
  504.7 4.4 copy-start.10
  508.1 1.2 copy-start.3
  508.1 1.5 copy-start.8
  508.1 1.7 copy-start.9
  509.8 1.4 copy-start.15
  509.8 1.5 copy-start.17
  509.8 1.6 copy-start.18
  509.8 1.7 copy-start.14

commit v4 on v3

--- a/solution.py
+++ b/solution.py
@@ -409,7 +409,20 @@
         go(bot.at[lax.rem(ha + d, 8)], xr.at[ha, wa], r_bot.at[d - 1], (lax.rem(ha + d, 8), wa))
         for d in range(1, 8)
     ]
+    got_w3 = spread_z(w3, w3v, r_w3)
+    got_wu = spread_z(wu, wuv, r_wu)
     got_w1 = spread(w1, w1q, 144, 0, 144, r_w1)
+    settle(own_bot)
+    arrive(*bots)
+    to_c = go(xr.at[:, wa], xr.at[:, wa], r_grp.at[0], c_peer)
+    to_y = go(xr.at[:, wa], xr.at[:, wa], r_grp.at[1], y_peer)
+    got_w2a = spread(w2, w2q, 288, 0, 144, r_w2.at[0])
+    got_w2b = spread(w2, w2q, 288, 144, 144, r_w2.at[1])
+    own_skip = stay(skip.at[ha], skv.at[ha])
+    skips = [
+        go(skip.at[lax.rem(ha + d, 8)], skv.at[ha], r_skip.at[d - 1], (lax.rem(ha + d, 8), wa))
+        for d in range(1, 8)
+    ]
     own_code = stay(code.at[ha], code_out.at[ha])
     codes = [
         go(code.at[lax.rem(ha + d, 8)], code_out.at[ha], r_code.at[d - 1], (lax.rem(ha + d, 8), wa))
@@ -420,10 +433,6 @@
     for step in range(1, 32):
         other = lax.rem(mine + step, 32)
         heads.append(go(wh, whv.at[mine], r_wh.at[step - 1], (other // 4, lax.rem(other, 4))))
-    settle(own_bot)
-    arrive(*bots)
-    to_c = go(xr.at[:, wa], xr.at[:, wa], r_grp.at[0], c_peer)
-    to_y = go(xr.at[:, wa], xr.at[:, wa], r_grp.at[1], y_peer)
     if compute:
         x0[:, 0] = jnp.zeros((3, 32, 512), HALF)
         x0[:, 17] = jnp.zeros((3, 32, 512), HALF)
@@ -432,8 +441,6 @@
         for shift in range(3):
             tiles[shift, :, 0] = jnp.zeros((3, 16, 1024), HALF)
             tiles[shift, :, 33] = jnp.zeros((3, 16, 1024), HALF)
-    passed_w1 = pass_x(w1q, 144, 0, 144, got_w1, r_w1x)
-    got_w2a = spread(w2, w2q, 288, 0, 144, r_w2.at[0])
     arrive(to_y)
     part = xr.at[:, 2 * (1 - y) + c]
     on_c = go(part, part, r_grp.at[2], c_peer)
@@ -451,8 +458,14 @@
 
         lax.fori_loop(0, 8, reorder, 0)
     stay(x0.at[:, pl.ds(1, 16)], x0_out)
+    got_w3 = spread_two(w3v, got_w3, r_w3, 384, 512)
+    got_wu = spread_two(wuv, got_wu, r_wu, 1536, 2048)
+    got_w3 = spread_three(w3v, got_w3, r_w3, 384, 512)
+    got_wu = spread_three(wuv, got_wu, r_wu, 1536, 2048)
+    passed_w1 = pass_x(w1q, 144, 0, 144, got_w1, r_w1x)
+    spread_four(w3v, got_w3, r_w3, 384, 512)
+    stay(w3v, w3_out)
     passed_w2a = pass_x(w2q, 288, 0, 144, got_w2a, r_w2x.at[0])
-    got_w2b = spread(w2, w2q, 288, 144, 144, r_w2.at[1])
     arrive(*passed_w1)
     if compute:
 
@@ -471,20 +484,29 @@
     h1_c = go(h1s, lanes(wa), r_h1.at[0], c_peer)
     h1_y = go(h1s, lanes(wa), r_h1.at[1], y_peer)
 
+    spread_four(wuv, got_wu, r_wu, 1536, 2048)
+    stay(wuv, wu_out)
     passed_w2b = pass_x(w2q, 288, 144, 144, got_w2b, r_w2x.at[1])
-    got_wu = spread_z(wu, wuv, r_wu)
-    got_w3 = spread_z(w3, w3v, r_w3)
-    own_skip = stay(skip.at[ha], skv.at[ha])
-    skips = [
-        go(skip.at[lax.rem(ha + d, 8)], skv.at[ha], r_skip.at[d - 1], (lax.rem(ha + d, 8), wa))
-        for d in range(1, 8)
-    ]
     arrive(h1_y)
     h1_on = go(lanes(2 * (1 - y) + c), lanes(2 * (1 - y) + c), r_h1.at[2], c_peer)
     settle(own_h1)
     arrive(h1_c, h1_on)
     stay(h1.at[:, pl.ds(1, 16)], h1_out)
-    got_wu = spread_two(wuv, got_wu, r_wu, 1536, 2048)
+    settle(own_skip)
+    arrive(*skips)
+
+    def skip_slice(s):
+        return skv[:, 64 * s : 64 * s + 64].astype(FLOAT).reshape(32, 16, 512)
+
+    if compute:
+        for s in range(3):
+            value = skip_slice(s)
+            rims[0, s] = value[:, 0].astype(HALF)
+            rims[1, s] = value[:, 15].astype(HALF)
+    before = (ha, lax.rem(wa + 3, 4))
+    after = (ha, lax.rem(wa + 1, 4))
+    rim_right = go(rims.at[0], rims_got.at[1], r_rim.at[1], before)
+    rim_left = go(rims.at[1], rims_got.at[0], r_rim.at[0], after)
     arrive(*passed_w2a, *passed_w2b)
     stay(w2q, w2_out)
     if compute:
@@ -509,25 +531,7 @@
         go(h2s.at[lax.rem(wa + d, 4)], h2_lanes, r_h2.at[d - 1], (ha, lax.rem(wa + d, 4)))
         for d in range(1, 4)
     ]
-    got_w3 = spread_two(w3v, got_w3, r_w3, 384, 512)
-    got_wu = spread_three(wuv, got_wu, r_wu, 1536, 2048)
-
-    settle(own_skip)
-    arrive(*skips)
-
-    def skip_slice(s):
-        return skv[:, 64 * s : 64 * s + 64].astype(FLOAT).reshape(32, 16, 512)
-
-    if compute:
-        for s in range(3):
-            value = skip_slice(s)
-            rims[0, s] = value[:, 0].astype(HALF)
-            rims[1, s] = value[:, 15].astype(HALF)
-    before = (ha, lax.rem(wa + 3, 4))
-    after = (ha, lax.rem(wa + 1, 4))
-    rim_right = go(rims.at[0], rims_got.at[1], r_rim.at[1], before)
-    rim_left = go(rims.at[1], rims_got.at[0], r_rim.at[0], after)
-    got_w3 = spread_three(w3v, got_w3, r_w3, 384, 512)
+
     arrive(rim_right, rim_left)
     if compute:
         for s in range(3):
@@ -536,8 +540,28 @@
             put_shifts(
                 tiles, pl.ds(512, 512), s, skip_slice(s), left[:, None, :], right[:, None, :]
             )
-    spread_four(wuv, got_wu, r_wu, 1536, 2048)
-    stay(wuv, wu_out)
+    def half_conv(first, fresh):
+        rows = w3v.reshape(9216, 512)
+
+        def one_slice(s, carry):
+            if fresh:
+                pre3_out[s] = jnp.zeros((512, 512), FLOAT)
+
+            def tap(t, inner_carry):
+                window = tiles[t % 3, s, pl.ds(t // 3, 32), :, pl.ds(first, 512)].reshape(512, 512)
+                start = pl.multiple_of(1024 * t + first, 512)
+                pre3_out[s] += jnp.dot(
+                    window, rows[pl.ds(start, 512), :], preferred_element_type=FLOAT
+                )
+                return inner_carry
+
+            lax.fori_loop(0, 9, tap, 0)
+            return carry
+
+        lax.fori_loop(0, 3, one_slice, 0)
+
+    if compute:
+        half_conv(512, True)
     settle(own_h2)
     arrive(*h2_got)
     stay(h2v, h2_out)
@@ -569,33 +593,22 @@
             value = jnp.stack(fine, axis=1).reshape(32, 16, 512)
             left, right = [jnp.stack(side, axis=1).reshape(32, 1, 512) for side in sides]
             put_shifts(tiles, pl.ds(0, 512), s, value, left, right)
+
     stay(tiles.at[1, :, pl.ds(1, 32)], joined_out)
     settle(own_head)
     arrive(*heads)
     settle(own_code)
     arrive(*codes)
-    spread_four(w3v, got_w3, r_w3, 384, 512)
-    stay(w3v, w3_out)
     if compute:
         head = whv.reshape(512, 128)[...].astype(FLOAT).T[:16].astype(HALF)
         head_out[...] = head
-        rows = w3v.reshape(9216, 512)
         row = lax.broadcasted_iota(jnp.int32, (8, 128), 0)
         lane = lax.broadcasted_iota(jnp.int32, (8, 128), 1)
         sums_out[0] = jnp.zeros((8, 128), FLOAT)
 
+        half_conv(0, False)
+
         def three(s, carry):
-            pre3_out[s] = jnp.zeros((512, 512), FLOAT)
-
-            def tap(t, inner_carry):
-                window = tiles[t % 3, s, pl.ds(t // 3, 32)].reshape(512, 1024)
-                start = pl.multiple_of(1024 * t, 1024)
-                pre3_out[s] += jnp.dot(
-                    window, rows[pl.ds(start, 1024), :], preferred_element_type=FLOAT
-                )
-                return inner_carry
-
-            lax.fori_loop(0, 9, tap, 0)
             hidden = gelu_of(pre3_out[s]).astype(HALF)
             hidden_out[s] = hidden
             logits = lax.dot_general(
@@ -786,7 +799,7 @@
     ]
     got_wu = stay(wu_in, wu)
     got_h2 = stay(h2_in.at[pl.ds(0, 384)], h2)
-    got_joined = stay(joined_in, joined)
+    got_h1 = stay(h1_in, joined)
     greet_all()
 
     settle(got_hidden)
@@ -930,7 +943,7 @@
         step(y)
         return copies
 
-    def all_x(grad, rows, along_y, along_x, recv, got):
+    def all_x(grad, rows, along_y, along_x, recv, some, got):
         for copy in got:
             copy.wait_recv()
 
@@ -940,12 +953,12 @@
                 add_rows(grad, number * rows, along_y[bz * 2 + bx], rows)
                 return carry
 
-            lax.fori_loop(0, 4, add, 0)
+            lax.fori_loop(some[0], some[-1] + 1, add, 0)
 
         step(1 - x)
         copies = [
             go(block(grad, rows, bz, 1 - x, y, c), along_x.at[bz], recv.at[24 + bz], x_peer)
-            for bz in range(4)
+            for bz in some
         ]
         step(x)
         return copies
@@ -977,30 +990,31 @@
             total = total + along_z[d].astype(FLOAT)
         out[...] = total
 
-    def quarter_x(grad, rows, along_x, recv, bz):
-        source = grad.at[pl.ds(pl.multiple_of((bz * 2 + 1 - x) * 4 * rows, 16), 4 * rows)]
-        return go(source, along_x.at[bz], recv.at[bz], x_peer)
-
-    def quarter_z(grad, rows, along_x, along_z, recv, got):
-        for copy in got:
-            copy.wait_recv()
-
-        def add(d, carry):
-            bz = lax.rem(z + d, 4)
-            add_rows(grad, (bz * 2 + x) * 4 * rows, along_x[bz], 4 * rows)
-            return carry
-
-        lax.fori_loop(0, 4, add, 0)
+    def quarter_rows(rows, bz, bx):
+        return pl.ds(pl.multiple_of((bz * 2 + bx) * 4 * rows, 16), 4 * rows)
+
+    def quarter_x(grad, rows, along_x, recv, d):
+        bz = lax.rem(z + d, 4)
+        return go(grad.at[quarter_rows(rows, bz, 1 - x)], along_x.at[d - 1], recv.at[d - 1], x_peer)
+
+    def quarter_z(grad, rows, along_x, along_z, recv, got, d):
+        got[d - 1].wait_recv()
+        bz = lax.rem(z + d, 4)
+        add_rows(grad, (bz * 2 + x) * 4 * rows, along_x[d - 1], 4 * rows)
+        if d == 4:
+            return None
+        return go(
+            grad.at[quarter_rows(rows, bz, x)],
+            along_z.at[d - 1],
+            recv.at[3 + d],
+            spot(bz, x, y, c),
+        )
+
+    def quarter_taps(taps):
+        first = 2 * lax.rem(z + 1, 4)
         return [
-            go(
-                grad.at[
-                    pl.ds(pl.multiple_of((lax.rem(z + d, 4) * 2 + x) * 4 * rows, 16), 4 * rows)
-                ],
-                along_z.at[d - 1],
-                recv.at[3 + d],
-                spot(lax.rem(z + d, 4), x, y, c),
-            )
-            for d in range(1, 4)
+            (d + 1, span, lambda i, carry: taps(lax.rem(first + i, 9), carry))
+            for d, span in enumerate(((0, 3), (3, 6), (6, 8), (8, 9)))
         ]
 
     def quarter_w(grad, rows, along_z, out, recv, got):
@@ -1029,7 +1043,40 @@
         ]
 
     su = all_core(wu, 32, du_c, r_u, (0, 1, 2, 3))
-    settle(got_joined)
+    su = all_y(wu, 32, du_c, du_y, r_u, (0, 1, 2, 3), su)
+
+    def put_columns(target, s, value):
+        put_shifts(target, pl.ds(0, 256), s, value, 0.0, 0.0)
+
+    for e in range(3):
+        gs2[e, :, 0] = jnp.zeros((3, 32, 256), HALF)
+        gs2[e, :, 17] = jnp.zeros((3, 32, 256), HALF)
+    settle(stay(pre2_in, pre))
+    settle(own_wa)
+    for copy in got_wa:
+        copy.wait_recv()
+
+    def two_grad(s, carry):
+        rows = pl.ds(pl.multiple_of(128 * s, 128), 128)
+        parts = [from_wa[w, rows].astype(FLOAT).reshape(16, 8, 256) for w in range(4)]
+        put_columns(gs2, s, jnp.concatenate(parts, axis=1) * gelu_slope(pre[s]))
+        return carry
+
+    lax.fori_loop(0, 3, two_grad, 0)
+    got_pre1 = stay(pre1_in, pre)
+    settle(got_h1)
+
+    def two_weight(t, carry):
+        window = gs2[2 - t % 3, :, pl.ds(2 - t // 3, 16)].reshape(1536, 256)
+        rows = pl.ds(pl.multiple_of(1024 * t, 1024), 1024)
+        d2[rows] = across(joined[...], window).astype(HALF)
+        return carry
+
+    s2 = []
+    for d, (first, last), taps in quarter_taps(two_weight):
+        lax.fori_loop(first, last, taps, 0)
+        s2.append(quarter_x(d2, 288, d2_x, r_2, d))
+    settle(stay(joined_in, joined))
 
     def three_weight(t, carry):
         window = gs3[2 - t % 3, :, pl.ds(2 - t // 3, 32)].reshape(1536, 512)
@@ -1039,54 +1086,14 @@
 
     lax.fori_loop(0, 5, three_weight, 0)
     s3 = all_core(d3, 288, d3_c, r_3, (0, 1))
-    su = all_y(wu, 32, du_c, du_y, r_u, (0, 1, 2, 3), su)
+    z2 = [quarter_z(d2, 288, d2_x, d2_z, r_2, s2, 1)]
     s3_low = all_y(d3, 288, d3_c, d3_y, r_3, (0, 1), s3)
     pl.semaphore_signal(free, inc=1, device_id=c_peer, device_id_type=MESH)
     lax.fori_loop(5, 9, three_weight, 0)
     pl.semaphore_wait(free, 1)
     s3 = all_core(d3, 288, d3_c, r_3, (2, 3))
-    got_h1 = stay(h1_in, joined)
-
-    settle(own_wa)
-    for copy in got_wa:
-        copy.wait_recv()
-
-    def put_columns(target, s, value):
-        column = lax.broadcasted_iota(jnp.int32, (16, 32, 256), 1)
-        target[0, s, pl.ds(1, 16)] = jnp.where(column > 0, pltpu.roll(value, 1, 1), 0.0).astype(HALF)
-        target[1, s, pl.ds(1, 16)] = value.astype(HALF)
-        target[2, s, pl.ds(1, 16)] = jnp.where(column < 31, pltpu.roll(value, 31, 1), 0.0).astype(
-            HALF
-        )
-
-    for e in range(3):
-        gs2[e, :, 0] = jnp.zeros((3, 32, 256), HALF)
-        gs2[e, :, 17] = jnp.zeros((3, 32, 256), HALF)
-    settle(stay(pre2_in, pre))
-
-    def two_grad(s, carry):
-        rows = pl.ds(pl.multiple_of(128 * s, 128), 128)
-        parts = [from_wa[w, rows].astype(FLOAT).reshape(16, 8, 256) for w in range(4)]
-        put_columns(gs2, s, jnp.concatenate(parts, axis=1) * gelu_slope(pre[s]))
-        return carry
-
-    lax.fori_loop(0, 3, two_grad, 0)
-    got_pre1 = stay(pre1_in, pre)
-    settle(got_h1)
-
-    def two_weight(t, carry):
-        window = gs2[2 - t % 3, :, pl.ds(2 - t // 3, 16)].reshape(1536, 256)
-        rows = pl.ds(pl.multiple_of(1024 * t, 1024), 1024)
-        d2[rows] = across(joined[...], window).astype(HALF)
-        return carry
-
-    s2 = []
-    for bz, (first, last) in enumerate(((0, 3), (3, 5), (5, 7), (7, 9))):
-        lax.fori_loop(first, last, two_weight, 0)
-        s2.append(quarter_x(d2, 288, d2_x, r_2, bz))
-
-    s3_high = all_y(d3, 288, d3_c, d3_y, r_3, (2, 3), s3)
     got_x0 = stay(x0_in, joined.at[:, pl.ds(0, 512)])
+    z2.append(quarter_z(d2, 288, d2_x, d2_z, r_2, s2, 2))
     settle(got_w2)
 
     def source_two(s):
@@ -1105,22 +1112,27 @@
     def d_lanes(halves, s, core):
         return gs3.at[halves, s, pl.ds(0, 32), :, pl.ds(pl.multiple_of(256 * core, 256), 256)]
 
-    sd = []
-    for s in range(3):
-        source_two(s)
-        sd.append(go(d_lanes(pl.ds(0, 2), s, 1 - c), d_core.at[s], r_d.at[s], c_peer))
-        if s == 0:
-            su = all_x(wu, 32, du_y, du_x, r_u, su)
-    sy = []
     own_lanes = pl.ds(pl.multiple_of(256 * c, 256), 256)
-    for s in range(3):
+
+    def d_pass(s):
         sd[s].wait_recv()
         for half in range(2):
             value = gs3[half, s, pl.ds(0, 32), :, own_lanes].astype(FLOAT)
             value = value + d_core[s, half].astype(FLOAT)
             gs3[half, s, pl.ds(0, 32), :, own_lanes] = value.astype(HALF)
-        sy.append(go(d_lanes(1 - y, s, c), d_y.at[s], r_d.at[3 + s], y_peer))
-    s2 = quarter_z(d2, 288, d2_x, d2_z, r_2, s2)
+        return go(d_lanes(1 - y, s, c), d_y.at[s], r_d.at[3 + s], y_peer)
+
+    sd = []
+    sy = []
+    for s in range(3):
+        source_two(s)
+        sd.append(go(d_lanes(pl.ds(0, 2), s, 1 - c), d_core.at[s], r_d.at[s], c_peer))
+        if s > 0:
+            sy.append(d_pass(s - 1))
+    sy.append(d_pass(2))
+    s3_high = all_y(d3, 288, d3_c, d3_y, r_3, (2, 3), s3)
+    z2.append(quarter_z(d2, 288, d2_x, d2_z, r_2, s2, 3))
+    su = all_x(wu, 32, du_y, du_x, r_u, (0, 1, 2, 3), su)
     settle(got_pre1)
     for s in range(3):
         sy[s].wait_recv()
@@ -1135,23 +1147,26 @@
         return carry
 
     s1 = []
-    for bz, (first, last) in enumerate(((0, 3), (3, 5), (5, 7), (7, 9))):
-        lax.fori_loop(first, last, one_weight, 0)
-        s1.append(quarter_x(slot, 144, d1_x, r_1, bz))
-
-    s3 = all_x(d3, 288, d3_y, d3_x, r_3, s3_low + s3_high)
+    for d, (first, last), taps in quarter_taps(one_weight):
+        lax.fori_loop(first, last, taps, 0)
+        s1.append(quarter_x(slot, 144, d1_x, r_1, d))
+
+    quarter_z(d2, 288, d2_x, d2_z, r_2, s2, 4)
+    x3 = all_x(d3, 288, d3_y, d3_x, r_3, (0, 1), s3_low)
     su = all_z(wu, 32, du_x, du_z, r_u, su)
-    s2 = quarter_w(d2, 288, d2_z, g2, r_2, s2)
-    s1 = quarter_z(slot, 144, d1_x, d1_z, r_1, s1)
-    s3 = all_z(d3, 288, d3_x, d3_z, r_3, s3)
+    z1 = [quarter_z(slot, 144, d1_x, d1_z, r_1, s1, d) for d in range(1, 4)]
+    x3 += all_x(d3, 288, d3_y, d3_x, r_3, (2, 3), s3_high)
+    s2 = quarter_w(d2, 288, d2_z, g2, r_2, z2)
+    quarter_z(slot, 144, d1_x, d1_z, r_1, s1, 4)
     settle(own_head)
     total = hh[0]
     for step in range(1, 32):
         heads[step - 1].wait_recv()
         total = total + hh[step]
     gh[...] = total
+    s3 = all_z(d3, 288, d3_x, d3_z, r_3, x3)
     all_end(wu, 32, du_z, gu, su)
-    s1 = quarter_w(slot, 144, d1_z, g1, r_1, s1)
+    s1 = quarter_w(slot, 144, d1_z, g1, r_1, z1)
     all_end(d3, 288, d3_z, g3, s3)
     for copy in s2 + s1:
         copy.wait_recv()

time: 525 us -> 485 us (0.924)
  Pallas kernels: 488 us -> 449 us
    pallas_call x1, Pallas kernels: 232 us -> 195 us  [back(): pl.pallas_call(back_kernel, name='back', out_shape=(shape((288, 512), FLO...]
where the time goes in v4:
time: 485 us; the launch traced here: 476 us
  Pallas kernels  449 us (93%)
  other arithmetic  15.1 us (3%)
  local copies, waits for them, and re-layouts  7.02 us (1%)
    pallas_call x1, Pallas kernels, front(): pl.pallas_call(functools.partial(front_kernel, compute), name='front', ou...  254 us
    pallas_call x1, Pallas kernels, back(): pl.pallas_call(back_kernel, name='back', out_shape=(shape((288, 512), FLO...  195 us

profile of v4, /device:TPU:14, one launch (start us, length us, event | category | flops | bytes accessed | tf_op | source)
XLA Modules:
  0.0 476.5 jit_solution(8489768537887953012)
XLA Ops:
  0.7 0.8 eq.45
  1.5 0.1 copy.58
  1.6 0.7 fusion.5
  2.3 0.8 add_convert_fusion
  3.1 0.1 copy.59
  3.2 0.1 reshape.129
  3.3 0.7 pad_select_fusion.code
  4.0 1.9 convert_element_type.35.w1
  5.9 0.9 convert_element_type.36.w2
  6.8 0.7 convert_element_type.37.wu
  7.4 0.8 convert_element_type.38.w3
  8.2 0.1 copy.60
  8.3 0.6 pad.18.wh
  8.9 254.0 %front.1 = (bf16[3,16,32,512]{3,2,1,0:T(8,128)(2,1)}, bf16[3,16,32,1024]{3,2,1,0:T(8,128)(2,1)}, bf16[480,1024]{1,0:T(8,128)(2,1)}, bf16[3,32,16,1024]{3,2,1,0:T...) custom-call(bf16[8,48,512]{2,1,0:T(8,128)(2,1)} %bitcast.25, ...), custom_call_target="tpu_custom_call" | custom-call | tf_op jit(solution)/shard_map/front/pallas_call | solution.py:675
  262.9 0.9 slice.15
  263.8 0.9 convolution_bitcast_fusion
  264.8 0.6 multiply_divide_fusion
  266.1 0.7 dynamic-slice
  266.8 0.2 fusion.9
  267.0 0.6 pad.19.slopes
  267.6 195.4 %back.1 = (f32[288,512]{1,0:T(8,128)}, f32[32,2048]{1,0:T(8,128)}, bf16[288,1024]{1,0:T(8,128)(2,1)}, bf16[144,1024]{1,0:T(8,128)(2,1)}, f32[16,128]{1,0:T(8,128)}) custom-call(bf16[9216,512]{1,0:T(8,128)(2,1)} %bitcast.18, bf16[1024,2048]{1,0:T(8,128)(2,1)} %bitcast.19, bf16[9216,256]{1,0:T(8,128)(2,1)} %get-tuple-element.39.w2_in, ...), custom_call_target="tpu_custom_call" | custom-call | tf_op jit(solution)/shard_map/back/pallas_call | solution.py:1189
  463.1 3.1 add_multiply_fusion.2
  466.2 3.4 add_multiply_fusion
  469.6 0.9 add_multiply_fusion.3
  470.6 0.2 copy-done.3
  470.8 0.3 copy-done.8
  471.1 0.2 copy-done.9
  471.3 1.4 add_multiply_fusion.1
  472.9 0.1 copy.63
  473.0 0.6 copy.67
  473.6 0.6 copy.68
  474.3 0.6 copy.69
  (43 shorter events, 0.3 us)
Async XLA Ops:
  0.6 5.2 %copy-start = (f32[288,1024]{1,0:T(8,128)S(1)}, f32[288,1024]{1,0:T(8,128)}, u32[]{:S(2)}) copy-start(f32[288,1024]{1,0:T(8,128)} %param.28) | copy-start | bytes 3538948
  4.0 2.8 copy-start.6
  5.9 1.6 copy-start.2
  5.9 2.3 copy-start.16
  463.0 3.1 copy-start.1
  463.0 3.1 copy-start.4
  463.1 3.1 copy-start.5
  466.2 3.4 copy-start.7
  466.2 3.4 copy-start.11
  466.2 3.4 copy-start.12
  466.2 3.4 copy-start.13
  466.2 4.4 copy-start.10
  469.6 1.2 copy-start.3
  469.6 1.5 copy-start.8
  469.6 1.7 copy-start.9
  471.3 1.4 copy-start.15
  471.3 1.5 copy-start.17
  471.3 1.6 copy-start.18
  471.3 1.7 copy-start.14

commit v5 on v4

--- a/solution.py
+++ b/solution.py
@@ -292,7 +292,7 @@
     x0_out, h1_out, h2_out, joined_out, w2_out, wu_out, w3_out, pre1_out, pre2_out, pre3_out,
     hidden_out, logit_out, code_out, sums_out, head_out,
     xr, x0, w1q, w2q, h1s, h1, parts, h2s, h2v, wuv, w3v, skv, rims, rims_got, tiles, whv,
-    send, here, r_bot, r_grp, r_w1, r_w1x, r_w2, r_w2x, r_h1, r_h2, r_skip, r_wh, r_w3, r_wu,
+    send, here, r_bot, r_grp, r_w1, r_w2, r_h1, r_h2, r_skip, r_wh, r_w3, r_wu,
     r_code, r_rim, r_sum,
 ):
     z, x, y, c = place()
@@ -306,7 +306,7 @@
     def go(source, target, recv_sem, device):
         copy = remote(source, target, send.at[len(sends)], recv_sem, device)
         copy.start()
-        sends.append(copy)
+        sends.append((copy, None))
         return copy
 
     def stay(source, target):
@@ -324,105 +324,137 @@
         for copy in copies:
             copy.wait_recv()
 
-    def spread(shard, whole, rows, first, count, recv):
-        start = pl.multiple_of(mine * rows + first, 16)
-        place_rows = whole.at[pl.ds(start, count)]
+    def go_if(when, source, target, recv_sem, device):
+        copy = remote(source, target, send.at[len(sends)], recv_sem, device)
+        pl.when(when)(lambda: copy.start())
+        sends.append((copy, when))
+        return (copy, when)
+
+    def arrive_if(copy, when):
+        pl.when(when)(lambda: copy.wait_recv())
+
+    above, below = (spot(lax.rem(z + 1, 4), x, y, c), spot(lax.rem(z + 3, 4), x, y, c))
+
+    def line_start(part, line):
+        go_if(z < 3, part(z), part(z), line.at[0], above)
+        go_if(z > 0, part(z), part(z), line.at[3], below)
+
+    def line_hop(part, line, j, passes):
+        for first, other, more, last, neighbour in (
+            (0, lax.rem(z + 3 - j, 4), z >= j + 1, z < 3, above),
+            (3, lax.rem(z + 1 + j, 4), z <= 2 - j, z > 0, below),
+        ):
+            piece = part(other)
+            arrive_if(remote(piece, piece, send.at[0], line.at[first + j], x_peer), more)
+            if j < 2:
+                go_if(
+                    jnp.logical_and(more, last), piece, piece, line.at[first + j + 1], neighbour
+                )
+            for recv, got, device in passes:
+                got.append(go_if(more, piece, piece, recv.at[1 + first + j], device))
+
+    def swap(shard, whole, first, count, recv):
         source_rows = pl.ds(first, count)
+        target = whole.at[ha, wa, source_rows]
         lanes = [pl.ds(pl.multiple_of(lax.rem(wa + dw, 4) * 256, 256), 256) for dw in range(4)]
-        own = stay(shard.at[source_rows, lanes[0]], place_rows)
+        own = stay(shard.at[source_rows, lanes[0]], target)
         copies = [
-            go(
-                shard.at[source_rows, lanes[dw]],
-                place_rows,
-                recv.at[dz, dw],
-                (lax.rem(z + dz, 4) * 2 + x, lax.rem(wa + dw, 4)),
-            )
-            for dz in (1, 2, 3, 0)
-            for dw in range(4)
-            if dz + dw > 0
+            go(shard.at[source_rows, lanes[dw]], target, recv.at[dw], (ha, lax.rem(wa + dw, 4)))
+            for dw in range(1, 4)
         ]
         return (own, copies)
 
-    def pass_x(whole, rows, first, count, got, recv):
-        own, copies = got
-        settle(own)
-        arrive(*copies)
-        if count == rows:
-            spans = [(dz, 0, 4 * rows) for dz in range(4)]
-        else:
-            spans = [(dz, w * rows + first, count) for dz in range(4) for w in range(4)]
-        passed = []
-        for number, (dz, offset, length) in enumerate(spans):
-            start = (lax.rem(z + 4 - dz, 4) * 2 + x) * 4 * rows + offset
-            block = whole.at[pl.ds(pl.multiple_of(start, 16), length)]
-            passed.append(go(block, block, recv.at[number], x_peer))
-        return passed
-
-    def spread_z(shard, whole, recv):
-        own = stay(shard, whole.at[z, x, y, c])
-        copies = [
-            go(shard, whole.at[z, x, y, c], recv.at[d - 1], spot(lax.rem(z + d, 4), x, y, c))
-            for d in range(1, 4)
-        ]
-        return (own, copies)
-
-    def spread_two(whole, got, recv, half, width):
-        settle(got[0])
-        arrive(*got[1])
-        low, high = (pl.ds(0, half), pl.ds(half, width - half))
-        part = whole.at[:, x, y, c, :, low]
-        first = go(part, part, recv.at[4], x_peer)
-        part = whole.at[:, x, y, c, :, high]
-        second = go(part, part, recv.at[5], y_peer)
-        part = whole.at[:, x, y, c]
-        core = go(part, part, recv.at[3], c_peer)
-        return (core, first, second)
-
-    def spread_three(whole, got, recv, half, width):
-        core, first, second = got
-        low, high = (pl.ds(0, half), pl.ds(half, width - half))
-        arrive(first)
-        part = whole.at[:, :, y, c, :, low]
-        third = go(part, part, recv.at[6], y_peer)
-        part = whole.at[:, 1 - x, y, c, :, low]
-        core_first = go(part, part, recv.at[8], c_peer)
-        arrive(second)
-        part = whole.at[:, x, :, c, :, high]
-        fourth = go(part, part, recv.at[7], x_peer)
-        part = whole.at[:, x, 1 - y, c, :, high]
-        core_second = go(part, part, recv.at[9], c_peer)
-        return (core, core_first, core_second, third, fourth)
-
-    def spread_four(whole, got, recv, half, width):
-        core, core_first, core_second, third, fourth = got
-        low, high = (pl.ds(0, half), pl.ds(half, width - half))
-        arrive(third)
-        part = whole.at[:, :, 1 - y, c, :, low]
-        core_third = go(part, part, recv.at[10], c_peer)
-        arrive(fourth)
-        part = whole.at[:, 1 - x, :, c, :, high]
-        core_fourth = go(part, part, recv.at[11], c_peer)
-        arrive(core, core_first, core_second, core_third, core_fourth)
+    class Quarter:
+        def __init__(self, shard, whole, first, count, line, recv):
+            self.line, self.recv, self.got = (line, recv, [])
+            self.part = lambda bz: whole.at[bz * 2 + x, :, pl.ds(first, count)]
+            self.swapped = swap(shard, whole, first, count, recv.at[1])
+
+        def start(self):
+            settle(self.swapped[0])
+            arrive(*self.swapped[1])
+            line_start(self.part, self.line)
+            own = self.part(z)
+            self.got.append((go(own, own, self.recv.at[0, 0], x_peer), None))
+
+        def hop(self, j):
+            line_hop(self.part, self.line, j, [(self.recv.at[0], self.got, x_peer)])
+
+        def done(self):
+            for copy, when in self.got:
+                if when is None:
+                    copy.wait_recv()
+                else:
+                    arrive_if(copy, when)
+
+    class Whole:
+        def __init__(self, shard, whole, line, recv):
+            self.whole, self.line, self.recv = (whole, line, recv)
+            self.part = lambda bz: whole.at[bz, x, y, c]
+            self.own = stay(shard, self.part(z))
+            self.along_x, self.along_y, self.core = ([], [], [])
+
+        def start(self):
+            settle(self.own)
+            line_start(self.part, self.line)
+            own = self.part(z)
+            self.along_x.append((go(own, own, self.recv.at[0, 0], x_peer), None))
+            self.along_y.append((go(own, own, self.recv.at[1, 0], y_peer), None))
+            self.core.append((go(own, own, self.recv.at[2, 0], c_peer), None))
+
+        def hop(self, j):
+            passes = [
+                (self.recv.at[0], self.along_x, x_peer),
+                (self.recv.at[1], self.along_y, y_peer),
+                (self.recv.at[2], self.core, c_peer),
+            ]
+            line_hop(self.part, self.line, j, passes)
+
+        def wait(self, got):
+            for copy, when in got:
+                if when is None:
+                    copy.wait_recv()
+                else:
+                    arrive_if(copy, when)
+
+        def turn(self):
+            self.wait(self.along_x)
+            part = self.whole.at[:, 1 - x, y, c]
+            self.last = go(part, part, self.recv.at[1, 7], y_peer)
+            self.core.append((go(part, part, self.recv.at[2, 7], c_peer), None))
+
+        def finish(self):
+            self.wait(self.along_y)
+            part = self.whole.at[:, x, 1 - y, c]
+            self.core.append((go(part, part, self.recv.at[0, 7], c_peer), None))
+            arrive(self.last)
+            part = self.whole.at[:, 1 - x, 1 - y, c]
+            self.core.append((go(part, part, self.recv.at[3, 0], c_peer), None))
+
+        def done(self):
+            self.wait(self.core)
 
     own_bot = stay(bot.at[ha], xr.at[ha, wa])
     bots = [
         go(bot.at[lax.rem(ha + d, 8)], xr.at[ha, wa], r_bot.at[d - 1], (lax.rem(ha + d, 8), wa))
         for d in range(1, 8)
     ]
-    got_w3 = spread_z(w3, w3v, r_w3)
-    got_wu = spread_z(wu, wuv, r_wu)
-    got_w1 = spread(w1, w1q, 144, 0, 144, r_w1)
+    whole_three = Whole(w3, w3v, r_w3.at[4, pl.ds(0, 6)], r_w3)
+    whole_up = Whole(wu, wuv, r_wu.at[4, pl.ds(0, 6)], r_wu)
+    one_part = Quarter(w1, w1q, 0, 144, r_w1.at[2], r_w1)
+    two_low = Quarter(w2, w2q, 0, 144, r_w2.at[0, 2], r_w2.at[0])
+    two_high = Quarter(w2, w2q, 144, 144, r_w2.at[1, 2], r_w2.at[1])
+    whole_three.start()
+    whole_up.start()
     settle(own_bot)
     arrive(*bots)
     to_c = go(xr.at[:, wa], xr.at[:, wa], r_grp.at[0], c_peer)
     to_y = go(xr.at[:, wa], xr.at[:, wa], r_grp.at[1], y_peer)
-    got_w2a = spread(w2, w2q, 288, 0, 144, r_w2.at[0])
-    got_w2b = spread(w2, w2q, 288, 144, 144, r_w2.at[1])
-    own_skip = stay(skip.at[ha], skv.at[ha])
-    skips = [
-        go(skip.at[lax.rem(ha + d, 8)], skv.at[ha], r_skip.at[d - 1], (lax.rem(ha + d, 8), wa))
-        for d in range(1, 8)
-    ]
+    whole_three.hop(0)
+    whole_up.hop(0)
+    one_part.start()
+    whole_three.hop(1)
+    whole_up.hop(1)
     own_code = stay(code.at[ha], code_out.at[ha])
     codes = [
         go(code.at[lax.rem(ha + d, 8)], code_out.at[ha], r_code.at[d - 1], (lax.rem(ha + d, 8), wa))
@@ -441,6 +473,11 @@
         for shift in range(3):
             tiles[shift, :, 0] = jnp.zeros((3, 16, 1024), HALF)
             tiles[shift, :, 33] = jnp.zeros((3, 16, 1024), HALF)
+    whole_three.hop(2)
+    two_low.start()
+    whole_up.hop(2)
+    one_part.hop(0)
+    two_high.start()
     arrive(to_y)
     part = xr.at[:, 2 * (1 - y) + c]
     on_c = go(part, part, r_grp.at[2], c_peer)
@@ -458,19 +495,25 @@
 
         lax.fori_loop(0, 8, reorder, 0)
     stay(x0.at[:, pl.ds(1, 16)], x0_out)
-    got_w3 = spread_two(w3v, got_w3, r_w3, 384, 512)
-    got_wu = spread_two(wuv, got_wu, r_wu, 1536, 2048)
-    got_w3 = spread_three(w3v, got_w3, r_w3, 384, 512)
-    got_wu = spread_three(wuv, got_wu, r_wu, 1536, 2048)
-    passed_w1 = pass_x(w1q, 144, 0, 144, got_w1, r_w1x)
-    spread_four(w3v, got_w3, r_w3, 384, 512)
-    stay(w3v, w3_out)
-    passed_w2a = pass_x(w2q, 288, 0, 144, got_w2a, r_w2x.at[0])
-    arrive(*passed_w1)
+    one_part.hop(1)
+    two_low.hop(0)
+    one_part.hop(2)
+    two_high.hop(0)
+    whole_three.turn()
+    two_low.hop(1)
+    two_high.hop(1)
+    whole_up.turn()
+    own_skip = stay(skip.at[ha], skv.at[ha])
+    skips = [
+        go(skip.at[lax.rem(ha + d, 8)], skv.at[ha], r_skip.at[d - 1], (lax.rem(ha + d, 8), wa))
+        for d in range(1, 8)
+    ]
+    two_low.hop(2)
+    one_part.done()
     if compute:
 
         def one(s, carry):
-            value = conv_slice(x0, w1q, parts, s, 512)
+            value = conv_slice(x0, w1q.reshape(4608, 256), parts, s, 512)
             pre1_out[s] = value
             h1s[s] = gelu_of(value).astype(HALF)
             return carry
@@ -484,35 +527,21 @@
     h1_c = go(h1s, lanes(wa), r_h1.at[0], c_peer)
     h1_y = go(h1s, lanes(wa), r_h1.at[1], y_peer)
 
-    spread_four(wuv, got_wu, r_wu, 1536, 2048)
-    stay(wuv, wu_out)
-    passed_w2b = pass_x(w2q, 288, 144, 144, got_w2b, r_w2x.at[1])
+    two_high.hop(2)
+    whole_three.finish()
+    whole_up.finish()
     arrive(h1_y)
     h1_on = go(lanes(2 * (1 - y) + c), lanes(2 * (1 - y) + c), r_h1.at[2], c_peer)
     settle(own_h1)
     arrive(h1_c, h1_on)
     stay(h1.at[:, pl.ds(1, 16)], h1_out)
-    settle(own_skip)
-    arrive(*skips)
-
-    def skip_slice(s):
-        return skv[:, 64 * s : 64 * s + 64].astype(FLOAT).reshape(32, 16, 512)
-
-    if compute:
-        for s in range(3):
-            value = skip_slice(s)
-            rims[0, s] = value[:, 0].astype(HALF)
-            rims[1, s] = value[:, 15].astype(HALF)
-    before = (ha, lax.rem(wa + 3, 4))
-    after = (ha, lax.rem(wa + 1, 4))
-    rim_right = go(rims.at[0], rims_got.at[1], r_rim.at[1], before)
-    rim_left = go(rims.at[1], rims_got.at[0], r_rim.at[0], after)
-    arrive(*passed_w2a, *passed_w2b)
+    two_low.done()
+    two_high.done()
     stay(w2q, w2_out)
     if compute:
 
         def two(s, carry):
-            value = conv_slice(h1, w2q, parts, s, 1024)
+            value = conv_slice(h1, w2q.reshape(9216, 256), parts, s, 1024)
             pre2_out[s] = value
             hidden = gelu_of(value)
             for w in range(4):
@@ -532,6 +561,21 @@
         for d in range(1, 4)
     ]
 
+    settle(own_skip)
+    arrive(*skips)
+
+    def skip_slice(s):
+        return skv[:, 64 * s : 64 * s + 64].astype(FLOAT).reshape(32, 16, 512)
+
+    if compute:
+        for s in range(3):
+            value = skip_slice(s)
+            rims[0, s] = value[:, 0].astype(HALF)
+            rims[1, s] = value[:, 15].astype(HALF)
+    before = (ha, lax.rem(wa + 3, 4))
+    after = (ha, lax.rem(wa + 1, 4))
+    rim_right = go(rims.at[0], rims_got.at[1], r_rim.at[1], before)
+    rim_left = go(rims.at[1], rims_got.at[0], r_rim.at[0], after)
     arrive(rim_right, rim_left)
     if compute:
         for s in range(3):
@@ -560,11 +604,15 @@
 
         lax.fori_loop(0, 3, one_slice, 0)
 
+    whole_three.done()
+    stay(w3v, w3_out)
     if compute:
         half_conv(512, True)
     settle(own_h2)
     arrive(*h2_got)
     stay(h2v, h2_out)
+    whole_up.done()
+    stay(wuv, wu_out)
     if compute:
         order = lax.broadcasted_iota(jnp.int32, (256, 256), 1)
         inner = order % 128
@@ -647,8 +695,11 @@
     for entry in stays:
         if not entry[1]:
             settle(entry)
-    for copy in sends:
-        copy.wait_send()
+    for copy, when in sends:
+        if when is None:
+            copy.wait_send()
+        else:
+            pl.when(when)(copy.wait_send)
 
 
 def class_terms(logits, codes, s):
@@ -680,7 +731,7 @@
             shape((3, 16, 32, 1024), HALF),
             shape((480, 1024), HALF),
             shape((3, 32, 16, 1024), HALF),
-            shape((9216, 256), HALF),
+            shape((8, 4, 288, 256), HALF),
             shape((4, 2, 2, 2, 32, 2048), HALF),
             shape((4, 2, 2, 2, 288, 512), HALF),
             shape((3, 16, 32, 256), FLOAT),
@@ -697,8 +748,8 @@
         scratch_shapes=[
             room(8, 4, 48, 512),
             room(3, 18, 32, 512),
-            room(4608, 256),
-            room(9216, 256),
+            room(8, 4, 144, 256),
+            room(8, 4, 288, 256),
             room(3, 16, 32, 256),
             room(3, 18, 32, 1024),
             pltpu.VMEM((3, 512, 256), FLOAT),
@@ -711,20 +762,18 @@
             room(2, 3, 32, 512),
             room(3, 3, 34, 16, 1024),
             room(32, 16, 128),
-            dma((220,)),
+            dma((256,)),
             dma((24,)),
             dma((7,)),
             dma((3,)),
-            dma((4, 4)),
-            dma((4,)),
-            dma((2, 4, 4)),
-            dma((2, 16)),
+            dma((3, 8)),
+            dma((2, 3, 8)),
             dma((3,)),
             dma((3,)),
             dma((7,)),
             dma((31,)),
-            dma((12,)),
-            dma((12,)),
+            dma((5, 8)),
+            dma((5, 8)),
             dma((7,)),
             dma((2,)),
             dma((31,)),
@@ -1279,6 +1328,7 @@
     )
     wu = wu.reshape(1024, 2048)
     w3 = w3.reshape(9216, 512)
+    w2 = w2.reshape(9216, 256)
     member = (groups[:, None] == jnp.arange(GROUPS)[None, :]).astype(FLOAT)
     step = lax.axis_index("ha") * 4 + lax.axis_index("wa")
     origin = (step - jnp.arange(32)) % 32

time: 485 us -> 438 us (0.903)
  the two profiles are of different devices: /device:TPU:14 before, /device:TPU:12 now
where the time goes in v5:
time: 438 us; the launch traced here: 429 us
  Pallas kernels  402 us (92%)
  other arithmetic  15.1 us (3%)
  local copies, waits for them, and re-layouts  7.02 us (2%)
    pallas_call x1, Pallas kernels, front(): pl.pallas_call(functools.partial(front_kernel, compute), name='front', ou...  208 us
    pallas_call x1, Pallas kernels, back(): pl.pallas_call(back_kernel, name='back', out_shape=(shape((288, 512), FLO...  194 us
    add x5, other arithmetic, renew_state(): average_new = AVERAGE_DECAY * average + (1.0 - AVERAGE_DECAY) * weight_new  8.83 us

profile of v5, /device:TPU:12, one launch (start us, length us, event | category | flops | bytes accessed | tf_op | source)
XLA Modules:
  0.0 429.2 jit_solution(12285689668423794173)
XLA Ops:
  0.7 0.8 eq.45
  1.5 0.1 copy.58
  1.6 0.7 fusion.5
  2.3 0.8 add_convert_fusion
  3.1 0.1 copy.59
  3.2 0.1 reshape.132
  3.3 0.7 pad_select_fusion.code
  4.0 1.9 convert_element_type.35.w1
  5.9 0.9 convert_element_type.36.w2
  6.8 0.7 convert_element_type.37.wu
  7.4 0.8 convert_element_type.38.w3
  8.2 0.1 copy.60
  8.3 0.6 pad.18.wh
  8.9 208.3 %front.1 = (bf16[3,16,32,512]{3,2,1,0:T(8,128)(2,1)}, bf16[3,16,32,1024]{3,2,1,0:T(8,128)(2,1)}, bf16[480,1024]{1,0:T(8,128)(2,1)}, bf16[3,32,16,1024]{3,2,1,0:T...) custom-call(bf16[8,48,512]{2,1,0:T(8,128)(2,1)} %bitcast.27, ...), custom_call_target="tpu_custom_call" | custom-call | tf_op jit(solution)/shard_map/front/pallas_call | solution.py:726
  217.3 0.9 slice.15
  218.2 0.9 convolution_bitcast_fusion
  219.1 0.6 multiply_divide_fusion
  220.4 0.7 dynamic-slice
  221.2 0.2 fusion.9
  221.3 0.6 pad.19.slopes
  221.9 193.8 %back.1 = (f32[288,512]{1,0:T(8,128)}, f32[32,2048]{1,0:T(8,128)}, bf16[288,1024]{1,0:T(8,128)(2,1)}, bf16[144,1024]{1,0:T(8,128)(2,1)}, f32[16,128]{1,0:T(8,128)}) custom-call(bf16[9216,512]{1,0:T(8,128)(2,1)} %bitcast.19, bf16[1024,2048]{1,0:T(8,128)(2,1)} %bitcast.21, bf16[9216,256]{1,0:T(8,128)(2,1)} %bitcast.20, bf16[1536,1024]{1,0:T(8,128)(2,1)} %bitcast.23, ...), custom_call_target="tpu_custom_call" | custom-call | tf_op jit(solution)/shard_map/back/pallas_call | solution.py:1238
  415.7 3.1 add_multiply_fusion.2
  418.9 3.4 add_multiply_fusion
  422.3 0.9 add_multiply_fusion.3
  423.3 0.2 copy-done.3
  423.4 0.3 copy-done.8
  423.8 0.2 copy-done.9
  424.0 1.4 add_multiply_fusion.1
  425.6 0.1 copy.63
  425.7 0.6 copy.67
  426.3 0.6 copy.68
  427.0 0.6 copy.69
  (43 shorter events, 0.3 us)
Async XLA Ops:
  0.6 5.2 %copy-start = (f32[288,1024]{1,0:T(8,128)S(1)}, f32[288,1024]{1,0:T(8,128)}, u32[]{:S(2)}) copy-start(f32[288,1024]{1,0:T(8,128)} %param.28) | copy-start | bytes 3538948
  4.0 2.8 copy-start.6
  5.9 1.6 copy-start.2
  5.9 2.3 copy-start.16
  415.7 3.1 copy-start.1
  415.7 3.1 copy-start.4
  415.7 3.1 copy-start.5
  418.8 3.4 copy-start.7
  418.9 3.4 copy-start.11
  418.9 3.4 copy-start.12
  418.9 3.4 copy-start.13
  418.9 4.4 %copy-start.10 = (f32[288,512]{1,0:T(8,128)S(1)}, f32[288,512]{1,0:T(8,128)}, u32[]{:S(2)}) copy-start(f32[288,512]{1,0:T(8,128)} %get-tuple-element.54) | copy-start | bytes 1769476
  422.3 1.2 copy-start.3
  422.3 1.5 copy-start.8
  422.3 1.7 copy-start.9
  424.0 1.4 copy-start.15
  424.0 1.5 copy-start.17
  424.0 1.6 copy-start.18
  424.0 1.7 copy-start.14
